TPU v7x, 32 devices: a whole 2x2x4 slice. The times are simulated.
32 devices in a mesh: band: 2 (over x), chan: 8 (over z, y), pair: 2 (over core).
Axes of the slice: x: 2, y: 2, z: 4, core: 2. Of those that a mesh axis runs over, the one named last changes fastest.
Arguments:
- samples: int32 [2, 2048, 32768], P(None, 'chan', ('band', 'pair')), parts along dimension 2, may hold values from -8 to 6, as said below
- taps: int32 [4, 1024], replicated, may hold values from -127 to 127
- tile_order: int32 [36], replicated, may hold values from 0 to 35, each once
Outputs:
- visibilities: bfloat16 [16, 36, 2, 256, 256], P(('band', 'chan'), 'pair'), parts along dimension 0
There are 2 independent parts, one for each index of `band`. A program takes and returns all parts, laid end to end along the dimension named above; an argument that names none is the same for every part. Nothing has to cross between parts.
Inputs may be any that keep to these rules, and one draw needn't show every extreme that they name: 4-bit voltage samples with a component common to all inputs.
All inputs are finite; a program needn't handle non-finite values.
Results may differ from a plain program's by a relative error of at most 0.0034.
Values may be sent and summed in bfloat16 or wider, within the bound.
No kernel may reach another device: no remote copies, remote signals or barrier semaphores. Data moves between devices by JAX's collectives and lax.ppermute only.
A program may use at most 320 MiB of HBM per device.

v0:
```python
import math

import jax
import jax.numpy as jnp
import numpy as np
from jax import lax
from jax.sharding import PartitionSpec as P

BLOCK = 256


def passed_along(block, axis, distance):
    devices = range(lax.axis_size(axis))
    route = [(i - distance, i) for i in devices if i - distance in devices]
    return lax.ppermute(block, axis, route)


def dft_table(length):
    index = jnp.arange(length, dtype=jnp.int32)
    phase = index[:, None] * index[None, :] % length
    angle = phase.astype(jnp.float32) * (2.0 * math.pi / length)
    cosine = jnp.cos(angle)
    sine = jnp.sin(angle)
    upper = jnp.stack([cosine, -sine], axis=1)
    lower = jnp.stack([sine, cosine], axis=1)
    return jnp.concatenate([upper, lower], axis=0).astype(jnp.bfloat16)


def tile_products(spectra, slots, tile_count):
    input_count = spectra.shape[0]
    block_count = input_count // BLOCK
    width = spectra.shape[1] * spectra.shape[2] * spectra.shape[3]
    rows_np, cols_np = np.triu_indices(block_count)
    numbers = jnp.arange(tile_count, dtype=jnp.int32)
    match = (slots[:, None] == numbers[None, :]).astype(jnp.int32)
    first = jnp.sum(match * jnp.asarray(rows_np.astype(np.int32))[None, :], axis=1)
    second = jnp.sum(match * jnp.asarray(cols_np.astype(np.int32))[None, :], axis=1)
    swapped = jnp.stack([spectra[:, :, 1], -spectra[:, :, 0]], axis=2)
    plain_blocks = spectra.reshape(block_count, BLOCK, width)
    paired = jnp.stack([plain_blocks, swapped.reshape(block_count, BLOCK, width)], axis=1)
    left_blocks = paired[first]
    right_blocks = plain_blocks[second]
    return jnp.einsum(
        "scuw,svw->scuv", left_blocks, right_blocks, preferred_element_type=jnp.float32
    )


def per_device(samples, taps, tile_order):
    inputs_here = samples.shape[1]
    sample_count = samples.shape[2]
    tap_count = taps.shape[0]
    fft_size = taps.shape[1]
    frame_count = sample_count // fft_size
    volts = samples.astype(jnp.bfloat16)
    rim_length = (tap_count - 1) * fft_size
    earlier = passed_along(volts[:, :, sample_count - rim_length :], "pair", 1)
    longer = jnp.concatenate([earlier, volts], axis=2).astype(jnp.float32)
    framed = longer.reshape(2, inputs_here, frame_count + tap_count - 1, fft_size)
    weights = taps.astype(jnp.float32)
    filtered = jnp.zeros((2, inputs_here, frame_count, fft_size), jnp.float32)
    for tap_index in range(tap_count):
        filtered = (
            filtered
            + weights[tap_index][None, None, None, :]
            * framed[:, :, tap_index : tap_index + frame_count, :]
        )
    filtered = filtered.astype(jnp.bfloat16)
    left = jnp.concatenate([filtered[0], filtered[1]], axis=-1)
    table = dft_table(fft_size)
    spectra = jnp.einsum("xfm,mck->xfck", left, table, preferred_element_type=jnp.float32)
    chan_size = lax.axis_size("chan")
    group_width = fft_size // chan_size
    spectra = (
        (spectra * 2.0 ** (-14))
        .astype(jnp.bfloat16)
        .reshape(inputs_here, frame_count, 2, chan_size, group_width)
    )
    turned = lax.all_to_all(spectra, "chan", split_axis=3, concat_axis=0, tiled=True)
    turned = turned.reshape(turned.shape[0], frame_count, 2, group_width)
    tile_count = tile_order.shape[0]
    pair_size = lax.axis_size("pair")
    factor = 1.0 / (frame_count * group_width * pair_size)
    summed = lax.psum_scatter(
        tile_products(turned, tile_order, tile_count), "pair", scatter_dimension=0, tiled=True
    )
    return (summed * factor).astype(jnp.bfloat16)[None]


def solution(mesh):
    in_specs = (P(None, "chan", ("band", "pair")), P(), P())
    out_specs = P(("band", "chan"), "pair", None, None, None)
    return jax.shard_map(
        per_device, mesh=mesh, in_specs=in_specs, out_specs=out_specs, check_vma=False
    )
```

profile of v0, /device:TPU:0, one launch (start us, length us, event | category | flops | bytes accessed | tf_op | source)
XLA Modules:
  0.0 667.3 jit_solution(5073412094975297140)
XLA Ops:
  6.5 17.4 %copy.25 = s32[2,256,8192]{1,2,0:T(8,128)} copy(s32[2,256,8192]{2,1,0:T(8,128)} %param.5) | data formatting | bytes 33554432 | tf_op args[0]
  24.0 6.6 convert_element_type.49
  30.6 0.2 slice.59
  30.8 2.6 collective-permute-start
  33.4 15.7 %fusion.22 = bf16[1024,1,1024]{2,0,1:T(8,128)(2,1)S(1)} fusion(), kind=kLoop, calls=%fused_computation.43 | loop fusion | flops 15728640 | bytes 2097152 | tf_op jit(solution)/shard_map/convert.3
  49.1 17.8 %negate_convert_fusion = (bf16[1024,1,1024]{2,0,1:T(8,128)(2,1)}, bf16[1024,1,1024]{2,0,1:T(8,128)(2,1)}) fusion(), kind=kLoop, calls=%fused_computation.37 | loop fusion | flops 17825792 | bytes 4194304 | tf_op jit(solution)/shard_map/convert.6
  67.0 29.3 %pad_maximum_fusion = bf16[2,256,11264]{1,2,0:T(8,128)(2,1)} fusion(bf16[2,256,8192]{1,2,0:T(8,128)(2,1)S(1)} %convert_element_type.49, bf16[2,256,3072]{1,2,0:T(8,128)(2,1)S(1)} %collective-permute-done), kind=kLoop, calls=%fused_computation.12 | loop fusion | flops 23068672 | bytes 23068672 | tf_op jit(solution)/shard_map/concatenate | solution.py:57
  96.2 31.4 %fusion.27 = (f32[2,256,8,1024]{1,3,2,0:T(8,128)}, f32[2,256,8,1024]{1,3,2,0:T(8,128)}, f32[2,256,8,1024]{1,3,2,0:T(8,128)}, f32[2,256,8,1024]{1,3,2,0:T(8,128)}) fusion(bf16[2,256,11,1024]{1,3,2,0:T(8,128)(2,1)} %bitcast.49), kind=kLoop, calls=%fused_computation.55 | loop fusion | bytes 134217728 | tf_op jit(solution)/shard_map/slice | solution.py:65
  127.7 17.3 %copy.42 = f32[2,256,8,1024]{3,1,2,0:T(8,128)} copy(f32[2,256,8,1024]{1,3,2,0:T(8,128)} %get-tuple-element.9) | data formatting | bytes 33554432
  145.0 17.3 %copy.43 = f32[2,256,8,1024]{3,1,2,0:T(8,128)} copy(f32[2,256,8,1024]{1,3,2,0:T(8,128)} %get-tuple-element.10) | data formatting | bytes 33554432
  162.2 17.3 %copy.44 = f32[2,256,8,1024]{3,1,2,0:T(8,128)} copy(f32[2,256,8,1024]{1,3,2,0:T(8,128)} %get-tuple-element.11) | data formatting | bytes 33554432
  179.5 17.3 %copy.45 = f32[2,256,8,1024]{3,1,2,0:T(8,128)} copy(f32[2,256,8,1024]{1,3,2,0:T(8,128)} %get-tuple-element.12) | data formatting | bytes 33554432
  196.8 22.5 %add_convert_fusion = bf16[2,256,8,1024]{3,1,2,0:T(8,128)(2,1)S(1)} fusion(f32[2,256,8,1024]{3,1,2,0:T(8,128)} %copy.45, f32[2,256,8,1024]{3,1,2,0:T(8,128)} %copy.44, f32[2,256,8,1024]{3,1,2,0:T(8,128)} %copy.43, f32[2,256,8,1024]{3,1,2,0:T(8,128)} %copy.42, f32[1024]{0:T(1024)S(1)} %bitcast.54, f32[1024]{0:T(1024)S(1)} %bitcast.55, f32[1024]{0:T(1024)S(1)} %bitcast.56, ...), kind=kLoop, calls=%fused_computation.11 | loop fusion | flops 33554432 | bytes 75513856 | tf_op jit(solution)/shard_map/convert_element_type | solution.py:67
  219.3 4.3 slice_bitcast_fusion.1
  223.6 24.3 %multiply_convert_fusion = bf16[256,8,2,1024]{3,0,2,1:T(8,128)(2,1)} fusion(bf16[256,8,1024]{2,0,1:T(8,128)(2,1)} %get-tuple-element.16, bf16[256,8,1024]{2,0,1:T(8,128)(2,1)} %get-tuple-element.15, bf16[1024,1,1024]{2,0,1:T(8,128)(2,1)} %get-tuple-element.22, bf16[1024,1,1024]{2,0,1:T(8,128)(2,1)S(1)} %fusion.22, bf16[1024,1,1024]{2,0,1:T(8,128)(2,1)} %get-tuple-element.21), kind=kOutput, calls=%fused_computation.10 | convolution fusion | flops 17238589440 | bytes 23068672 | tf_op jit(solution)/shard_map/xfm,mck->xfck/dot_general | solution.py:70
  247.9 8.8 %copy.46 = bf16[512,8,8,128]{3,2,1,0:T(8,128)(2,1)} copy(bf16[512,8,8,128]{3,1,2,0:T(8,128)(2,1)} %bitcast.52) | data formatting | bytes 16777216
  256.7 12.6 %copy.30 = bf16[256,8,2,8,128]{0,4,2,1,3:T(8,128)(2,1)} copy(bf16[256,8,2,8,128]{4,3,0,2,1:T(8,128)(2,1)} %bitcast.51) | data formatting | bytes 16777216 | tf_op jit(solution)/shard_map/reshape | solution.py:76
  269.3 6.8 %all-to-all-start = ((bf16[256,8,2,8,128]{0,4,2,1,3:T(8,128)(2,1)}), bf16[256,8,2,8,128]{0,4,2,1,3:T(8,128)(2,1)}, u32[]{:S(2)}, u32[]{:S(2)}) async-start(bf16[256,8,2,8,128]{0,4,2,1,3:T(8,128)(2,1)} %copy.30), calls=%async_computation | async-start | bytes 16777216 | tf_op jit(solution)/shard_map/all_to_all | solution.py:78
  276.4 182.2 %all-to-all-done = bf16[256,8,2,8,128]{0,4,2,1,3:T(8,128)(2,1)} async-done(((bf16[256,8,2,8,128]{0,4,2,1,3:T(8,128)(2,1)}), bf16[256,8,2,8,128]{0,4,2,1,3:T(8,128)(2,1)}, u32[]{:S(2)}, u32[]{:S(2)}) %all-to-all-start) | async-done | bytes 8388640 | tf_op jit(solution)/shard_map/all_to_all | solution.py:78
  458.6 12.7 %copy.31 = bf16[8,256,8,2,1,128]{5,2,4,3,1,0:T(8,128)(2,1)} copy(bf16[8,256,8,2,1,128]{1,5,3,2,0,4:T(8,128)(2,1)} %bitcast.12) | data formatting | bytes 16777216 | tf_op jit(solution)/shard_map/all_to_all | solution.py:78
  471.3 3.9 fusion.28
  475.2 1.4 pad_maximum_fusion.2
  476.7 10.4 %copy.38 = bf16[2048,8,2,128]{3,2,1,0:T(2,128)(2,1)} copy(bf16[2048,8,2,128]{3,1,2,0:T(8,128)(2,1)S(1)} %pad_maximum_fusion.2) | data formatting | bytes 16777216 | tf_op jit(solution)/shard_map/stack;reshape | solution.py:40
  487.0 14.5 %reshape.151 = bf16[8,1,256,2048]{3,2,1,0:T(8,128)(2,1)} reshape(bf16[2048,8,2,128]{3,2,1,0:T(2,128)(2,1)} %copy.38) | data formatting | bytes 16777216 | tf_op jit(solution)/shard_map/stack;reshape | solution.py:40
  501.5 11.5 %copy.33 = bf16[8,1,256,2048]{3,2,1,0:T(8,128)(2,1)} copy(bf16[8,1,256,2048]{2,3,0,1:T(8,128)(2,1)} %bitcast.13) | data formatting | bytes 16777216 | tf_op jit(solution)/shard_map/stack;reshape;reshape | solution.py:40
  513.0 11.8 %fusion.5 = (bf16[8,2,256,1024]{3,2,1,0:T(8,128)(2,1)}, bf16[8,2,256,1024]{3,2,1,0:T(8,128)(2,1)}) fusion(bf16[8,1,256,2048]{3,2,1,0:T(8,128)(2,1)} %copy.33, bf16[8,1,256,2048]{3,2,1,0:T(8,128)(2,1)} %reshape.151), kind=kLoop, calls=%fused_computation.14 | loop fusion | flops 33554432 | bytes 33554432 | tf_op jit(solution)/shard_map/stack | solution.py:40
  524.8 18.0 %gather_fusion.1 = bf16[36,2,256,1024]{3,2,1,0:T(8,128)(2,1)} fusion(bf16[8,2,256,1024]{3,2,1,0:T(8,128)(2,1)} %get-tuple-element.7, s32[1024]{0:T(1024)S(1)} %pad_clamp_fusion.1), kind=kCustom, calls=%fused_computation.1 | custom fusion | bytes 75497616 | tf_op jit(solution)/shard_map/gather | solution.py:41
  542.8 17.8 %gather_fusion.2 = bf16[36,2,256,1024]{3,2,1,0:T(8,128)(2,1)} fusion(bf16[8,2,256,1024]{3,2,1,0:T(8,128)(2,1)} %get-tuple-element.8, s32[1024]{0:T(1024)S(1)} %pad_clamp_fusion.1), kind=kCustom, calls=%fused_computation.2 | custom fusion | bytes 75497616 | tf_op jit(solution)/shard_map/gather | solution.py:41
  560.7 17.8 %gather_fusion = bf16[36,256,2048]{1,2,0:T(8,128)(2,1)} fusion(bf16[8,256,2048]{1,2,0:T(8,128)(2,1)} %bitcast.18, s32[1024]{0:T(1024)S(1)} %pad_clamp_fusion), kind=kCustom, calls=%fused_computation | custom fusion | bytes 75497616 | tf_op jit(solution)/shard_map/gather | solution.py:42
  578.5 47.4 %fusion = f32[36,2,256,256]{3,2,1,0:T(8,128)} fusion(bf16[36,2,256,1024]{3,2,1,0:T(8,128)(2,1)} %gather_fusion.2, bf16[36,2,256,1024]{3,2,1,0:T(8,128)(2,1)} %gather_fusion.1, bf16[36,256,2048]{1,2,0:T(8,128)(2,1)} %gather_fusion), kind=kOutput, calls=%fused_computation.3 | convolution fusion | flops 19478347776 | bytes 132120576 | tf_op jit(solution)/shard_map/scuw,svw->scuv/dot_general | solution.py:43
  625.9 27.5 %reduce-scatter.2.cloned.1.call-done = f32[18,2,256,256]{3,2,1,0:T(8,128)} async-done(((f32[36,2,256,256]{3,2,1,0:T(8,128)}), f32[18,2,256,256]{3,2,1,0:T(8,128)}) %reduce-scatter.2.cloned.1.call-update) | async-done | bytes 9437200 | tf_op jit(solution)/shard_map/reduce_scatter | solution.py:83
  653.4 7.1 %fusion.14 = bf16[1,18,2,256,256]{4,3,2,1,0:T(8,128)(2,1)} fusion(f32[18,2,256,256]{3,2,1,0:T(8,128)} %reduce-scatter.2.cloned.1.call-done), kind=kLoop, calls=%fused_computation.30 | loop fusion | flops 4718592 | bytes 14155776 | tf_op jit(solution)/shard_map/broadcast_in_dim | solution.py:86
  (18 shorter events, 0.3 us)
Async XLA Ops:
  24.0 9.4 %copy-start = (s32[4,1024]{1,0:T(4,128)S(1)}, s32[4,1024]{1,0:T(4,128)}, u32[]{:S(2)}) copy-start(s32[4,1024]{1,0:T(4,128)} %param.6) | copy-start | bytes 49156
  30.8 36.1 %collective-permute-start = (bf16[2,256,3072]{1,2,0:T(8,128)(2,1)S(1)}, bf16[2,256,3072]{1,2,0:T(8,128)(2,1)S(1)}, u32[]{:S(2)}, u32[]{:S(2)}) collective-permute-start(bf16[2,256,3072]{1,2,0:T(8,128)(2,1)S(1)} %slice.59), channel_id=1, source_target_pairs={{0,1},{2,3},{4,5},{6,7},{8,9},{10,11},{12,13},{14,15},{16,17},{18,... | collective-permute-start | bytes 9437192 | tf_op jit(solution)/shard_map/ppermute | solution.py:15
  269.3 6.9 %copy-start.1 = (s32[36]{0:T(128)S(1)}, s32[36]{0:T(128)}, u32[]{:S(2)}) copy-start(s32[36]{0:T(128)} %param.7) | copy-start | bytes 436
  269.3 6.9 %copy-start.2 = (s32[36]{0:T(128)S(1)}, s32[36]{0:T(128)}, u32[]{:S(2)}) copy-start(s32[36]{0:T(128)} %constant.32.clone) | copy-start | bytes 436
  269.3 6.9 %copy-start.3 = (s32[36]{0:T(128)S(1)}, s32[36]{0:T(128)}, u32[]{:S(2)}) copy-start(s32[36]{0:T(128)} %constant.31.clone) | copy-start | bytes 436
  269.3 189.3 %all-to-all-start = ((bf16[256,8,2,8,128]{0,4,2,1,3:T(8,128)(2,1)}), bf16[256,8,2,8,128]{0,4,2,1,3:T(8,128)(2,1)}, u32[]{:S(2)}, u32[]{:S(2)}) async-start(bf16[256,8,2,8,128]{0,4,2,1,3:T(8,128)(2,1)} %copy.30), calls=%async_computation | async-start | bytes 16777216 | tf_op jit(solution)/shard_map/all_to_all | solution.py:78
  276.1 377.3 %reduce-scatter.2.cloned.1.call-start = ((), (), s32[]{:S(2)}) async-start(), calls=%async_computation.2 | async-start | bytes 28311552 | tf_op jit(solution)/shard_map/reduce_scatter | solution.py:83
Sparse Core Ops, SparseCore 0:
  626.0 27.2 reduce-scatter.1
where the time goes:
time: 670 us; the launch traced here: 667 us
  local copies, waits for them, and re-layouts  247 us (37%)
  waiting for transfers between devices  210 us (31%)
  other arithmetic  116 us (17%)
  matrix products  71.7 us (11%)
  between operations  13.5 us (2%)
  starting transfers between devices  9.4 us (1%)
    all_to_all x1, waiting for transfers between devices, per_device(): lax.all_to_all(spectra, 'chan', split_axis=3, concat_axis=0, tiled=True)  182 us
    unnamed x14, local copies, waits for them, and re-layouts  95.4 us
    dot_general x1, matrix products, tile_products(): jnp.einsum('scuw,svw->scuv', left_blocks, right_blocks, preferred_element...  47.4 us
    another operation x3, local copies, waits for them, and re-layouts, tile_products(): jnp.stack([plain_blocks, swapped.reshape(block_count, BLOCK, width)], axi...  36.4 us
    gather x2, local copies, waits for them, and re-layouts, tile_products(): left_blocks = paired[first]  35.8 us
    another operation x2, other arithmetic  33.5 us
    slice x1, local copies, waits for them, and re-layouts, per_device(): framed[:, :, tap_index:tap_index + frame_count, :]  31.4 us
    concatenate x1, other arithmetic, per_device(): longer = jnp.concatenate([earlier, volts], axis=2).astype(jnp.float32)  29.3 us
  transfers between devices with their start and end apart: 3, of which 2 were waited for; matrix products, arithmetic and copies ran while one was open for 5% of the time, Pallas kernels for 0%

commit v1 on v0

--- a/solution.py
+++ b/solution.py
@@ -1,18 +1,344 @@
+import functools
 import math
 
 import jax
 import jax.numpy as jnp
+import ml_dtypes
 import numpy as np
 from jax import lax
+from jax.experimental import pallas as pl
+from jax.experimental.pallas import tpu as pltpu
 from jax.sharding import PartitionSpec as P
 
 BLOCK = 256
+UNROLL = 3
+COST = 10**11
+LANES = 128
+ROWS = 32
+SCALE = 2.0**-14
+VMEM_LIMIT = 56 * 1024 * 1024
+
+PLAN = (2, 3, 3)
 
 
 def passed_along(block, axis, distance):
     devices = range(lax.axis_size(axis))
     route = [(i - distance, i) for i in devices if i - distance in devices]
     return lax.ppermute(block, axis, route)
+
+
+def swapped_with(block, axis, mask):
+    return lax.ppermute(block, axis, [(i, i ^ mask) for i in range(lax.axis_size(axis))])
+
+
+def grouped_table(length, groups):
+    index = np.arange(length)
+    angle = (index[:, None] * index[None, :] % length).astype(np.float32) * np.float32(2.0 * math.pi / length)
+    cosine = np.cos(angle).astype(ml_dtypes.bfloat16).astype(np.float32) * SCALE
+    sine = np.sin(angle).astype(ml_dtypes.bfloat16).astype(np.float32) * SCALE
+    both = np.stack([cosine, sine], axis=1).reshape(length, 2, groups, length // groups)
+    return both.transpose(2, 0, 1, 3).reshape(groups, length, 2 * (length // groups)).astype(ml_dtypes.bfloat16)
+
+
+def front_kernel(geometry, samples, *refs):
+    first, count, sends, with_rim, gated, fft_size, tap_count = geometry
+    groups = len(sends)
+    reach = tap_count - 1
+    early = max(0, reach - first)
+    own = count + reach - early
+    refs = list(refs)
+    rim_in = refs.pop(0) if early else None
+    taps, table = refs.pop(0), refs.pop(0)
+    if gated:
+        refs.pop(0)
+    pieces = [[refs.pop(0) for _ in widths] for widths in sends[: groups // 2]]
+    near_out = refs.pop(0) if sends[-1] else None
+    for j in range(groups // 2, groups):
+        pieces.append([near_out.at[j - groups // 2]] if near_out is not None else [])
+    rim_out = refs.pop(0) if with_rim else None
+    held = refs.pop(0)
+    held_rim = refs.pop(0) if early else None
+    tables, left, results = refs.pop(0), refs.pop(0), refs.pop(0)
+    rim_made = refs.pop(0) if with_rim else None
+    in_sems, table_sems, out_sems = refs[:3]
+    steps = BLOCK // ROWS
+    me = lax.axis_index("chan")
+
+    def copies_in(step):
+        rows = pl.ds(pl.multiple_of(step * ROWS, ROWS), ROWS)
+        lanes = pl.ds((first - reach + early) * fft_size, own * fft_size)
+        made = [pltpu.make_async_copy(samples.at[:, rows, lanes], held.at[:, rows, :], in_sems.at[0, step])]
+        if early:
+            lanes = pl.ds((reach - early) * fft_size, early * fft_size)
+            made.append(pltpu.make_async_copy(rim_in.at[:, rows, lanes], held_rim.at[:, rows, :], in_sems.at[1, step]))
+        return made
+
+    def copy_table(j):
+        group = me ^ (j + groups // 2) if j < groups // 2 else me - lax.rem(me, groups // 2) + (j - groups // 2)
+        return pltpu.make_async_copy(table.at[group], tables.at[j], table_sems.at[j])
+
+    def copies_out(j):
+        made, f = [], 0
+        for w, width in enumerate(sends[j]):
+            part = results.at[j, :, f * BLOCK : (f + width) * BLOCK]
+            made.append(pltpu.make_async_copy(part, pieces[j][w], out_sems.at[j, w]))
+            f += width
+        return made
+
+    used = [j for j in range(groups) if sends[j]]
+    for step in range(steps):
+        for copy in copies_in(step):
+            copy.start()
+    for j in used:
+        copy_table(j).start()
+
+    def filter_rows(step, carry):
+        for copy in copies_in(step):
+            copy.wait()
+        rows = pl.ds(pl.multiple_of(step * ROWS, ROWS), ROWS)
+        for part in range(2):
+            for start in range(0, fft_size, LANES):
+                values = []
+                for k in range(early):
+                    lanes = slice(k * fft_size + start, k * fft_size + start + LANES)
+                    values.append(held_rim[part, rows, lanes].astype(jnp.float32))
+                for k in range(own):
+                    lanes = slice(k * fft_size + start, k * fft_size + start + LANES)
+                    values.append(held[part, rows, lanes].astype(jnp.float32))
+                lanes = slice(start, start + LANES)
+                weights = [taps[t : t + 1, lanes].astype(jnp.float32) for t in range(tap_count)]
+                for f in range(count):
+                    total = weights[0] * values[f]
+                    for t in range(1, tap_count):
+                        total = total + weights[t] * values[f + t]
+                    at = pl.ds(pl.multiple_of(f * BLOCK + step * ROWS, ROWS), ROWS)
+                    left[part, at, lanes] = total.astype(jnp.bfloat16)
+                if with_rim:
+                    for t in range(reach):
+                        lanes = slice(t * fft_size + start, t * fft_size + start + LANES)
+                        rim_made[part, rows, lanes] = values[count + t].astype(jnp.bfloat16)
+        return carry
+
+    lax.fori_loop(0, steps, filter_rows, 0)
+    if with_rim:
+        rim_copy = pltpu.make_async_copy(rim_made, rim_out, in_sems.at[1, 0])
+        rim_copy.start()
+
+    def transform(j, frames):
+        pltpu.make_async_copy(table.at[0], tables.at[j], table_sems.at[j]).wait()
+        rows = frames * BLOCK
+        product = [
+            jnp.dot(left[part, :rows, :], tables[j], preferred_element_type=jnp.float32) for part in range(2)
+        ]
+        real = (product[0][:, :LANES] + product[1][:, LANES:]).astype(jnp.bfloat16)
+        imag = (product[1][:, :LANES] - product[0][:, LANES:]).astype(jnp.bfloat16)
+        for f in range(frames):
+            results[j, :, f * BLOCK : f * BLOCK + LANES] = real[f * BLOCK : (f + 1) * BLOCK]
+            results[j, :, f * BLOCK + LANES : (f + 1) * BLOCK] = imag[f * BLOCK : (f + 1) * BLOCK]
+        for k in used:
+
+            @pl.when(j == k)
+            def _():
+                for copy in copies_out(k):
+                    copy.start()
+
+    begin = 0
+    while begin < len(used):
+        end = begin
+        while end < len(used) and sum(sends[end]) == sum(sends[begin]):
+            end += 1
+
+        def several(j, carry, frames=sum(sends[begin])):
+            transform(j, frames)
+            return carry
+
+        lax.fori_loop(begin, end, several, 0, unroll=2)
+        begin = end
+    if with_rim:
+        rim_copy.wait()
+    for j in used:
+        for copy in copies_out(j):
+            copy.wait()
+
+
+def front(samples, rim, taps, table, gate, first, count, sends, with_rim):
+    fft_size = taps.shape[1]
+    tap_count = taps.shape[0]
+    reach = tap_count - 1
+    groups, depth, columns = len(sends), table.shape[1], table.shape[2]
+    early = max(0, reach - first)
+    own = count + reach - early
+    anywhere = pl.BlockSpec(memory_space=pl.ANY)
+    vmem = pl.BlockSpec(memory_space=pltpu.VMEM)
+    operands = [samples] + ([rim] if early else []) + [taps, table] + ([] if gate is None else [gate])
+    in_specs = [anywhere] + ([anywhere] if early else []) + [vmem, anywhere] + ([] if gate is None else [anywhere])
+    out_shape = []
+    for widths in sends[: groups // 2]:
+        for width in widths:
+            out_shape.append(jax.ShapeDtypeStruct((BLOCK, width * columns), jnp.bfloat16))
+    if sends[-1]:
+        out_shape.append(jax.ShapeDtypeStruct((groups // 2, BLOCK, sends[-1][0] * columns), jnp.bfloat16))
+    scratch = [pltpu.VMEM((2, BLOCK, own * fft_size), jnp.int32)]
+    if early:
+        scratch.append(pltpu.VMEM((2, BLOCK, early * fft_size), jnp.bfloat16))
+    scratch += [
+        pltpu.VMEM((groups, depth, columns), jnp.bfloat16),
+        pltpu.VMEM((2, count * BLOCK, depth), jnp.bfloat16),
+        pltpu.VMEM((groups, BLOCK, count * columns), jnp.bfloat16),
+    ]
+    if with_rim:
+        out_shape.append(jax.ShapeDtypeStruct((2, BLOCK, reach * fft_size), jnp.bfloat16))
+        scratch.append(pltpu.VMEM((2, BLOCK, reach * fft_size), jnp.bfloat16))
+    scratch += [
+        pltpu.SemaphoreType.DMA((2, BLOCK // ROWS)),
+        pltpu.SemaphoreType.DMA((groups,)),
+        pltpu.SemaphoreType.DMA((groups, max(len(widths) for widths in sends))),
+    ]
+    geometry = (first, count, sends, with_rim, gate is not None, fft_size, tap_count)
+    results = list(
+        pl.pallas_call(
+            functools.partial(front_kernel, geometry),
+            in_specs=in_specs,
+            out_specs=[anywhere] * len(out_shape),
+            out_shape=out_shape,
+            scratch_shapes=scratch,
+            compiler_params=pltpu.CompilerParams(vmem_limit_bytes=VMEM_LIMIT),
+            cost_estimate=pl.CostEstimate(flops=COST, bytes_accessed=1, transcendentals=0),
+        )(*operands)
+    )
+    pieces = [[results.pop(0) for _ in widths] for widths in sends[: groups // 2]]
+    return pieces, results[0] if with_rim or sends[-1] else None
+
+
+def gather_kernel(layout, *refs):
+    parts, out, held, in_sems, out_sems = refs[:-4], *refs[-4:]
+    copies, sends = [], []
+    for d, places in enumerate(layout):
+        f = 0
+        for w, (number, at, start, width) in enumerate(places):
+            source = parts[number] if at is None else parts[number].at[at]
+            source = source.at[:, start * BLOCK : (start + width) * BLOCK]
+            target = held.at[d, :, f * BLOCK : (f + width) * BLOCK]
+            copies.append((d, pltpu.make_async_copy(source, target, in_sems.at[d, w])))
+            f += width
+        sends.append(pltpu.make_async_copy(held.at[d], out.at[d], out_sems.at[d]))
+    for _, copy in copies:
+        copy.start()
+    for d, send in enumerate(sends):
+        for owner, copy in copies:
+            if owner == d:
+                copy.wait()
+        send.start()
+    for send in sends:
+        send.wait()
+
+
+def gathered(blocks, after):
+    operands, layout = [], []
+    for block in blocks:
+        places = []
+        for array, at, start, width in block:
+            places.append((len(operands), at, start, width))
+            operands.append(array)
+        layout.append(tuple(places))
+    frames = sum(place[3] for place in layout[0])
+    shape = (len(blocks), BLOCK, frames * BLOCK)
+    operands += [] if after is None else [after]
+    return pl.pallas_call(
+        functools.partial(gather_kernel, tuple(layout)),
+        in_specs=[pl.BlockSpec(memory_space=pl.ANY)] * len(operands),
+        out_specs=pl.BlockSpec(memory_space=pl.ANY),
+        out_shape=jax.ShapeDtypeStruct(shape, jnp.bfloat16),
+        scratch_shapes=[
+            pltpu.VMEM(shape, jnp.bfloat16),
+            pltpu.SemaphoreType.DMA((len(blocks), max(len(places) for places in layout))),
+            pltpu.SemaphoreType.DMA((len(blocks),)),
+        ],
+        compiler_params=pltpu.CompilerParams(vmem_limit_bytes=VMEM_LIMIT),
+        cost_estimate=pl.CostEstimate(flops=1, bytes_accessed=1, transcendentals=0),
+    )(*operands)
+
+
+def tile_kernel(geometry, first, second, *refs):
+    count, has_sums, factor = geometry
+    blocks = refs[:count]
+    sums = refs[count] if has_sums else None
+    refs = refs[count + has_sums :]
+    out, held, totals = refs[0], refs[1 : 1 + count], refs[1 + count]
+    finished = refs[2 + count]
+    block_sems, sum_sems, out_sems = refs[-3:]
+    slots = totals.shape[0]
+    numbers = blocks[0].shape[0]
+    block_copies = [
+        pltpu.make_async_copy(blocks[k].at[d], held[k].at[d], block_sems.at[k, d])
+        for d in range(numbers)
+        for k in range(count)
+    ]
+    for copy in block_copies:
+        copy.start()
+
+    def copy_in(slot):
+        return pltpu.make_async_copy(sums.at[slot], totals.at[slot], sum_sems.at[slot])
+
+    def copy_out(slot):
+        return pltpu.make_async_copy(finished.at[slot], out.at[slot], out_sems.at[slot])
+
+    if has_sums:
+        for slot in range(slots):
+            copy_in(slot).start()
+    for copy in block_copies:
+        copy.wait()
+    if has_sums:
+        for slot in range(slots):
+            copy_in(slot).wait()
+
+    def correlate(slot, carry):
+        a, b = first[slot], second[slot]
+        total = None
+        for block in held:
+            left, right = block[a], block[b]
+            turned = []
+            for start in range(0, left.shape[1], 2 * LANES):
+                turned += [left[:, start + LANES : start + 2 * LANES], -left[:, start : start + LANES]]
+            both = jnp.concatenate([left, jnp.concatenate(turned, axis=1)], axis=0)
+            term = lax.dot_general(both, right, (((1,), (1,)), ((), ())), preferred_element_type=jnp.float32)
+            total = term if total is None else total + term
+        if has_sums:
+            total = total + totals[slot]
+        if factor is not None:
+            total = total * factor
+        finished[slot] = total.astype(finished.dtype)
+        copy_out(slot).start()
+        return carry
+
+    lax.fori_loop(0, slots, correlate, 0, unroll=UNROLL)
+    for slot in range(slots):
+        copy_out(slot).wait()
+
+
+def tiles(first, second, blocks, sums, factor):
+    slots = first.shape[0]
+    anywhere = pl.BlockSpec(memory_space=pl.ANY)
+    smem = pl.BlockSpec(memory_space=pltpu.SMEM)
+    operands = list(blocks) + ([] if sums is None else [sums])
+    width = sum(block.shape[2] for block in blocks)
+    shape = (slots, 2 * BLOCK, BLOCK)
+    kind = jnp.float32 if factor is None else jnp.bfloat16
+    scratch = [pltpu.VMEM(block.shape, block.dtype) for block in blocks] + [pltpu.VMEM(shape, jnp.float32), pltpu.VMEM(shape, kind)]
+    scratch += [
+        pltpu.SemaphoreType.DMA((len(blocks), blocks[0].shape[0])),
+        pltpu.SemaphoreType.DMA((slots,)),
+        pltpu.SemaphoreType.DMA((slots,)),
+    ]
+    return pl.pallas_call(
+        functools.partial(tile_kernel, (len(blocks), sums is not None, factor)),
+        in_specs=[smem, smem] + [anywhere] * len(operands),
+        out_specs=anywhere,
+        out_shape=jax.ShapeDtypeStruct(shape, kind),
+        scratch_shapes=scratch,
+        compiler_params=pltpu.CompilerParams(vmem_limit_bytes=VMEM_LIMIT),
+        cost_estimate=pl.CostEstimate(flops=COST, bytes_accessed=1, transcendentals=0),
+    )(first, second, *operands)
 
 
 def dft_table(length):
@@ -45,7 +371,7 @@
     )
 
 
-def per_device(samples, taps, tile_order):
+def any_sizes(samples, taps, tile_order):
     inputs_here = samples.shape[1]
     sample_count = samples.shape[2]
     tap_count = taps.shape[0]
@@ -86,9 +412,81 @@
     return (summed * factor).astype(jnp.bfloat16)[None]
 
 
+def per_device(samples, taps, tile_order):
+    fft_size = taps.shape[1]
+    groups = lax.axis_size("chan")
+    pair_size = lax.axis_size("pair")
+    me = lax.axis_index("chan").astype(jnp.int32)
+    far = groups // 2
+    table = jnp.asarray(grouped_table(fft_size, groups))
+
+    slots = tile_order.shape[0] // pair_size
+    own_slots = lax.dynamic_slice(tile_order, (lax.axis_index("pair") * slots,), (slots,))
+    rows_np, cols_np = np.triu_indices(groups)
+    match = (own_slots[:, None] == jnp.arange(tile_order.shape[0], dtype=jnp.int32)[None, :]).astype(jnp.int32)
+
+    def place_of(blocks_np):
+        block = jnp.sum(match * jnp.asarray(blocks_np.astype(np.int32))[None, :], axis=1)
+        return jnp.where(block // far == me // far, block % far, block ^ me)
+
+    first, second = place_of(rows_np), place_of(cols_np)
+
+    def after(value, *others):
+        return lax.optimization_barrier((value, *others))[0]
+
+    def to(mask, value):
+        return swapped_with(value, "chan", mask)
+
+    def other_core(value):
+        return swapped_with(value, "pair", 1)
+
+    def among_near(value):
+        halves = [list(range(start, start + far)) for start in range(0, groups, far)]
+        return lax.all_to_all(value, "chan", 0, 0, axis_index_groups=halves, tiled=True)
+
+    apart = range(far, groups)
+    FIRST, SECOND, THIRD = PLAN
+    end = samples.shape[2] // fft_size
+    start_a, start_b = end - FIRST, end - FIRST - SECOND
+    made_a, rim_here = front(samples, None, taps, table, None, start_a, FIRST, ((FIRST,),) * far + ((),) * far, True)
+    a = {mask: to(mask, made_a[mask - far][0]) for mask in apart}
+    rim = passed_along(rim_here, "pair", 1)
+    sends = ((SECOND,),) * far + ((SECOND + FIRST,),) * far
+    made_b, near_b = front(samples, None, taps, table, made_a[0][0], start_b, SECOND + FIRST, sends, False)
+    b = {mask: to(mask, after(made_b[mask - far][0], a[mask])) for mask in apart}
+    ab = among_near(near_b)
+    sends = ((THIRD,),) * far + ((THIRD,),) * far
+    made_c, near_c = front(samples, rim, taps, table, made_b[0][0], 0, THIRD, sends, False)
+    c = {}
+    for mask, gates in zip(apart, [(rim,), (b[far], ab)] + [(b[mask],) for mask in apart][1:]):
+        c[mask] = to(mask, after(made_c[mask - far][0], *gates))
+    cc = among_near(near_c)
+    blocks = [[(ab, k, 0, SECOND + FIRST)] for k in range(far)]
+    blocks += [[(b[mask], None, 0, SECOND), (a[mask], None, 0, FIRST)] for mask in apart]
+    mine = gathered(blocks, None)
+    other = other_core(mine)
+    sums = tiles(first, second, [mine], None, None)
+    sums = tiles(first, second, [other], sums, None)
+    blocks = [[(cc, k, 0, THIRD)] for k in range(far)] + [[(c[mask], None, 0, THIRD)] for mask in apart]
+    mine = gathered(blocks, sums)
+    other = other_core(mine)
+    sums = tiles(first, second, [mine], sums, None)
+    factor = 1.0 / (end * pair_size * (fft_size // groups))
+    sums = tiles(first, second, [other], sums, factor)
+    return sums.reshape(1, slots, 2, BLOCK, BLOCK)
+
+
+def chosen(samples, taps, tile_order):
+    groups, pair_size = lax.axis_size("chan"), lax.axis_size("pair")
+    whole_blocks = samples.shape[1] == BLOCK and taps.shape[1] == groups * LANES
+    halves = groups >= 2 and groups & (groups - 1) == 0 and pair_size == 2
+    planned = samples.shape[2] == sum(PLAN) * taps.shape[1] and taps.shape[0] - 1 <= PLAN[2]
+    if whole_blocks and halves and planned:
+        return per_device(samples, taps, tile_order)
+    return any_sizes(samples, taps, tile_order)
+
+
 def solution(mesh):
     in_specs = (P(None, "chan", ("band", "pair")), P(), P())
     out_specs = P(("band", "chan"), "pair", None, None, None)
-    return jax.shard_map(
-        per_device, mesh=mesh, in_specs=in_specs, out_specs=out_specs, check_vma=False
-    )
+    return jax.shard_map(chosen, mesh=mesh, in_specs=in_specs, out_specs=out_specs, check_vma=False)

time: 670 us -> 237 us (0.35)
  local copies, waits for them, and re-layouts: 247 us -> 4.78 us
  waiting for transfers between devices: 210 us -> 91 us
  other arithmetic: 116 us -> 0.77 us
  Pallas kernels: 0 us -> 100 us
  matrix products: 71.7 us -> 0 us
  starting transfers between devices: 9.4 us -> 39.1 us
  between operations: 13.5 us -> 0.42 us
    all_to_all x1 -> x2, waiting for transfers between devices: 182 us -> 0.01 us  [among_near(): lax.all_to_all(value, 'chan', 0, 0, axis_index_groups=halves, tiled=True)]
    pallas_call x0 -> x9, Pallas kernels: none -> 100 us  [the longest x4 50 us: tiles(): pl.pallas_call(functools.partial(tile_kernel, (len(blocks), sums is not N...]
    ppermute x0 -> x14, waiting for transfers between devices: none -> 91 us  [swapped_with(): lax.ppermute(block, axis, [(i, i ^ mask) for i in range(lax.axis_size(axi...]
    unnamed x14 -> x26, local copies, waits for them, and re-layouts: 95.4 us -> 4.7 us
    dot_general x2 -> x0, matrix products: 71.7 us -> none  [the longest x1 47.4 us: tile_products(): jnp.einsum('scuw,svw->scuv', left_blocks, right_blocks, preferred_element...]
    gather x3 -> x0, local copies, waits for them, and re-layouts: 53.7 us -> none  [the longest x2 35.8 us: tile_products(): left_blocks = paired[first]]
    another operation x4 -> x0, other arithmetic: 46.8 us -> none
    another operation x3 -> x0, local copies, waits for them, and re-layouts: 36.4 us -> none  [tile_products(): jnp.stack([plain_blocks, swapped.reshape(block_count, BLOCK, width)], axi...]
  transfers between devices with their start and end apart: 3 -> 17, of which waited for: 2 -> 4; matrix products, arithmetic and copies ran while one was open for 5% -> 0% of each run, Pallas kernels for 0% -> 33%
where the time goes in v1:
time: 237 us; the launch traced here: 236 us
  Pallas kernels  100 us (42%)
  waiting for transfers between devices  91 us (38%)
  starting transfers between devices  39.1 us (16%)
  local copies, waits for them, and re-layouts  4.78 us (2%)
    ppermute x14, waiting for transfers between devices, swapped_with(): lax.ppermute(block, axis, [(i, i ^ mask) for i in range(lax.axis_size(axi...  91 us
    pallas_call x4, Pallas kernels, tiles(): pl.pallas_call(functools.partial(tile_kernel, (len(blocks), sums is not N...  50 us
    pallas_call x3, Pallas kernels, front(): pl.pallas_call(functools.partial(front_kernel, geometry), in_specs=in_spe...  42.7 us
    ppermute x14, starting transfers between devices, swapped_with(): lax.ppermute(block, axis, [(i, i ^ mask) for i in range(lax.axis_size(axi...  26.3 us
    all_to_all x2, starting transfers between devices, among_near(): lax.all_to_all(value, 'chan', 0, 0, axis_index_groups=halves, tiled=True)  9.83 us
    pallas_call x2, Pallas kernels, gathered(): pl.pallas_call(functools.partial(gather_kernel, tuple(layout)), in_specs=...  7.46 us
  transfers between devices with their start and end apart: 17, of which 4 were waited for; matrix products, arithmetic and copies ran while one was open for 0% of the time, Pallas kernels for 33%

profile of v1, /device:TPU:0, one launch (start us, length us, event | category | flops | bytes accessed | tf_op | source)
XLA Modules:
  0.0 236.2 jit_solution(16960716730534735964)
XLA Ops:
  0.0 8.8 %shard_map.64 = (bf16[256,512]{1,0:T(8,128)(2,1)}, bf16[256,512]{1,0:T(8,128)(2,1)}, bf16[256,512]{1,0:T(8,128)(2,1)}, bf16[256,512]{1,0:T(8,128)(2,1)}, bf16[2,256,3072]{2,1,0:T(8,128)(2,1)}) custom-call(s32[2,256,8192]{2,1,0:T(8,128)} %samples.5, s32[4,1024]{1,0:T(4,128)} %refs_1_.3, bf16[8,1024,256]{2,1,0:T(8,128)(2,1)} %constant.72.clone.refs_1_.refs_2_), custom_call_target="tpu_custom_call" | custom-call | flops 99999997952 | bytes 1 | tf_op jit(solution)/shard_map/pallas_call | solution.py:199
  8.9 5.1 %collective-permute-start.5 = (bf16[256,512]{1,0:T(8,128)(2,1)}, bf16[256,512]{1,0:T(8,128)(2,1)S(1)}, u32[]{:S(2)}, u32[]{:S(2)}) collective-permute-start(bf16[256,512]{1,0:T(8,128)(2,1)} %get-tuple-element.40), channel_id=1, source_target_pairs={{0,10},{2,8},{4,14},{6,12},{8,2},{10,0},{12,6},{14,4},{1,11},{3,9}... | collective-permute-start | bytes 786440 | tf_op jit(solution)/shard_map/ppermute | solution.py:31
  13.9 1.3 collective-permute-start.8
  15.3 2.4 %collective-permute-start.11 = (bf16[256,512]{1,0:T(8,128)(2,1)}, bf16[256,512]{1,0:T(8,128)(2,1)S(1)}, u32[]{:S(2)}, u32[]{:S(2)}) collective-permute-start(bf16[256,512]{1,0:T(8,128)(2,1)} %get-tuple-element.49), channel_id=1, source_target_pairs={{0,14},{2,12},{4,10},{6,8},{8,6},{10,4},{12,2},{14,0},{1,15},{3,13... | collective-permute-start | bytes 786440 | tf_op jit(solution)/shard_map/ppermute | solution.py:31
  17.7 2.9 %collective-permute-start = (bf16[2,256,3072]{2,1,0:T(8,128)(2,1)}, bf16[2,256,3072]{2,1,0:T(8,128)(2,1)}, u32[]{:S(2)}, u32[]{:S(2)}) collective-permute-start(bf16[2,256,3072]{2,1,0:T(8,128)(2,1)} %get-tuple-element.28), channel_id=1, source_target_pairs={{0,1},{2,3},{4,5},{6,7},{8,9},{10,11},{12,13},{14,15},{16,17},{18,... | collective-permute-start | bytes 9437192 | tf_op jit(solution)/shard_map/ppermute | solution.py:27
  20.6 19.3 %shard_map.65 = (bf16[256,768]{1,0:T(8,128)(2,1)}, bf16[256,768]{1,0:T(8,128)(2,1)}, bf16[256,768]{1,0:T(8,128)(2,1)}, bf16[256,768]{1,0:T(8,128)(2,1)}, bf16[4,256,1280]{2,1,0:T(8,128)(2,1)}) custom-call(s32[2,256,8192]{2,1,0:T(8,128)} %samples.5, s32[4,1024]{1,0:T(4,128)} %refs_1_.3, bf16[8,1024,256]{2,1,0:T(8,128)(2,1)} %constant.72.clone.refs_1_.refs_2_, ...), custom_call_target="tpu_custom_call" | custom-call | flops 99999997952 | bytes 1 | tf_op jit(solution)/shard_map/pallas_call | solution.py:199
  39.9 4.3 %all-to-all-start.1 = ((bf16[4,256,1280]{2,1,0:T(8,128)(2,1)}), bf16[4,256,1280]{2,1,0:T(8,128)(2,1)S(1)}, u32[]{:S(2)}, u32[]{:S(2)}) async-start(bf16[4,256,1280]{2,1,0:T(8,128)(2,1)} %get-tuple-element.36), calls=%async_computation.1 | async-start | bytes 5242880 | tf_op jit(solution)/shard_map/all_to_all | solution.py:445
  44.2 0.1 dynamic_slice.3
  44.3 0.2 select_reduce_fusion
  44.5 0.6 compare_select_fusion
  45.1 18.0 %collective-permute-done.2.refs_5_ = bf16[256,512]{1,0:T(8,128)(2,1)} collective-permute-done((bf16[256,512]{1,0:T(8,128)(2,1)}, bf16[256,512]{1,0:T(8,128)(2,1)}, u32[]{:S(2)}, u32[]{:S(2)}) %collective-permute-start.2) | collective-permute-done | bytes 262176 | tf_op jit(solution)/shard_map/ppermute | solution.py:31
  63.2 5.0 %collective-permute-start.12 = (bf16[256,768]{1,0:T(8,128)(2,1)}, bf16[256,768]{1,0:T(8,128)(2,1)S(1)}, u32[]{:S(2)}, u32[]{:S(2)}) collective-permute-start(bf16[256,768]{1,0:T(8,128)(2,1)} %get-tuple-element.50), channel_id=1, source_target_pairs={{0,14},{2,12},{4,10},{6,8},{8,6},{10,4},{12,2},{14,0},{1,15},{3,13... | collective-permute-start | bytes 1179656 | tf_op jit(solution)/shard_map/ppermute | solution.py:31
  68.2 0.1 collective-permute-start.9
  68.3 2.8 %collective-permute-start.6 = (bf16[256,768]{1,0:T(8,128)(2,1)}, bf16[256,768]{1,0:T(8,128)(2,1)S(1)}, u32[]{:S(2)}, u32[]{:S(2)}) collective-permute-start(bf16[256,768]{1,0:T(8,128)(2,1)} %get-tuple-element.41), channel_id=1, source_target_pairs={{0,10},{2,8},{4,14},{6,12},{8,2},{10,0},{12,6},{14,4},{1,11},{3,9}... | collective-permute-start | bytes 1179656 | tf_op jit(solution)/shard_map/ppermute | solution.py:31
  71.1 14.6 %shard_map.66 = (bf16[256,768]{1,0:T(8,128)(2,1)}, bf16[256,768]{1,0:T(8,128)(2,1)}, bf16[256,768]{1,0:T(8,128)(2,1)}, bf16[256,768]{1,0:T(8,128)(2,1)}, bf16[4,256,768]{2,1,0:T(8,128)(2,1)}) custom-call(s32[2,256,8192]{2,1,0:T(8,128)} %samples.5, bf16[2,256,3072]{2,1,0:T(8,128)(2,1)} %collective-permute-done.refs_0_, s32[4,1024]{1,0:T(4,128)} %refs_1_.3, ...), custom_call_target="tpu_custom_call" | custom-call | flops 99999997952 | bytes 1 | tf_op jit(solution)/shard_map/pallas_call | solution.py:199
  85.7 48.3 %collective-permute-done.6.refs_6_ = bf16[256,768]{1,0:T(8,128)(2,1)S(1)} collective-permute-done((bf16[256,768]{1,0:T(8,128)(2,1)}, bf16[256,768]{1,0:T(8,128)(2,1)S(1)}, u32[]{:S(2)}, u32[]{:S(2)}) %collective-permute-start.6) | collective-permute-done | bytes 393248 | tf_op jit(solution)/shard_map/ppermute | solution.py:31
  134.0 6.3 %collective-permute-start.10 = (bf16[256,768]{1,0:T(8,128)(2,1)}, bf16[256,768]{1,0:T(8,128)(2,1)}, u32[]{:S(2)}, u32[]{:S(2)}) collective-permute-start(bf16[256,768]{1,0:T(8,128)(2,1)} %get-tuple-element.47), channel_id=1, source_target_pairs={{0,14},{2,12},{4,10},{6,8},{8,6},{10,4},{12,2},{14,0},{1,15},{3,13... | collective-permute-start | bytes 1179656 | tf_op jit(solution)/shard_map/ppermute | solution.py:31
  140.3 0.1 collective-permute-start.1
  140.4 5.6 %all-to-all-start = ((bf16[4,256,768]{2,1,0:T(8,128)(2,1)}), bf16[4,256,768]{2,1,0:T(8,128)(2,1)}, u32[]{:S(2)}, u32[]{:S(2)}) async-start(bf16[4,256,768]{2,1,0:T(8,128)(2,1)} %get-tuple-element.31), calls=%async_computation | async-start | bytes 3145728 | tf_op jit(solution)/shard_map/all_to_all | solution.py:445
  146.0 3.1 %collective-permute-start.4 = (bf16[256,768]{1,0:T(8,128)(2,1)}, bf16[256,768]{1,0:T(8,128)(2,1)}, u32[]{:S(2)}, u32[]{:S(2)}) collective-permute-start(bf16[256,768]{1,0:T(8,128)(2,1)} %get-tuple-element.37), channel_id=1, source_target_pairs={{0,10},{2,8},{4,14},{6,12},{8,2},{10,0},{12,6},{14,4},{1,11},{3,9}... | collective-permute-start | bytes 1179656 | tf_op jit(solution)/shard_map/ppermute | solution.py:31
  149.1 0.7 copy-done.2
  149.8 4.7 %shard_map.67.refs_0_ = bf16[8,256,1280]{2,1,0:T(8,128)(2,1)} custom-call(bf16[4,256,1280]{2,1,0:T(8,128)(2,1)} %copy-done, bf16[4,256,1280]{2,1,0:T(8,128)(2,1)} %copy-done, bf16[4,256,1280]{2,1,0:T(8,128)(2,1)} %copy-done, bf16[4,256,1280]{2,1,0:T(8,128)(2,1)} %copy-done, bf16[256,768]{1,0:T(8,128)(2,1)} %copy-done.1, ...), custom_call_target="tpu_custom_call" | custom-call | flops 1 | bytes 1 | tf_op jit(solution)/shard_map/pallas_call | solution.py:247
  154.6 12.0 %shard_map.68.refs_1_ = f32[18,512,256]{2,1,0:T(8,128)} custom-call(s32[18]{0:T(128)} %get-tuple-element.54.first, s32[18]{0:T(128)} %get-tuple-element.53.second, bf16[8,256,1280]{2,1,0:T(8,128)(2,1)} %shard_map.67.refs_0_), custom_call_target="tpu_custom_call" | custom-call | flops 99999997952 | bytes 1 | tf_op jit(solution)/shard_map/pallas_call | solution.py:333
  166.6 2.3 copy-done.10
  168.8 14.9 %shard_map.69.refs_8_.refs_1_ = f32[18,512,256]{2,1,0:T(8,128)} custom-call(s32[18]{0:T(128)} %get-tuple-element.54.first, s32[18]{0:T(128)} %get-tuple-element.53.second, bf16[8,256,1280]{2,1,0:T(8,128)(2,1)} %copy-done.10, f32[18,512,256]{2,1,0:T(8,128)} %shard_map.68.refs_1_), custom_call_target="tpu_custom_call" | custom-call | flops 99999997952 | bytes 1 | tf_op jit(solution)/shard_map/pallas_call | solution.py:333
  183.7 16.8 %collective-permute-done.1.refs_4_ = bf16[256,768]{1,0:T(8,128)(2,1)} collective-permute-done((bf16[256,768]{1,0:T(8,128)(2,1)}, bf16[256,768]{1,0:T(8,128)(2,1)}, u32[]{:S(2)}, u32[]{:S(2)}) %collective-permute-start.1) | collective-permute-done | bytes 393248 | tf_op jit(solution)/shard_map/ppermute | solution.py:31
  200.5 7.8 %collective-permute-done.4.refs_5_ = bf16[256,768]{1,0:T(8,128)(2,1)} collective-permute-done((bf16[256,768]{1,0:T(8,128)(2,1)}, bf16[256,768]{1,0:T(8,128)(2,1)}, u32[]{:S(2)}, u32[]{:S(2)}) %collective-permute-start.4) | collective-permute-done | bytes 393248 | tf_op jit(solution)/shard_map/ppermute | solution.py:31
  208.3 2.8 %shard_map.70.refs_0_ = bf16[8,256,768]{2,1,0:T(8,128)(2,1)} custom-call(bf16[4,256,768]{2,1,0:T(8,128)(2,1)} %all-to-all-done.refs_0_.refs_1_.refs_2_.refs_3_, bf16[4,256,768]{2,1,0:T(8,128)(2,1)} %all-to-all-done.refs_0_.refs_1_.refs_2_.refs_3_, bf16[4,256,768]{2,1,0:T(8,128)(2,1)} %all-to-all-done.refs_0_.refs_1_.refs_2_.refs_3_, ...), custom_call_target="tpu_custom_call" | custom-call | flops 1 | bytes 1 | tf_op jit(solution)/shard_map/pallas_call | solution.py:247
  211.1 0.1 collective-permute-start.14
  211.2 11.8 %shard_map.71.refs_1_ = f32[18,512,256]{2,1,0:T(8,128)} custom-call(s32[18]{0:T(128)} %get-tuple-element.54.first, s32[18]{0:T(128)} %get-tuple-element.53.second, bf16[8,256,768]{2,1,0:T(8,128)(2,1)} %shard_map.70.refs_0_, f32[18,512,256]{2,1,0:T(8,128)} %shard_map.69.refs_8_.refs_1_), custom_call_target="tpu_custom_call" | custom-call | flops 99999997952 | bytes 1 | tf_op jit(solution)/shard_map/pallas_call | solution.py:333
  223.0 1.6 copy-done.11
  224.6 11.4 %shard_map.72 = bf16[18,512,256]{2,1,0:T(8,128)(2,1)} custom-call(s32[18]{0:T(128)} %get-tuple-element.54.first, s32[18]{0:T(128)} %get-tuple-element.53.second, bf16[8,256,768]{2,1,0:T(8,128)(2,1)} %copy-done.11, f32[18,512,256]{2,1,0:T(8,128)} %shard_map.71.refs_1_), custom_call_target="tpu_custom_call" | custom-call | flops 99999997952 | bytes 1 | tf_op jit(solution)/shard_map/pallas_call | solution.py:333
  (40 shorter events, 0.2 us)
Async XLA Ops:
  8.9 36.2 %collective-permute-start.5 = (bf16[256,512]{1,0:T(8,128)(2,1)}, bf16[256,512]{1,0:T(8,128)(2,1)S(1)}, u32[]{:S(2)}, u32[]{:S(2)}) collective-permute-start(bf16[256,512]{1,0:T(8,128)(2,1)} %get-tuple-element.40), channel_id=1, source_target_pairs={{0,10},{2,8},{4,14},{6,12},{8,2},{10,0},{12,6},{14,4},{1,11},{3,9}... | collective-permute-start | bytes 786440 | tf_op jit(solution)/shard_map/ppermute | solution.py:31
  13.9 31.1 %collective-permute-start.8 = (bf16[256,512]{1,0:T(8,128)(2,1)}, bf16[256,512]{1,0:T(8,128)(2,1)S(1)}, u32[]{:S(2)}, u32[]{:S(2)}) collective-permute-start(bf16[256,512]{1,0:T(8,128)(2,1)} %get-tuple-element.45), channel_id=1, source_target_pairs={{0,12},{2,14},{4,8},{6,10},{8,4},{10,6},{12,0},{14,2},{1,13},{3,15... | collective-permute-start | bytes 786440 | tf_op jit(solution)/shard_map/ppermute | solution.py:31
  15.3 29.8 %collective-permute-start.11 = (bf16[256,512]{1,0:T(8,128)(2,1)}, bf16[256,512]{1,0:T(8,128)(2,1)S(1)}, u32[]{:S(2)}, u32[]{:S(2)}) collective-permute-start(bf16[256,512]{1,0:T(8,128)(2,1)} %get-tuple-element.49), channel_id=1, source_target_pairs={{0,14},{2,12},{4,10},{6,8},{8,6},{10,4},{12,2},{14,0},{1,15},{3,13... | collective-permute-start | bytes 786440 | tf_op jit(solution)/shard_map/ppermute | solution.py:31
  17.7 45.4 %collective-permute-start.2 = (bf16[256,512]{1,0:T(8,128)(2,1)}, bf16[256,512]{1,0:T(8,128)(2,1)}, u32[]{:S(2)}, u32[]{:S(2)}) collective-permute-start(bf16[256,512]{1,0:T(8,128)(2,1)} %get-tuple-element.29.refs_2_), channel_id=1, source_target_pairs={{0,8},{2,10},{4,12},{6,14},{8,0},{10,2},{12,4},{14,6},{1,9},{3,11}... | collective-permute-start | bytes 786440 | tf_op jit(solution)/shard_map/ppermute | solution.py:31
  17.7 53.4 %collective-permute-start = (bf16[2,256,3072]{2,1,0:T(8,128)(2,1)}, bf16[2,256,3072]{2,1,0:T(8,128)(2,1)}, u32[]{:S(2)}, u32[]{:S(2)}) collective-permute-start(bf16[2,256,3072]{2,1,0:T(8,128)(2,1)} %get-tuple-element.28), channel_id=1, source_target_pairs={{0,1},{2,3},{4,5},{6,7},{8,9},{10,11},{12,13},{14,15},{16,17},{18,... | collective-permute-start | bytes 9437192 | tf_op jit(solution)/shard_map/ppermute | solution.py:27
  39.9 4.3 %copy-start.12 = (s32[36]{0:T(128)S(1)}, s32[36]{0:T(128)}, u32[]{:S(2)}) copy-start(s32[36]{0:T(128)} %param.8) | copy-start | bytes 436
  39.9 4.4 %copy-start.8 = (s32[36]{0:T(128)S(1)}, s32[36]{0:T(128)}, u32[]{:S(2)}) copy-start(s32[36]{0:T(128)} %constant.74.clone) | copy-start | bytes 436
  39.9 4.4 %copy-start.9 = (s32[36]{0:T(128)S(1)}, s32[36]{0:T(128)}, u32[]{:S(2)}) copy-start(s32[36]{0:T(128)} %constant.73.clone) | copy-start | bytes 436
  39.9 100.5 %all-to-all-start.1 = ((bf16[4,256,1280]{2,1,0:T(8,128)(2,1)}), bf16[4,256,1280]{2,1,0:T(8,128)(2,1)S(1)}, u32[]{:S(2)}, u32[]{:S(2)}) async-start(bf16[4,256,1280]{2,1,0:T(8,128)(2,1)} %get-tuple-element.36), calls=%async_computation.1 | async-start | bytes 5242880 | tf_op jit(solution)/shard_map/all_to_all | solution.py:445
  45.0 18.1 %copy-start.5 = (bf16[256,512]{1,0:T(8,128)(2,1)}, bf16[256,512]{1,0:T(8,128)(2,1)S(1)}, u32[]{:S(2)}) copy-start(bf16[256,512]{1,0:T(8,128)(2,1)S(1)} %collective-permute-done.5.refs_7_) | copy-start | bytes 786436
  45.1 18.1 %copy-start.6 = (bf16[256,512]{1,0:T(8,128)(2,1)}, bf16[256,512]{1,0:T(8,128)(2,1)S(1)}, u32[]{:S(2)}) copy-start(bf16[256,512]{1,0:T(8,128)(2,1)S(1)} %collective-permute-done.8.refs_9_) | copy-start | bytes 786436
  45.1 18.0 %copy-start.7 = (bf16[256,512]{1,0:T(8,128)(2,1)}, bf16[256,512]{1,0:T(8,128)(2,1)S(1)}, u32[]{:S(2)}) copy-start(bf16[256,512]{1,0:T(8,128)(2,1)S(1)} %collective-permute-done.11.refs_11_) | copy-start | bytes 786436
  63.1 82.8 %collective-permute-start.3 = (bf16[256,768]{1,0:T(8,128)(2,1)}, bf16[256,768]{1,0:T(8,128)(2,1)S(1)}, u32[]{:S(2)}, u32[]{:S(2)}) collective-permute-start(bf16[256,768]{1,0:T(8,128)(2,1)} %get-tuple-element.35.refs_3_), channel_id=1, source_target_pairs={{0,8},{2,10},{4,12},{6,14},{8,0},{10,2},{12,4},{14,6},{1,9},{3,11}... | collective-permute-start | bytes 1179656 | tf_op jit(solution)/shard_map/ppermute | solution.py:31
  63.2 85.9 %collective-permute-start.12 = (bf16[256,768]{1,0:T(8,128)(2,1)}, bf16[256,768]{1,0:T(8,128)(2,1)S(1)}, u32[]{:S(2)}, u32[]{:S(2)}) collective-permute-start(bf16[256,768]{1,0:T(8,128)(2,1)} %get-tuple-element.50), channel_id=1, source_target_pairs={{0,14},{2,12},{4,10},{6,8},{8,6},{10,4},{12,2},{14,0},{1,15},{3,13... | collective-permute-start | bytes 1179656 | tf_op jit(solution)/shard_map/ppermute | solution.py:31
  68.2 65.9 %collective-permute-start.9 = (bf16[256,768]{1,0:T(8,128)(2,1)}, bf16[256,768]{1,0:T(8,128)(2,1)S(1)}, u32[]{:S(2)}, u32[]{:S(2)}) collective-permute-start(bf16[256,768]{1,0:T(8,128)(2,1)} %get-tuple-element.46), channel_id=1, source_target_pairs={{0,12},{2,14},{4,8},{6,10},{8,4},{10,6},{12,0},{14,2},{1,13},{3,15... | collective-permute-start | bytes 1179656 | tf_op jit(solution)/shard_map/ppermute | solution.py:31
  68.3 65.7 %collective-permute-start.6 = (bf16[256,768]{1,0:T(8,128)(2,1)}, bf16[256,768]{1,0:T(8,128)(2,1)S(1)}, u32[]{:S(2)}, u32[]{:S(2)}) collective-permute-start(bf16[256,768]{1,0:T(8,128)(2,1)} %get-tuple-element.41), channel_id=1, source_target_pairs={{0,10},{2,8},{4,14},{6,12},{8,2},{10,0},{12,6},{14,4},{1,11},{3,9}... | collective-permute-start | bytes 1179656 | tf_op jit(solution)/shard_map/ppermute | solution.py:31
  134.0 6.3 %copy-start.4 = (bf16[256,768]{1,0:T(8,128)(2,1)}, bf16[256,768]{1,0:T(8,128)(2,1)S(1)}, u32[]{:S(2)}) copy-start(bf16[256,768]{1,0:T(8,128)(2,1)S(1)} %collective-permute-done.6.refs_6_) | copy-start | bytes 1179652
  134.0 6.3 %copy-start.3 = (bf16[256,768]{1,0:T(8,128)(2,1)}, bf16[256,768]{1,0:T(8,128)(2,1)S(1)}, u32[]{:S(2)}) copy-start(bf16[256,768]{1,0:T(8,128)(2,1)S(1)} %collective-permute-done.9.refs_8_) | copy-start | bytes 1179652
  134.0 49.7 %collective-permute-start.10 = (bf16[256,768]{1,0:T(8,128)(2,1)}, bf16[256,768]{1,0:T(8,128)(2,1)}, u32[]{:S(2)}, u32[]{:S(2)}) collective-permute-start(bf16[256,768]{1,0:T(8,128)(2,1)} %get-tuple-element.47), channel_id=1, source_target_pairs={{0,14},{2,12},{4,10},{6,8},{8,6},{10,4},{12,2},{14,0},{1,15},{3,13... | collective-permute-start | bytes 1179656 | tf_op jit(solution)/shard_map/ppermute | solution.py:31
  140.3 43.5 %collective-permute-start.7 = (bf16[256,768]{1,0:T(8,128)(2,1)}, bf16[256,768]{1,0:T(8,128)(2,1)}, u32[]{:S(2)}, u32[]{:S(2)}) collective-permute-start(bf16[256,768]{1,0:T(8,128)(2,1)} %get-tuple-element.42), channel_id=1, source_target_pairs={{0,12},{2,14},{4,8},{6,10},{8,4},{10,6},{12,0},{14,2},{1,13},{3,15... | collective-permute-start | bytes 1179656 | tf_op jit(solution)/shard_map/ppermute | solution.py:31
  140.3 60.2 %collective-permute-start.1 = (bf16[256,768]{1,0:T(8,128)(2,1)}, bf16[256,768]{1,0:T(8,128)(2,1)}, u32[]{:S(2)}, u32[]{:S(2)}) collective-permute-start(bf16[256,768]{1,0:T(8,128)(2,1)} %get-tuple-element.33), channel_id=1, source_target_pairs={{0,8},{2,10},{4,12},{6,14},{8,0},{10,2},{12,4},{14,6},{1,9},{3,11}... | collective-permute-start | bytes 1179656 | tf_op jit(solution)/shard_map/ppermute | solution.py:31
  140.4 8.7 %copy-start = (bf16[4,256,1280]{2,1,0:T(8,128)(2,1)}, bf16[4,256,1280]{2,1,0:T(8,128)(2,1)S(1)}, u32[]{:S(2)}) copy-start(bf16[4,256,1280]{2,1,0:T(8,128)(2,1)S(1)} %all-to-all-done.1.refs_0_.refs_1_.refs_2_.refs_3_) | copy-start | bytes 7864324
  140.4 67.9 %all-to-all-start = ((bf16[4,256,768]{2,1,0:T(8,128)(2,1)}), bf16[4,256,768]{2,1,0:T(8,128)(2,1)}, u32[]{:S(2)}, u32[]{:S(2)}) async-start(bf16[4,256,768]{2,1,0:T(8,128)(2,1)} %get-tuple-element.31), calls=%async_computation | async-start | bytes 3145728 | tf_op jit(solution)/shard_map/all_to_all | solution.py:445
  146.0 3.1 %copy-start.1 = (bf16[256,768]{1,0:T(8,128)(2,1)}, bf16[256,768]{1,0:T(8,128)(2,1)S(1)}, u32[]{:S(2)}) copy-start(bf16[256,768]{1,0:T(8,128)(2,1)S(1)} %collective-permute-done.3.refs_4_) | copy-start | bytes 1179652
  146.0 62.4 %collective-permute-start.4 = (bf16[256,768]{1,0:T(8,128)(2,1)}, bf16[256,768]{1,0:T(8,128)(2,1)}, u32[]{:S(2)}, u32[]{:S(2)}) collective-permute-start(bf16[256,768]{1,0:T(8,128)(2,1)} %get-tuple-element.37), channel_id=1, source_target_pairs={{0,10},{2,8},{4,14},{6,12},{8,2},{10,0},{12,6},{14,4},{1,11},{3,9}... | collective-permute-start | bytes 1179656 | tf_op jit(solution)/shard_map/ppermute | solution.py:31
  149.1 0.7 copy-start.2
  154.5 12.0 %collective-permute-start.13 = (bf16[8,256,1280]{2,1,0:T(8,128)(2,1)}, bf16[8,256,1280]{2,1,0:T(8,128)(2,1)S(1)}, u32[]{:S(2)}, u32[]{:S(2)}) collective-permute-start(bf16[8,256,1280]{2,1,0:T(8,128)(2,1)} %shard_map.67.refs_0_), channel_id=1, source_target_pairs={{0,1},{1,0},{2,3},{3,2},{4,5},{5,4},{6,7},{7,6},{8,9},{9,8},{10,11... | collective-permute-start | bytes 15728648 | tf_op jit(solution)/shard_map/ppermute | solution.py:31
  166.6 2.3 copy-start.10
  211.1 11.9 %collective-permute-start.14 = (bf16[8,256,768]{2,1,0:T(8,128)(2,1)}, bf16[8,256,768]{2,1,0:T(8,128)(2,1)S(1)}, u32[]{:S(2)}, u32[]{:S(2)}) collective-permute-start(bf16[8,256,768]{2,1,0:T(8,128)(2,1)} %shard_map.70.refs_0_), channel_id=1, source_target_pairs={{0,1},{1,0},{2,3},{3,2},{4,5},{5,4},{6,7},{7,6},{8,9},{9,8},{10,11... | collective-permute-start | bytes 9437192 | tf_op jit(solution)/shard_map/ppermute | solution.py:31
  223.0 1.6 copy-start.11

commit v2 on v1

--- a/solution.py
+++ b/solution.py
@@ -16,7 +16,7 @@
 LANES = 128
 ROWS = 32
 SCALE = 2.0**-14
-VMEM_LIMIT = 56 * 1024 * 1024
+VMEM_LIMIT = 60 * 1024 * 1024
 
 PLAN = (2, 3, 3)
 
@@ -52,9 +52,9 @@
     if gated:
         refs.pop(0)
     pieces = [[refs.pop(0) for _ in widths] for widths in sends[: groups // 2]]
-    near_out = refs.pop(0) if sends[-1] else None
+    near_out = [refs.pop(0) for _ in sends[-1]]
     for j in range(groups // 2, groups):
-        pieces.append([near_out.at[j - groups // 2]] if near_out is not None else [])
+        pieces.append([out.at[j - groups // 2] for out in near_out])
     rim_out = refs.pop(0) if with_rim else None
     held = refs.pop(0)
     held_rim = refs.pop(0) if early else None
@@ -176,8 +176,8 @@
     for widths in sends[: groups // 2]:
         for width in widths:
             out_shape.append(jax.ShapeDtypeStruct((BLOCK, width * columns), jnp.bfloat16))
-    if sends[-1]:
-        out_shape.append(jax.ShapeDtypeStruct((groups // 2, BLOCK, sends[-1][0] * columns), jnp.bfloat16))
+    for width in sends[-1]:
+        out_shape.append(jax.ShapeDtypeStruct((groups // 2, BLOCK, width * columns), jnp.bfloat16))
     scratch = [pltpu.VMEM((2, BLOCK, own * fft_size), jnp.int32)]
     if early:
         scratch.append(pltpu.VMEM((2, BLOCK, early * fft_size), jnp.bfloat16))
@@ -207,7 +207,7 @@
         )(*operands)
     )
     pieces = [[results.pop(0) for _ in widths] for widths in sends[: groups // 2]]
-    return pieces, results[0] if with_rim or sends[-1] else None
+    return pieces, results
 
 
 def gather_kernel(layout, *refs):
@@ -260,20 +260,20 @@
 
 
 def tile_kernel(geometry, first, second, *refs):
-    count, has_sums, factor = geometry
-    blocks = refs[:count]
-    sums = refs[count] if has_sums else None
-    refs = refs[count + has_sums :]
+    layout, inputs, has_sums, factor = geometry
+    count = len(layout)
+    arrays = refs[:inputs]
+    sums = refs[inputs] if has_sums else None
+    refs = refs[inputs + has_sums :]
     out, held, totals = refs[0], refs[1 : 1 + count], refs[1 + count]
     finished = refs[2 + count]
     block_sems, sum_sems, out_sems = refs[-3:]
     slots = totals.shape[0]
-    numbers = blocks[0].shape[0]
-    block_copies = [
-        pltpu.make_async_copy(blocks[k].at[d], held[k].at[d], block_sems.at[k, d])
-        for d in range(numbers)
-        for k in range(count)
-    ]
+    block_copies = []
+    for k, places in enumerate(layout):
+        for d, (number, at) in enumerate(places):
+            source = arrays[number] if at is None else arrays[number].at[at]
+            block_copies.append(pltpu.make_async_copy(source, held[k].at[d], block_sems.at[k, d]))
     for copy in block_copies:
         copy.start()
 
@@ -320,18 +320,28 @@
     slots = first.shape[0]
     anywhere = pl.BlockSpec(memory_space=pl.ANY)
     smem = pl.BlockSpec(memory_space=pltpu.SMEM)
-    operands = list(blocks) + ([] if sums is None else [sums])
-    width = sum(block.shape[2] for block in blocks)
+    operands, layout = [], []
+    for places in blocks:
+        if not isinstance(places, list):
+            places = [(places, d) for d in range(places.shape[0])]
+        numbered = []
+        for array, at in places:
+            number = next((n for n, known in enumerate(operands) if known is array), len(operands))
+            operands += [array] if number == len(operands) else []
+            numbered.append((number, at))
+        layout.append(tuple(numbered))
+    inputs = len(operands)
+    operands += [] if sums is None else [sums]
     shape = (slots, 2 * BLOCK, BLOCK)
     kind = jnp.float32 if factor is None else jnp.bfloat16
-    scratch = [pltpu.VMEM(block.shape, block.dtype) for block in blocks] + [pltpu.VMEM(shape, jnp.float32), pltpu.VMEM(shape, kind)]
+    scratch = [pltpu.VMEM((len(places),) + operands[places[0][0]].shape[-2:], jnp.bfloat16) for places in layout] + [pltpu.VMEM(shape, jnp.float32), pltpu.VMEM(shape, kind)]
     scratch += [
-        pltpu.SemaphoreType.DMA((len(blocks), blocks[0].shape[0])),
+        pltpu.SemaphoreType.DMA((len(layout), len(layout[0]))),
         pltpu.SemaphoreType.DMA((slots,)),
         pltpu.SemaphoreType.DMA((slots,)),
     ]
     return pl.pallas_call(
-        functools.partial(tile_kernel, (len(blocks), sums is not None, factor)),
+        functools.partial(tile_kernel, (tuple(layout), inputs, sums is not None, factor)),
         in_specs=[smem, smem] + [anywhere] * len(operands),
         out_specs=anywhere,
         out_shape=jax.ShapeDtypeStruct(shape, kind),
@@ -448,31 +458,35 @@
     FIRST, SECOND, THIRD = PLAN
     end = samples.shape[2] // fft_size
     start_a, start_b = end - FIRST, end - FIRST - SECOND
-    made_a, rim_here = front(samples, None, taps, table, None, start_a, FIRST, ((FIRST,),) * far + ((),) * far, True)
+    made_a, (rim_here,) = front(samples, None, taps, table, None, start_a, FIRST, ((FIRST,),) * far + ((),) * far, True)
     a = {mask: to(mask, made_a[mask - far][0]) for mask in apart}
     rim = passed_along(rim_here, "pair", 1)
-    sends = ((SECOND,),) * far + ((SECOND + FIRST,),) * far
-    made_b, near_b = front(samples, None, taps, table, made_a[0][0], start_b, SECOND + FIRST, sends, False)
-    b = {mask: to(mask, after(made_b[mask - far][0], a[mask])) for mask in apart}
-    ab = among_near(near_b)
+    sends = ((SECOND,),) * far + ((SECOND, FIRST),) * far
+    made_b, (near_b, near_a) = front(samples, rim, taps, table, made_a[0][0], start_b, SECOND + FIRST, sends, False)
+    b = {}
+    for mask, gate in zip(apart, [a[far], a[far + 1], a[far + 2], a[far + 3]]):
+        b[mask] = to(mask, after(made_b[mask - far][0], gate))
+    aa = among_near(near_a)
+    bb = among_near(near_b)
     sends = ((THIRD,),) * far + ((THIRD,),) * far
-    made_c, near_c = front(samples, rim, taps, table, made_b[0][0], 0, THIRD, sends, False)
-    c = {}
-    for mask, gates in zip(apart, [(rim,), (b[far], ab)] + [(b[mask],) for mask in apart][1:]):
-        c[mask] = to(mask, after(made_c[mask - far][0], *gates))
-    cc = among_near(near_c)
-    blocks = [[(ab, k, 0, SECOND + FIRST)] for k in range(far)]
-    blocks += [[(b[mask], None, 0, SECOND), (a[mask], None, 0, FIRST)] for mask in apart]
-    mine = gathered(blocks, None)
+    made_c, (near_c,) = front(samples, rim, taps, table, made_b[0][0], 0, THIRD, sends, False)
+    mine = gathered([[(aa, k, 0, FIRST)] for k in range(far)] + [[(a[mask], None, 0, FIRST)] for mask in apart], made_c[0][0])
     other = other_core(mine)
     sums = tiles(first, second, [mine], None, None)
     sums = tiles(first, second, [other], sums, None)
-    blocks = [[(cc, k, 0, THIRD)] for k in range(far)] + [[(c[mask], None, 0, THIRD)] for mask in apart]
-    mine = gathered(blocks, sums)
+    c = {}
+    for mask, gate in zip(apart, [rim, b[far], b[far + 2], b[far + 3]]):
+        c[mask] = to(mask, after(made_c[mask - far][0], gate))
+    cc = among_near(near_c)
+    mine = gathered([[(bb, k, 0, SECOND)] for k in range(far)] + [[(b[mask], None, 0, SECOND)] for mask in apart], sums)
     other = other_core(mine)
     sums = tiles(first, second, [mine], sums, None)
+    sums = tiles(first, second, [other], sums, None)
+    last = [(cc, k) for k in range(far)] + [(c[mask], None) for mask in apart]
+    near_there = other_core(cc)
+    there = [(near_there, k) for k in range(far)] + [(other_core(after(c[mask], sums)), None) for mask in apart]
     factor = 1.0 / (end * pair_size * (fft_size // groups))
-    sums = tiles(first, second, [other], sums, factor)
+    sums = tiles(first, second, [last, there], sums, factor)
     return sums.reshape(1, slots, 2, BLOCK, BLOCK)
 
 

time: 237 us -> 223 us (0.941)
  waiting for transfers between devices: 91 us -> 43.5 us
  starting transfers between devices: 39.1 us -> 71 us
  Pallas kernels: 100 us -> 105 us
  local copies, waits for them, and re-layouts: 4.78 us -> 1.48 us
    ppermute x14 -> x19, waiting for transfers between devices: 91 us -> 27 us  [swapped_with(): lax.ppermute(block, axis, [(i, i ^ mask) for i in range(lax.axis_size(axi...]
    ppermute x14 -> x19, starting transfers between devices: 26.3 us -> 56.1 us  [swapped_with(): lax.ppermute(block, axis, [(i, i ^ mask) for i in range(lax.axis_size(axi...]
    all_to_all x2 -> x3, waiting for transfers between devices: 0.01 us -> 16.5 us  [among_near(): lax.all_to_all(value, 'chan', 0, 0, axis_index_groups=halves, tiled=True)]
    pallas_call x4 -> x5, Pallas kernels: 50 us -> 57.5 us  [tiles(): pl.pallas_call(functools.partial(tile_kernel, (tuple(layout), inputs, sum...]
    unnamed x26, local copies, waits for them, and re-layouts: 4.7 us -> 1.4 us
    all_to_all x2 -> x3, starting transfers between devices: 9.83 us -> 11.8 us  [among_near(): lax.all_to_all(value, 'chan', 0, 0, axis_index_groups=halves, tiled=True)]
  transfers between devices with their start and end apart: 17 -> 23, of which waited for: 4 -> 9; matrix products, arithmetic and copies ran while one was open for 0% -> 0% of each run, Pallas kernels for 33% -> 36%
where the time goes in v2:
time: 223 us
  Pallas kernels  105 us (47%)
  starting transfers between devices  71 us (32%)
  waiting for transfers between devices  43.5 us (20%)
    pallas_call x5, Pallas kernels, tiles(): pl.pallas_call(functools.partial(tile_kernel, (tuple(layout), inputs, sum...  57.5 us
    ppermute x19, starting transfers between devices, swapped_with(): lax.ppermute(block, axis, [(i, i ^ mask) for i in range(lax.axis_size(axi...  56.1 us
    pallas_call x3, Pallas kernels, front(): pl.pallas_call(functools.partial(front_kernel, geometry), in_specs=in_spe...  42.8 us
    ppermute x19, waiting for transfers between devices, swapped_with(): lax.ppermute(block, axis, [(i, i ^ mask) for i in range(lax.axis_size(axi...  27 us
    all_to_all x3, waiting for transfers between devices, among_near(): lax.all_to_all(value, 'chan', 0, 0, axis_index_groups=halves, tiled=True)  16.5 us
    all_to_all x3, starting transfers between devices, among_near(): lax.all_to_all(value, 'chan', 0, 0, axis_index_groups=halves, tiled=True)  11.8 us
    pallas_call x2, Pallas kernels, gathered(): pl.pallas_call(functools.partial(gather_kernel, tuple(layout)), in_specs=...  5.19 us
  transfers between devices with their start and end apart: 23, of which 9 were waited for; matrix products, arithmetic and copies ran while one was open for 0% of the time, Pallas kernels for 36%

profile of v2, /device:TPU:0, one launch (start us, length us, event | category | flops | bytes accessed | tf_op | source)
XLA Modules:
  0.0 222.6 jit_solution(10128343642034273670)
XLA Ops:
  0.0 8.9 %shard_map.64 = (bf16[256,512]{1,0:T(8,128)(2,1)}, bf16[256,512]{1,0:T(8,128)(2,1)}, bf16[256,512]{1,0:T(8,128)(2,1)}, bf16[256,512]{1,0:T(8,128)(2,1)}, bf16[2,256,3072]{2,1,0:T(8,128)(2,1)}) custom-call(s32[2,256,8192]{2,1,0:T(8,128)} %samples.5, s32[4,1024]{1,0:T(4,128)} %refs_1_.3, bf16[8,1024,256]{2,1,0:T(8,128)(2,1)} %constant.72.clone.refs_1_.refs_2_), custom_call_target="tpu_custom_call" | custom-call | flops 99999997952 | bytes 1 | tf_op jit(solution)/shard_map/pallas_call | solution.py:199
  8.9 5.1 %collective-permute-start.5 = (bf16[256,512]{1,0:T(8,128)(2,1)}, bf16[256,512]{1,0:T(8,128)(2,1)S(1)}, u32[]{:S(2)}, u32[]{:S(2)}) collective-permute-start(bf16[256,512]{1,0:T(8,128)(2,1)} %get-tuple-element.44), channel_id=1, source_target_pairs={{0,12},{2,14},{4,8},{6,10},{8,4},{10,6},{12,0},{14,2},{1,13},{3,15... | collective-permute-start | bytes 786440 | tf_op jit(solution)/shard_map/ppermute | solution.py:31
  14.0 1.2 collective-permute-start.8
  15.2 0.7 collective-permute-start.12
  15.9 2.0 collective-permute-start.2
  17.9 3.1 %collective-permute-start = (bf16[2,256,3072]{2,1,0:T(8,128)(2,1)}, bf16[2,256,3072]{2,1,0:T(8,128)(2,1)}, u32[]{:S(2)}, u32[]{:S(2)}) collective-permute-start(bf16[2,256,3072]{2,1,0:T(8,128)(2,1)} %get-tuple-element.33), channel_id=1, source_target_pairs={{0,1},{2,3},{4,5},{6,7},{8,9},{10,11},{12,13},{14,15},{16,17},{18,... | collective-permute-start | bytes 9437192 | tf_op jit(solution)/shard_map/ppermute | solution.py:27
  20.9 19.4 %shard_map.65 = (bf16[256,768]{1,0:T(8,128)(2,1)}, bf16[256,768]{1,0:T(8,128)(2,1)}, bf16[256,768]{1,0:T(8,128)(2,1)}, bf16[256,768]{1,0:T(8,128)(2,1)}, bf16[4,...) custom-call(s32[2,256,8192]{2,1,0:T(8,128)} %samples.5, s32[4,1024]{1,0:T(4,128)} %refs_1_.3, ...), custom_call_target="tpu_custom_call" | custom-call | flops 99999997952 | bytes 1 | tf_op jit(solution)/shard_map/pallas_call | solution.py:199
  40.3 3.6 %all-to-all-start.2 = ((bf16[4,256,512]{2,1,0:T(8,128)(2,1)}), bf16[4,256,512]{2,1,0:T(8,128)(2,1)S(1)}, u32[]{:S(2)}, u32[]{:S(2)}) async-start(bf16[4,256,512]{2,1,0:T(8,128)(2,1)} %get-tuple-element.56), calls=%async_computation.2 | async-start | bytes 2097152 | tf_op jit(solution)/shard_map/all_to_all | solution.py:455
  44.2 0.6 compare_select_fusion
  44.9 12.5 %collective-permute-done.12.refs_5_ = bf16[256,512]{1,0:T(8,128)(2,1)S(1)} collective-permute-done((bf16[256,512]{1,0:T(8,128)(2,1)}, bf16[256,512]{1,0:T(8,128)(2,1)S(1)}, u32[]{:S(2)}, u32[]{:S(2)}) %collective-permute-start.12) | collective-permute-done | bytes 262176 | tf_op jit(solution)/shard_map/ppermute | solution.py:31
  57.3 3.9 %collective-permute-done.2.refs_4_ = bf16[256,512]{1,0:T(8,128)(2,1)S(1)} collective-permute-done((bf16[256,512]{1,0:T(8,128)(2,1)}, bf16[256,512]{1,0:T(8,128)(2,1)S(1)}, u32[]{:S(2)}, u32[]{:S(2)}) %collective-permute-start.2) | collective-permute-done | bytes 262176 | tf_op jit(solution)/shard_map/ppermute | solution.py:31
  61.2 3.7 %collective-permute-start.13 = (bf16[256,768]{1,0:T(8,128)(2,1)}, bf16[256,768]{1,0:T(8,128)(2,1)}, u32[]{:S(2)}, u32[]{:S(2)}) collective-permute-start(bf16[256,768]{1,0:T(8,128)(2,1)} %get-tuple-element.55), channel_id=1, source_target_pairs={{0,10},{2,8},{4,14},{6,12},{8,2},{10,0},{12,6},{14,4},{1,11},{3,9}... | collective-permute-start | bytes 1179656 | tf_op jit(solution)/shard_map/ppermute | solution.py:31
  64.9 1.3 collective-permute-start.9
  66.2 2.7 %collective-permute-start.6 = (bf16[256,768]{1,0:T(8,128)(2,1)}, bf16[256,768]{1,0:T(8,128)(2,1)}, u32[]{:S(2)}, u32[]{:S(2)}) collective-permute-start(bf16[256,768]{1,0:T(8,128)(2,1)} %get-tuple-element.45), channel_id=1, source_target_pairs={{0,12},{2,14},{4,8},{6,10},{8,4},{10,6},{12,0},{14,2},{1,13},{3,15... | collective-permute-start | bytes 1179656 | tf_op jit(solution)/shard_map/ppermute | solution.py:31
  68.9 14.6 %shard_map.66 = (bf16[256,768]{1,0:T(8,128)(2,1)}, bf16[256,768]{1,0:T(8,128)(2,1)}, bf16[256,768]{1,0:T(8,128)(2,1)}, bf16[256,768]{1,0:T(8,128)(2,1)}, bf16[4,256,768]{2,1,0:T(8,128)(2,1)}) custom-call(s32[2,256,8192]{2,1,0:T(8,128)} %samples.5, bf16[2,256,3072]{2,1,0:T(8,128)(2,1)} %collective-permute-done.refs_0_, s32[4,1024]{1,0:T(4,128)} %refs_1_.3, ...), custom_call_target="tpu_custom_call" | custom-call | flops 99999997952 | bytes 1 | tf_op jit(solution)/shard_map/pallas_call | solution.py:199
  83.5 4.4 %all-to-all-start.1 = ((bf16[4,256,768]{2,1,0:T(8,128)(2,1)}), bf16[4,256,768]{2,1,0:T(8,128)(2,1)}, u32[]{:S(2)}, u32[]{:S(2)}) async-start(bf16[4,256,768]{2,1,0:T(8,128)(2,1)} %get-tuple-element.52), calls=%async_computation.1 | async-start | bytes 3145728 | tf_op jit(solution)/shard_map/all_to_all | solution.py:455
  87.9 2.4 %shard_map.67.refs_0_ = bf16[8,256,512]{2,1,0:T(8,128)(2,1)} custom-call(bf16[4,256,512]{2,1,0:T(8,128)(2,1)} %copy-done, bf16[4,256,512]{2,1,0:T(8,128)(2,1)} %copy-done, bf16[4,256,512]{2,1,0:T(8,128)(2,1)} %copy-done, bf16[4,256,512]{2,1,0:T(8,128)(2,1)} %copy-done, bf16[256,512]{1,0:T(8,128)(2,1)} %copy-done.5, bf16[256,512]{1,0:T(8,128)(2,1)} %copy-done.4, ...), custom_call_target="tpu_custom_call" | custom-call | flops 1 | bytes 1 | tf_op jit(solution)/shard_map/pallas_call | solution.py:247
  90.4 7.5 %shard_map.68.refs_1_ = f32[18,512,256]{2,1,0:T(8,128)} custom-call(s32[18]{0:T(128)} %get-tuple-element.64.first, s32[18]{0:T(128)} %get-tuple-element.63.second, bf16[8,256,512]{2,1,0:T(8,128)(2,1)} %shard_map.67.refs_0_), custom_call_target="tpu_custom_call" | custom-call | flops 99999997952 | bytes 1 | tf_op jit(solution)/shard_map/pallas_call | solution.py:343
  98.1 33.5 %collective-permute-start.1 = (bf16[256,768]{1,0:T(8,128)(2,1)}, bf16[256,768]{1,0:T(8,128)(2,1)}, u32[]{:S(2)}, u32[]{:S(2)}) collective-permute-start(bf16[256,768]{1,0:T(8,128)(2,1)} %get-tuple-element.38.refs_8_), channel_id=1, source_target_pairs={{0,8},{2,10},{4,12},{6,14},{8,0},{10,2},{12,4},{14,6},{1,9},{3,11}... | collective-permute-start | bytes 1179656 | tf_op jit(solution)/shard_map/ppermute | solution.py:31
  131.7 2.2 collective-permute-start.10
  133.8 2.6 %collective-permute-start.7 = (bf16[256,768]{1,0:T(8,128)(2,1)}, bf16[256,768]{1,0:T(8,128)(2,1)}, u32[]{:S(2)}, u32[]{:S(2)}) collective-permute-start(bf16[256,768]{1,0:T(8,128)(2,1)} %get-tuple-element.46), channel_id=1, source_target_pairs={{0,12},{2,14},{4,8},{6,10},{8,4},{10,6},{12,0},{14,2},{1,13},{3,15... | collective-permute-start | bytes 1179656 | tf_op jit(solution)/shard_map/ppermute | solution.py:31
  136.5 1.3 copy-done.8
  137.8 10.3 %shard_map.69.refs_8_.refs_1_ = f32[18,512,256]{2,1,0:T(8,128)} custom-call(s32[18]{0:T(128)} %get-tuple-element.64.first, s32[18]{0:T(128)} %get-tuple-element.63.second, bf16[8,256,512]{2,1,0:T(8,128)(2,1)} %copy-done.8, f32[18,512,256]{2,1,0:T(8,128)} %shard_map.68.refs_1_), custom_call_target="tpu_custom_call" | custom-call | flops 99999997952 | bytes 1 | tf_op jit(solution)/shard_map/pallas_call | solution.py:343
  148.1 3.8 %all-to-all-start = ((bf16[4,256,768]{2,1,0:T(8,128)(2,1)}), bf16[4,256,768]{2,1,0:T(8,128)(2,1)S(1)}, u32[]{:S(2)}, u32[]{:S(2)}) async-start(bf16[4,256,768]{2,1,0:T(8,128)(2,1)} %get-tuple-element.36), calls=%async_computation | async-start | bytes 3145728 | tf_op jit(solution)/shard_map/all_to_all | solution.py:455
  151.9 2.8 %shard_map.70.refs_0_ = bf16[8,256,768]{2,1,0:T(8,128)(2,1)} custom-call(bf16[4,256,768]{2,1,0:T(8,128)(2,1)} %all-to-all-done.1.refs_0_.refs_1_.refs_2_.refs_3_, bf16[4,256,768]{2,1,0:T(8,128)(2,1)} %all-to-all-done.1.refs_0_.refs_1_.refs_2_.refs_3_, bf16[4,256,768]{2,1,0:T(8,128)(2,1)} %all-to-all-done.1.refs_0_.refs_1_.refs_2_.refs_3_, ...), custom_call_target="tpu_custom_call" | custom-call | flops 1 | bytes 1 | tf_op jit(solution)/shard_map/pallas_call | solution.py:247
  154.8 11.8 %shard_map.71.refs_1_ = f32[18,512,256]{2,1,0:T(8,128)} custom-call(s32[18]{0:T(128)} %get-tuple-element.64.first, s32[18]{0:T(128)} %get-tuple-element.63.second, bf16[8,256,768]{2,1,0:T(8,128)(2,1)} %shard_map.70.refs_0_, f32[18,512,256]{2,1,0:T(8,128)} %shard_map.69.refs_8_.refs_1_), custom_call_target="tpu_custom_call" | custom-call | flops 99999997952 | bytes 1 | tf_op jit(solution)/shard_map/pallas_call | solution.py:343
  166.6 16.5 %all-to-all-done.refs_0_ = bf16[4,256,768]{2,1,0:T(8,128)(2,1)S(1)} async-done(((bf16[4,256,768]{2,1,0:T(8,128)(2,1)}), bf16[4,256,768]{2,1,0:T(8,128)(2,1)S(1)}, u32[]{:S(2)}, u32[]{:S(2)}) %all-to-all-start) | async-done | bytes 1572896 | tf_op jit(solution)/shard_map/all_to_all | solution.py:455
  183.1 11.8 %shard_map.72.refs_10_ = f32[18,512,256]{2,1,0:T(8,128)} custom-call(s32[18]{0:T(128)} %get-tuple-element.64.first, s32[18]{0:T(128)} %get-tuple-element.63.second, bf16[8,256,768]{2,1,0:T(8,128)(2,1)} %collective-permute-done.15.refs_0_, f32[18,512,256]{2,1,0:T(8,128)} %shard_map.71.refs_1_), custom_call_target="tpu_custom_call" | custom-call | flops 99999997952 | bytes 1 | tf_op jit(solution)/shard_map/pallas_call | solution.py:343
  194.9 7.6 %collective-permute-done.4.refs_2_ = bf16[256,768]{1,0:T(8,128)(2,1)} collective-permute-done((bf16[256,768]{1,0:T(8,128)(2,1)}, bf16[256,768]{1,0:T(8,128)(2,1)}, u32[]{:S(2)}, u32[]{:S(2)}) %collective-permute-start.4) | collective-permute-done | bytes 393248 | tf_op jit(solution)/shard_map/ppermute | solution.py:31
  203.6 0.9 collective-permute-done.16.refs_6_
  204.5 1.1 collective-permute-done.17.refs_7_
  206.3 16.1 %shard_map.73 = bf16[18,512,256]{2,1,0:T(8,128)(2,1)} custom-call(s32[18]{0:T(128)} %get-tuple-element.64.first, s32[18]{0:T(128)} %get-tuple-element.63.second, bf16[4,256,768]{2,1,0:T(8,128)(2,1)} %copy-done.1, bf16[256,768]{1,0:T(8,128)(2,1)} %collective-permute-done.1.refs_1_, bf16[256,768]{1,0:T(8,128)(2,1)} %collective-permute-done.4.refs_2_, ...), custom_call_target="tpu_custom_call" | custom-call | flops 99999997952 | bytes 1 | tf_op jit(solution)/shard_map/pallas_call | solution.py:343
  (53 shorter events, 2.6 us)
Async XLA Ops:
  8.9 36.0 %collective-permute-start.5 = (bf16[256,512]{1,0:T(8,128)(2,1)}, bf16[256,512]{1,0:T(8,128)(2,1)S(1)}, u32[]{:S(2)}, u32[]{:S(2)}) collective-permute-start(bf16[256,512]{1,0:T(8,128)(2,1)} %get-tuple-element.44), channel_id=1, source_target_pairs={{0,12},{2,14},{4,8},{6,10},{8,4},{10,6},{12,0},{14,2},{1,13},{3,15... | collective-permute-start | bytes 786440 | tf_op jit(solution)/shard_map/ppermute | solution.py:31
  14.0 30.9 %collective-permute-start.8 = (bf16[256,512]{1,0:T(8,128)(2,1)}, bf16[256,512]{1,0:T(8,128)(2,1)S(1)}, u32[]{:S(2)}, u32[]{:S(2)}) collective-permute-start(bf16[256,512]{1,0:T(8,128)(2,1)} %get-tuple-element.49), channel_id=1, source_target_pairs={{0,14},{2,12},{4,10},{6,8},{8,6},{10,4},{12,2},{14,0},{1,15},{3,13... | collective-permute-start | bytes 786440 | tf_op jit(solution)/shard_map/ppermute | solution.py:31
  15.2 42.2 %collective-permute-start.12 = (bf16[256,512]{1,0:T(8,128)(2,1)}, bf16[256,512]{1,0:T(8,128)(2,1)S(1)}, u32[]{:S(2)}, u32[]{:S(2)}) collective-permute-start(bf16[256,512]{1,0:T(8,128)(2,1)} %get-tuple-element.54), channel_id=1, source_target_pairs={{0,10},{2,8},{4,14},{6,12},{8,2},{10,0},{12,6},{14,4},{1,11},{3,9}... | collective-permute-start | bytes 786440 | tf_op jit(solution)/shard_map/ppermute | solution.py:31
  15.9 45.3 %collective-permute-start.2 = (bf16[256,512]{1,0:T(8,128)(2,1)}, bf16[256,512]{1,0:T(8,128)(2,1)S(1)}, u32[]{:S(2)}, u32[]{:S(2)}) collective-permute-start(bf16[256,512]{1,0:T(8,128)(2,1)} %get-tuple-element.34.refs_2_), channel_id=1, source_target_pairs={{0,8},{2,10},{4,12},{6,14},{8,0},{10,2},{12,4},{14,6},{1,9},{3,11}... | collective-permute-start | bytes 786440 | tf_op jit(solution)/shard_map/ppermute | solution.py:31
  17.9 26.1 %copy-start.12 = (s32[36]{0:T(128)S(1)}, s32[36]{0:T(128)}, u32[]{:S(2)}) copy-start(s32[36]{0:T(128)} %param.8) | copy-start | bytes 436
  17.9 26.1 %copy-start.6 = (s32[36]{0:T(128)S(1)}, s32[36]{0:T(128)}, u32[]{:S(2)}) copy-start(s32[36]{0:T(128)} %constant.74.clone) | copy-start | bytes 436
  17.9 26.1 %copy-start.7 = (s32[36]{0:T(128)S(1)}, s32[36]{0:T(128)}, u32[]{:S(2)}) copy-start(s32[36]{0:T(128)} %constant.73.clone) | copy-start | bytes 436
  17.9 51.0 %collective-permute-start = (bf16[2,256,3072]{2,1,0:T(8,128)(2,1)}, bf16[2,256,3072]{2,1,0:T(8,128)(2,1)}, u32[]{:S(2)}, u32[]{:S(2)}) collective-permute-start(bf16[2,256,3072]{2,1,0:T(8,128)(2,1)} %get-tuple-element.33), channel_id=1, source_target_pairs={{0,1},{2,3},{4,5},{6,7},{8,9},{10,11},{12,13},{14,15},{16,17},{18,... | collective-permute-start | bytes 9437192 | tf_op jit(solution)/shard_map/ppermute | solution.py:27
  40.3 43.2 %all-to-all-start.2 = ((bf16[4,256,512]{2,1,0:T(8,128)(2,1)}), bf16[4,256,512]{2,1,0:T(8,128)(2,1)S(1)}, u32[]{:S(2)}, u32[]{:S(2)}) async-start(bf16[4,256,512]{2,1,0:T(8,128)(2,1)} %get-tuple-element.56), calls=%async_computation.2 | async-start | bytes 2097152 | tf_op jit(solution)/shard_map/all_to_all | solution.py:455
  44.8 38.6 %copy-start.2 = (bf16[256,512]{1,0:T(8,128)(2,1)}, bf16[256,512]{1,0:T(8,128)(2,1)S(1)}, u32[]{:S(2)}) copy-start(bf16[256,512]{1,0:T(8,128)(2,1)S(1)} %collective-permute-done.5.refs_6_) | copy-start | bytes 786436
  44.8 38.6 %copy-start.3 = (bf16[256,512]{1,0:T(8,128)(2,1)}, bf16[256,512]{1,0:T(8,128)(2,1)S(1)}, u32[]{:S(2)}) copy-start(bf16[256,512]{1,0:T(8,128)(2,1)S(1)} %collective-permute-done.8.refs_7_) | copy-start | bytes 786436
  57.3 26.1 %copy-start.4 = (bf16[256,512]{1,0:T(8,128)(2,1)}, bf16[256,512]{1,0:T(8,128)(2,1)S(1)}, u32[]{:S(2)}) copy-start(bf16[256,512]{1,0:T(8,128)(2,1)S(1)} %collective-permute-done.12.refs_5_) | copy-start | bytes 786436
  61.2 22.3 %copy-start.5 = (bf16[256,512]{1,0:T(8,128)(2,1)}, bf16[256,512]{1,0:T(8,128)(2,1)S(1)}, u32[]{:S(2)}) copy-start(bf16[256,512]{1,0:T(8,128)(2,1)S(1)} %collective-permute-done.2.refs_4_) | copy-start | bytes 786436
  61.2 72.6 %collective-permute-start.3 = (bf16[256,768]{1,0:T(8,128)(2,1)}, bf16[256,768]{1,0:T(8,128)(2,1)}, u32[]{:S(2)}, u32[]{:S(2)}) collective-permute-start(bf16[256,768]{1,0:T(8,128)(2,1)} %get-tuple-element.40.refs_3_), channel_id=1, source_target_pairs={{0,8},{2,10},{4,12},{6,14},{8,0},{10,2},{12,4},{14,6},{1,9},{3,11}... | collective-permute-start | bytes 1179656 | tf_op jit(solution)/shard_map/ppermute | solution.py:31
  61.2 90.6 %collective-permute-start.13 = (bf16[256,768]{1,0:T(8,128)(2,1)}, bf16[256,768]{1,0:T(8,128)(2,1)}, u32[]{:S(2)}, u32[]{:S(2)}) collective-permute-start(bf16[256,768]{1,0:T(8,128)(2,1)} %get-tuple-element.55), channel_id=1, source_target_pairs={{0,10},{2,8},{4,14},{6,12},{8,2},{10,0},{12,6},{14,4},{1,11},{3,9}... | collective-permute-start | bytes 1179656 | tf_op jit(solution)/shard_map/ppermute | solution.py:31
  64.9 66.7 %collective-permute-start.9 = (bf16[256,768]{1,0:T(8,128)(2,1)}, bf16[256,768]{1,0:T(8,128)(2,1)}, u32[]{:S(2)}, u32[]{:S(2)}) collective-permute-start(bf16[256,768]{1,0:T(8,128)(2,1)} %get-tuple-element.50), channel_id=1, source_target_pairs={{0,14},{2,12},{4,10},{6,8},{8,6},{10,4},{12,2},{14,0},{1,15},{3,13... | collective-permute-start | bytes 1179656 | tf_op jit(solution)/shard_map/ppermute | solution.py:31
  66.2 31.9 %collective-permute-start.6 = (bf16[256,768]{1,0:T(8,128)(2,1)}, bf16[256,768]{1,0:T(8,128)(2,1)}, u32[]{:S(2)}, u32[]{:S(2)}) collective-permute-start(bf16[256,768]{1,0:T(8,128)(2,1)} %get-tuple-element.45), channel_id=1, source_target_pairs={{0,12},{2,14},{4,8},{6,10},{8,4},{10,6},{12,0},{14,2},{1,13},{3,15... | collective-permute-start | bytes 1179656 | tf_op jit(solution)/shard_map/ppermute | solution.py:31
  83.5 4.4 %copy-start = (bf16[4,256,512]{2,1,0:T(8,128)(2,1)}, bf16[4,256,512]{2,1,0:T(8,128)(2,1)S(1)}, u32[]{:S(2)}) copy-start(bf16[4,256,512]{2,1,0:T(8,128)(2,1)S(1)} %all-to-all-done.2.refs_0_.refs_1_.refs_2_.refs_3_) | copy-start | bytes 3145732
  83.5 64.6 %all-to-all-start.1 = ((bf16[4,256,768]{2,1,0:T(8,128)(2,1)}), bf16[4,256,768]{2,1,0:T(8,128)(2,1)}, u32[]{:S(2)}, u32[]{:S(2)}) async-start(bf16[4,256,768]{2,1,0:T(8,128)(2,1)} %get-tuple-element.52), calls=%async_computation.1 | async-start | bytes 3145728 | tf_op jit(solution)/shard_map/all_to_all | solution.py:455
  90.3 46.2 %collective-permute-start.14 = (bf16[8,256,512]{2,1,0:T(8,128)(2,1)}, bf16[8,256,512]{2,1,0:T(8,128)(2,1)S(1)}, u32[]{:S(2)}, u32[]{:S(2)}) collective-permute-start(bf16[8,256,512]{2,1,0:T(8,128)(2,1)} %shard_map.67.refs_0_), channel_id=1, source_target_pairs={{0,1},{1,0},{2,3},{3,2},{4,5},{5,4},{6,7},{7,6},{8,9},{9,8},{10,11... | collective-permute-start | bytes 6291464 | tf_op jit(solution)/shard_map/ppermute | solution.py:31
  98.1 104.4 %collective-permute-start.1 = (bf16[256,768]{1,0:T(8,128)(2,1)}, bf16[256,768]{1,0:T(8,128)(2,1)}, u32[]{:S(2)}, u32[]{:S(2)}) collective-permute-start(bf16[256,768]{1,0:T(8,128)(2,1)} %get-tuple-element.38.refs_8_), channel_id=1, source_target_pairs={{0,8},{2,10},{4,12},{6,14},{8,0},{10,2},{12,4},{14,6},{1,9},{3,11}... | collective-permute-start | bytes 1179656 | tf_op jit(solution)/shard_map/ppermute | solution.py:31
  131.7 63.3 %collective-permute-start.10 = (bf16[256,768]{1,0:T(8,128)(2,1)}, bf16[256,768]{1,0:T(8,128)(2,1)}, u32[]{:S(2)}, u32[]{:S(2)}) collective-permute-start(bf16[256,768]{1,0:T(8,128)(2,1)} %get-tuple-element.51), channel_id=1, source_target_pairs={{0,14},{2,12},{4,10},{6,8},{8,6},{10,4},{12,2},{14,0},{1,15},{3,13... | collective-permute-start | bytes 1179656 | tf_op jit(solution)/shard_map/ppermute | solution.py:31
  133.8 61.1 %collective-permute-start.7 = (bf16[256,768]{1,0:T(8,128)(2,1)}, bf16[256,768]{1,0:T(8,128)(2,1)}, u32[]{:S(2)}, u32[]{:S(2)}) collective-permute-start(bf16[256,768]{1,0:T(8,128)(2,1)} %get-tuple-element.46), channel_id=1, source_target_pairs={{0,12},{2,14},{4,8},{6,10},{8,4},{10,6},{12,0},{14,2},{1,13},{3,15... | collective-permute-start | bytes 1179656 | tf_op jit(solution)/shard_map/ppermute | solution.py:31
  136.5 66.1 %collective-permute-start.4 = (bf16[256,768]{1,0:T(8,128)(2,1)}, bf16[256,768]{1,0:T(8,128)(2,1)}, u32[]{:S(2)}, u32[]{:S(2)}) collective-permute-start(bf16[256,768]{1,0:T(8,128)(2,1)} %get-tuple-element.41), channel_id=1, source_target_pairs={{0,10},{2,8},{4,14},{6,12},{8,2},{10,0},{12,6},{14,4},{1,11},{3,9}... | collective-permute-start | bytes 1179656 | tf_op jit(solution)/shard_map/ppermute | solution.py:31
  148.1 35.0 %all-to-all-start = ((bf16[4,256,768]{2,1,0:T(8,128)(2,1)}), bf16[4,256,768]{2,1,0:T(8,128)(2,1)S(1)}, u32[]{:S(2)}, u32[]{:S(2)}) async-start(bf16[4,256,768]{2,1,0:T(8,128)(2,1)} %get-tuple-element.36), calls=%async_computation | async-start | bytes 3145728 | tf_op jit(solution)/shard_map/all_to_all | solution.py:455
  154.7 28.4 %collective-permute-start.15 = (bf16[8,256,768]{2,1,0:T(8,128)(2,1)}, bf16[8,256,768]{2,1,0:T(8,128)(2,1)}, u32[]{:S(2)}, u32[]{:S(2)}) collective-permute-start(bf16[8,256,768]{2,1,0:T(8,128)(2,1)} %shard_map.70.refs_0_), channel_id=1, source_target_pairs={{0,1},{1,0},{2,3},{3,2},{4,5},{5,4},{6,7},{7,6},{8,9},{9,8},{10,11... | collective-permute-start | bytes 9437192 | tf_op jit(solution)/shard_map/ppermute | solution.py:31
  183.1 11.8 %copy-start.1 = (bf16[4,256,768]{2,1,0:T(8,128)(2,1)}, bf16[4,256,768]{2,1,0:T(8,128)(2,1)S(1)}, u32[]{:S(2)}) copy-start(bf16[4,256,768]{2,1,0:T(8,128)(2,1)S(1)} %all-to-all-done.refs_0_) | copy-start | bytes 4718596
  183.1 20.5 %collective-permute-start.11 = (bf16[4,256,768]{2,1,0:T(8,128)(2,1)S(1)}, bf16[4,256,768]{2,1,0:T(8,128)(2,1)S(1)}, u32[]{:S(2)}, u32[]{:S(2)}) collective-permute-start(bf16[4,256,768]{2,1,0:T(8,128)(2,1)S(1)} %all-to-all-done.refs_0_), channel_id=1, source_target_pairs={{0,1},{1,0},{2,3},{3,2},{4,5},{5,4},{6,7},{7,6},{8,9},{9,8},{10,11... | collective-permute-start | bytes 4718600 | tf_op jit(solution)/shard_map/ppermute | solution.py:31
  202.5 1.9 collective-permute-start.16
  202.5 3.1 %collective-permute-start.17 = (bf16[256,768]{1,0:T(8,128)(2,1)}, bf16[256,768]{1,0:T(8,128)(2,1)S(1)}, u32[]{:S(2)}, u32[]{:S(2)}) collective-permute-start(bf16[256,768]{1,0:T(8,128)(2,1)} %collective-permute-done.4.refs_2_), channel_id=1, source_target_pairs={{0,1},{1,0},{2,3},{3,2},{4,5},{5,4},{6,7},{7,6},{8,9},{9,8},{10,11... | collective-permute-start | bytes 1179656 | tf_op jit(solution)/shard_map/ppermute | solution.py:31
  203.1 2.7 %collective-permute-start.18 = (bf16[256,768]{1,0:T(8,128)(2,1)}, bf16[256,768]{1,0:T(8,128)(2,1)}, u32[]{:S(2)}, u32[]{:S(2)}) collective-permute-start(bf16[256,768]{1,0:T(8,128)(2,1)} %collective-permute-done.7.refs_3_), channel_id=1, source_target_pairs={{0,1},{1,0},{2,3},{3,2},{4,5},{5,4},{6,7},{7,6},{8,9},{9,8},{10,11... | collective-permute-start | bytes 1179656 | tf_op jit(solution)/shard_map/ppermute | solution.py:31
  203.1 3.2 %collective-permute-start.19 = (bf16[256,768]{1,0:T(8,128)(2,1)}, bf16[256,768]{1,0:T(8,128)(2,1)}, u32[]{:S(2)}, u32[]{:S(2)}) collective-permute-start(bf16[256,768]{1,0:T(8,128)(2,1)} %collective-permute-done.10.refs_4_), channel_id=1, source_target_pairs={{0,1},{1,0},{2,3},{3,2},{4,5},{5,4},{6,7},{7,6},{8,9},{9,8},{10,11... | collective-permute-start | bytes 1179656 | tf_op jit(solution)/shard_map/ppermute | solution.py:31
  (4 other events, 6.6 us)

commit v3 on v2

--- a/solution.py
+++ b/solution.py
@@ -62,6 +62,8 @@
     rim_made = refs.pop(0) if with_rim else None
     in_sems, table_sems, out_sems = refs[:3]
     steps = BLOCK // ROWS
+    turns = left.shape[0]
+    each, share = steps // turns, BLOCK // turns
     me = lax.axis_index("chan")
 
     def copies_in(step):
@@ -92,7 +94,7 @@
     for j in used:
         copy_table(j).start()
 
-    def filter_rows(step, carry):
+    def filter_rows(turn, step, carry):
         for copy in copies_in(step):
             copy.wait()
         rows = pl.ds(pl.multiple_of(step * ROWS, ROWS), ROWS)
@@ -111,30 +113,31 @@
                     total = weights[0] * values[f]
                     for t in range(1, tap_count):
                         total = total + weights[t] * values[f + t]
-                    at = pl.ds(pl.multiple_of(f * BLOCK + step * ROWS, ROWS), ROWS)
-                    left[part, at, lanes] = total.astype(jnp.bfloat16)
+                    at = pl.ds(pl.multiple_of(f * share + (step - turn * each) * ROWS, ROWS), ROWS)
+                    left[turn, part, at, lanes] = total.astype(jnp.bfloat16)
                 if with_rim:
                     for t in range(reach):
                         lanes = slice(t * fft_size + start, t * fft_size + start + LANES)
                         rim_made[part, rows, lanes] = values[count + t].astype(jnp.bfloat16)
         return carry
 
-    lax.fori_loop(0, steps, filter_rows, 0)
-    if with_rim:
-        rim_copy = pltpu.make_async_copy(rim_made, rim_out, in_sems.at[1, 0])
-        rim_copy.start()
-
-    def transform(j, frames):
-        pltpu.make_async_copy(table.at[0], tables.at[j], table_sems.at[j]).wait()
-        rows = frames * BLOCK
+
+    def transform(j, frames, turn):
+        if turn == 0:
+            pltpu.make_async_copy(table.at[0], tables.at[j], table_sems.at[j]).wait()
+
+        rows = frames * share
         product = [
-            jnp.dot(left[part, :rows, :], tables[j], preferred_element_type=jnp.float32) for part in range(2)
+            jnp.dot(left[turn, part, :rows, :], tables[j], preferred_element_type=jnp.float32) for part in range(2)
         ]
         real = (product[0][:, :LANES] + product[1][:, LANES:]).astype(jnp.bfloat16)
         imag = (product[1][:, :LANES] - product[0][:, LANES:]).astype(jnp.bfloat16)
+        at = slice(turn * share, (turn + 1) * share)
         for f in range(frames):
-            results[j, :, f * BLOCK : f * BLOCK + LANES] = real[f * BLOCK : (f + 1) * BLOCK]
-            results[j, :, f * BLOCK + LANES : (f + 1) * BLOCK] = imag[f * BLOCK : (f + 1) * BLOCK]
+            results[j, at, f * BLOCK : f * BLOCK + LANES] = real[f * share : (f + 1) * share]
+            results[j, at, f * BLOCK + LANES : (f + 1) * BLOCK] = imag[f * share : (f + 1) * share]
+        if turn + 1 < turns:
+            return
         for k in used:
 
             @pl.when(j == k)
@@ -142,18 +145,23 @@
                 for copy in copies_out(k):
                     copy.start()
 
-    begin = 0
-    while begin < len(used):
-        end = begin
-        while end < len(used) and sum(sends[end]) == sum(sends[begin]):
-            end += 1
-
-        def several(j, carry, frames=sum(sends[begin])):
-            transform(j, frames)
-            return carry
-
-        lax.fori_loop(begin, end, several, 0, unroll=2)
-        begin = end
+    for turn in range(turns):
+        lax.fori_loop(turn * each, (turn + 1) * each, functools.partial(filter_rows, turn), 0)
+        if with_rim and turn + 1 == turns:
+            rim_copy = pltpu.make_async_copy(rim_made, rim_out, in_sems.at[1, 0])
+            rim_copy.start()
+        begin = used[0]
+        while begin <= used[-1]:
+            end = begin
+            while end <= used[-1] and sum(sends[end]) == sum(sends[begin]):
+                end += 1
+
+            def several(j, carry, frames=sum(sends[begin]), turn=turn):
+                transform(j, frames, turn)
+                return carry
+
+            lax.fori_loop(begin, end, several, 0, unroll=2)
+            begin = end
     if with_rim:
         rim_copy.wait()
     for j in used:
@@ -168,6 +176,7 @@
     groups, depth, columns = len(sends), table.shape[1], table.shape[2]
     early = max(0, reach - first)
     own = count + reach - early
+    turns = 1
     anywhere = pl.BlockSpec(memory_space=pl.ANY)
     vmem = pl.BlockSpec(memory_space=pltpu.VMEM)
     operands = [samples] + ([rim] if early else []) + [taps, table] + ([] if gate is None else [gate])
@@ -183,7 +192,7 @@
         scratch.append(pltpu.VMEM((2, BLOCK, early * fft_size), jnp.bfloat16))
     scratch += [
         pltpu.VMEM((groups, depth, columns), jnp.bfloat16),
-        pltpu.VMEM((2, count * BLOCK, depth), jnp.bfloat16),
+        pltpu.VMEM((turns, 2, count * BLOCK // turns, depth), jnp.bfloat16),
         pltpu.VMEM((groups, BLOCK, count * columns), jnp.bfloat16),
     ]
     if with_rim:
@@ -267,14 +276,16 @@
     refs = refs[inputs + has_sums :]
     out, held, totals = refs[0], refs[1 : 1 + count], refs[1 + count]
     finished = refs[2 + count]
+    partial = refs[3 + count] if count == 2 else None
     block_sems, sum_sems, out_sems = refs[-3:]
     slots = totals.shape[0]
-    block_copies = []
+    copies = []
     for k, places in enumerate(layout):
+        copies.append([])
         for d, (number, at) in enumerate(places):
             source = arrays[number] if at is None else arrays[number].at[at]
-            block_copies.append(pltpu.make_async_copy(source, held[k].at[d], block_sems.at[k, d]))
-    for copy in block_copies:
+            copies[k].append(pltpu.make_async_copy(source, held[k].at[d], block_sems.at[k, d]))
+    for copy in copies[0]:
         copy.start()
 
     def copy_in(slot):
@@ -283,26 +294,39 @@
     def copy_out(slot):
         return pltpu.make_async_copy(finished.at[slot], out.at[slot], out_sems.at[slot])
 
-    if has_sums:
+    stage = -(-slots // 3)
+    stages = [range(start, min(start + stage, slots)) for start in range(0, slots, stage)]
+    if has_sums and count == 1:
+        for slot in stages[0]:
+            copy_in(slot).start()
+    for copy in copies[0]:
+        copy.wait()
+
+    def term_of(block, slot):
+        left, right = block[first[slot]], block[second[slot]]
+        turned = []
+        for start in range(0, left.shape[1], 2 * LANES):
+            turned += [left[:, start + LANES : start + 2 * LANES], -left[:, start : start + LANES]]
+        both = jnp.concatenate([left, jnp.concatenate(turned, axis=1)], axis=0)
+        return lax.dot_general(both, right, (((1,), (1,)), ((), ())), preferred_element_type=jnp.float32)
+
+    def begin(slot, carry):
+        partial[slot] = term_of(held[0], slot)
+        return carry
+
+    if count == 2:
+        for copy in copies[1]:
+            copy.start()
         for slot in range(slots):
             copy_in(slot).start()
-    for copy in block_copies:
-        copy.wait()
-    if has_sums:
-        for slot in range(slots):
-            copy_in(slot).wait()
+        lax.fori_loop(0, slots, begin, 0, unroll=6)
+        for copy in copies[1]:
+            copy.wait()
 
     def correlate(slot, carry):
-        a, b = first[slot], second[slot]
-        total = None
-        for block in held:
-            left, right = block[a], block[b]
-            turned = []
-            for start in range(0, left.shape[1], 2 * LANES):
-                turned += [left[:, start + LANES : start + 2 * LANES], -left[:, start : start + LANES]]
-            both = jnp.concatenate([left, jnp.concatenate(turned, axis=1)], axis=0)
-            term = lax.dot_general(both, right, (((1,), (1,)), ((), ())), preferred_element_type=jnp.float32)
-            total = term if total is None else total + term
+        total = term_of(held[-1], slot)
+        if count == 2:
+            total = total + partial[slot]
         if has_sums:
             total = total + totals[slot]
         if factor is not None:
@@ -311,7 +335,13 @@
         copy_out(slot).start()
         return carry
 
-    lax.fori_loop(0, slots, correlate, 0, unroll=UNROLL)
+    for number, several in enumerate(stages):
+        if has_sums:
+            for slot in several:
+                copy_in(slot).wait()
+            for slot in stages[number + 1] if number + 1 < len(stages) and count == 1 else ():
+                copy_in(slot).start()
+        lax.fori_loop(several.start, several.stop, correlate, 0, unroll=UNROLL if factor is None else 6)
     for slot in range(slots):
         copy_out(slot).wait()
 
@@ -335,6 +365,7 @@
     shape = (slots, 2 * BLOCK, BLOCK)
     kind = jnp.float32 if factor is None else jnp.bfloat16
     scratch = [pltpu.VMEM((len(places),) + operands[places[0][0]].shape[-2:], jnp.bfloat16) for places in layout] + [pltpu.VMEM(shape, jnp.float32), pltpu.VMEM(shape, kind)]
+    scratch += [pltpu.VMEM(shape, jnp.float32)] if len(blocks) == 2 else []
     scratch += [
         pltpu.SemaphoreType.DMA((len(layout), len(layout[0]))),
         pltpu.SemaphoreType.DMA((slots,)),
@@ -461,15 +492,17 @@
     made_a, (rim_here,) = front(samples, None, taps, table, None, start_a, FIRST, ((FIRST,),) * far + ((),) * far, True)
     a = {mask: to(mask, made_a[mask - far][0]) for mask in apart}
     rim = passed_along(rim_here, "pair", 1)
-    sends = ((SECOND,),) * far + ((SECOND, FIRST),) * far
-    made_b, (near_b, near_a) = front(samples, rim, taps, table, made_a[0][0], start_b, SECOND + FIRST, sends, False)
+    sends = ((SECOND,),) * far + ((),) * far
+    made_b, _ = front(samples, rim, taps, table, made_a[0][0], start_b, SECOND, sends, False)
+    sends = ((),) * far + ((SECOND, FIRST),) * far
+    _, (near_b, near_a) = front(samples, rim, taps, table, made_b[0][0], start_b, SECOND + FIRST, sends, False)
     b = {}
     for mask, gate in zip(apart, [a[far], a[far + 1], a[far + 2], a[far + 3]]):
         b[mask] = to(mask, after(made_b[mask - far][0], gate))
     aa = among_near(near_a)
     bb = among_near(near_b)
     sends = ((THIRD,),) * far + ((THIRD,),) * far
-    made_c, (near_c,) = front(samples, rim, taps, table, made_b[0][0], 0, THIRD, sends, False)
+    made_c, (near_c,) = front(samples, rim, taps, table, near_b, 0, THIRD, sends, False)
     mine = gathered([[(aa, k, 0, FIRST)] for k in range(far)] + [[(a[mask], None, 0, FIRST)] for mask in apart], made_c[0][0])
     other = other_core(mine)
     sums = tiles(first, second, [mine], None, None)

time: 223 us -> 219 us (0.982)
  waiting for transfers between devices: 43.5 us -> 36.7 us
  Pallas kernels: 105 us -> 109 us
    ppermute x19, waiting for transfers between devices: 27 us -> 21.2 us  [swapped_with(): lax.ppermute(block, axis, [(i, i ^ mask) for i in range(lax.axis_size(axi...]
    pallas_call x3 -> x4, Pallas kernels: 42.8 us -> 48.4 us  [front(): pl.pallas_call(functools.partial(front_kernel, geometry), in_specs=in_spe...]
    pallas_call x5, Pallas kernels: 57.5 us -> 55.2 us  [tiles(): pl.pallas_call(functools.partial(tile_kernel, (tuple(layout), inputs, sum...]
  transfers between devices with their start and end apart: 23 -> 23, of which waited for: 9 -> 9; matrix products, arithmetic and copies ran while one was open for 0% -> 0% of each run, Pallas kernels for 36% -> 40%
where the time goes in v3:
time: 219 us; the launch traced here: 218 us
  Pallas kernels  109 us (50%)
  starting transfers between devices  69.8 us (32%)
  waiting for transfers between devices  36.7 us (17%)
    pallas_call x5, Pallas kernels, tiles(): pl.pallas_call(functools.partial(tile_kernel, (tuple(layout), inputs, sum...  55.2 us
    ppermute x19, starting transfers between devices, swapped_with(): lax.ppermute(block, axis, [(i, i ^ mask) for i in range(lax.axis_size(axi...  54.8 us
    pallas_call x4, Pallas kernels, front(): pl.pallas_call(functools.partial(front_kernel, geometry), in_specs=in_spe...  48.4 us
    ppermute x19, waiting for transfers between devices, swapped_with(): lax.ppermute(block, axis, [(i, i ^ mask) for i in range(lax.axis_size(axi...  21.2 us
    all_to_all x3, waiting for transfers between devices, among_near(): lax.all_to_all(value, 'chan', 0, 0, axis_index_groups=halves, tiled=True)  15.5 us
    all_to_all x3, starting transfers between devices, among_near(): lax.all_to_all(value, 'chan', 0, 0, axis_index_groups=halves, tiled=True)  12.1 us
    pallas_call x2, Pallas kernels, gathered(): pl.pallas_call(functools.partial(gather_kernel, tuple(layout)), in_specs=...  5.18 us
  transfers between devices with their start and end apart: 23, of which 9 were waited for; matrix products, arithmetic and copies ran while one was open for 0% of the time, Pallas kernels for 40%

profile of v3, /device:TPU:0, one launch (start us, length us, event | category | flops | bytes accessed | tf_op | source)
XLA Modules:
  0.0 217.9 jit_solution(8951463183570900963)
XLA Ops:
  0.0 8.9 %shard_map.64 = (bf16[256,512]{1,0:T(8,128)(2,1)}, bf16[256,512]{1,0:T(8,128)(2,1)}, bf16[256,512]{1,0:T(8,128)(2,1)}, bf16[256,512]{1,0:T(8,128)(2,1)}, bf16[2,256,3072]{2,1,0:T(8,128)(2,1)}) custom-call(s32[2,256,8192]{2,1,0:T(8,128)} %samples.7, s32[4,1024]{1,0:T(4,128)} %refs_1_.4, bf16[8,1024,256]{2,1,0:T(8,128)(2,1)} %constant.72.clone.refs_1_.refs_2_), custom_call_target="tpu_custom_call" | custom-call | flops 99999997952 | bytes 1 | tf_op jit(solution)/shard_map/pallas_call | solution.py:208
  8.9 5.1 %collective-permute-start.5 = (bf16[256,512]{1,0:T(8,128)(2,1)}, bf16[256,512]{1,0:T(8,128)(2,1)}, u32[]{:S(2)}, u32[]{:S(2)}) collective-permute-start(bf16[256,512]{1,0:T(8,128)(2,1)} %get-tuple-element.45), channel_id=1, source_target_pairs={{0,12},{2,14},{4,8},{6,10},{8,4},{10,6},{12,0},{14,2},{1,13},{3,15... | collective-permute-start | bytes 786440 | tf_op jit(solution)/shard_map/ppermute | solution.py:31
  14.0 1.2 collective-permute-start.8
  15.9 2.0 collective-permute-start.2
  17.9 2.9 %collective-permute-start = (bf16[2,256,3072]{2,1,0:T(8,128)(2,1)}, bf16[2,256,3072]{2,1,0:T(8,128)(2,1)}, u32[]{:S(2)}, u32[]{:S(2)}) collective-permute-start(bf16[2,256,3072]{2,1,0:T(8,128)(2,1)} %get-tuple-element.33), channel_id=1, source_target_pairs={{0,1},{2,3},{4,5},{6,7},{8,9},{10,11},{12,13},{14,15},{16,17},{18,... | collective-permute-start | bytes 9437192 | tf_op jit(solution)/shard_map/ppermute | solution.py:27
  20.8 10.6 %shard_map.65 = (bf16[256,768]{1,0:T(8,128)(2,1)}, bf16[256,768]{1,0:T(8,128)(2,1)}, bf16[256,768]{1,0:T(8,128)(2,1)}, bf16[256,768]{1,0:T(8,128)(2,1)}) custom-call(s32[2,256,8192]{2,1,0:T(8,128)} %samples.7, s32[4,1024]{1,0:T(4,128)} %refs_1_.4, bf16[8,1024,256]{2,1,0:T(8,128)(2,1)} %constant.72.clone.refs_1_.refs_2_, ...), custom_call_target="tpu_custom_call" | custom-call | flops 99999997952 | bytes 1 | tf_op jit(solution)/shard_map/pallas_call | solution.py:208
  31.4 14.4 %shard_map.66 = (bf16[4,256,768]{2,1,0:T(8,128)(2,1)}, bf16[4,256,512]{2,1,0:T(8,128)(2,1)}) custom-call(s32[2,256,8192]{2,1,0:T(8,128)} %samples.7, s32[4,1024]{1,0:T(4,128)} %refs_1_.4, bf16[8,1024,256]{2,1,0:T(8,128)(2,1)} %constant.72.clone.refs_1_.refs_2_, bf16[256,768]{1,0:T(8,128)(2,1)} %get-tuple-element.41.refs_2_), custom_call_target="tpu_custom_call" | custom-call | flops 99999997952 | bytes 1 | tf_op jit(solution)/shard_map/pallas_call | solution.py:208
  45.8 3.6 %all-to-all-start.2 = ((bf16[4,256,512]{2,1,0:T(8,128)(2,1)}), bf16[4,256,512]{2,1,0:T(8,128)(2,1)S(1)}, u32[]{:S(2)}, u32[]{:S(2)}) async-start(bf16[4,256,512]{2,1,0:T(8,128)(2,1)} %get-tuple-element.56), calls=%async_computation.2 | async-start | bytes 2097152 | tf_op jit(solution)/shard_map/all_to_all | solution.py:486
  50.3 5.3 %collective-permute-done.12.refs_5_ = bf16[256,512]{1,0:T(8,128)(2,1)} collective-permute-done((bf16[256,512]{1,0:T(8,128)(2,1)}, bf16[256,512]{1,0:T(8,128)(2,1)}, u32[]{:S(2)}, u32[]{:S(2)}) %collective-permute-start.12) | collective-permute-done | bytes 262176 | tf_op jit(solution)/shard_map/ppermute | solution.py:31
  55.5 3.7 %collective-permute-done.2.refs_4_ = bf16[256,512]{1,0:T(8,128)(2,1)} collective-permute-done((bf16[256,512]{1,0:T(8,128)(2,1)}, bf16[256,512]{1,0:T(8,128)(2,1)}, u32[]{:S(2)}, u32[]{:S(2)}) %collective-permute-start.2) | collective-permute-done | bytes 262176 | tf_op jit(solution)/shard_map/ppermute | solution.py:31
  59.2 3.9 %collective-permute-start.13 = (bf16[256,768]{1,0:T(8,128)(2,1)}, bf16[256,768]{1,0:T(8,128)(2,1)}, u32[]{:S(2)}, u32[]{:S(2)}) collective-permute-start(bf16[256,768]{1,0:T(8,128)(2,1)} %get-tuple-element.55), channel_id=1, source_target_pairs={{0,10},{2,8},{4,14},{6,12},{8,2},{10,0},{12,6},{14,4},{1,11},{3,9}... | collective-permute-start | bytes 1179656 | tf_op jit(solution)/shard_map/ppermute | solution.py:31
  63.1 2.4 %collective-permute-start.9 = (bf16[256,768]{1,0:T(8,128)(2,1)}, bf16[256,768]{1,0:T(8,128)(2,1)}, u32[]{:S(2)}, u32[]{:S(2)}) collective-permute-start(bf16[256,768]{1,0:T(8,128)(2,1)} %get-tuple-element.51), channel_id=1, source_target_pairs={{0,14},{2,12},{4,10},{6,8},{8,6},{10,4},{12,2},{14,0},{1,15},{3,13... | collective-permute-start | bytes 1179656 | tf_op jit(solution)/shard_map/ppermute | solution.py:31
  65.5 1.3 collective-permute-start.6
  66.9 14.6 %shard_map.67 = (bf16[256,768]{1,0:T(8,128)(2,1)}, bf16[256,768]{1,0:T(8,128)(2,1)}, bf16[256,768]{1,0:T(8,128)(2,1)}, bf16[256,768]{1,0:T(8,128)(2,1)}, bf16[4,256,768]{2,1,0:T(8,128)(2,1)}) custom-call(s32[2,256,8192]{2,1,0:T(8,128)} %samples.7, bf16[2,256,3072]{2,1,0:T(8,128)(2,1)} %collective-permute-done.refs_0_, s32[4,1024]{1,0:T(4,128)} %refs_1_.4, ...), custom_call_target="tpu_custom_call" | custom-call | flops 99999997952 | bytes 1 | tf_op jit(solution)/shard_map/pallas_call | solution.py:208
  81.5 4.5 %all-to-all-start.1 = ((bf16[4,256,768]{2,1,0:T(8,128)(2,1)}), bf16[4,256,768]{2,1,0:T(8,128)(2,1)}, u32[]{:S(2)}, u32[]{:S(2)}) async-start(bf16[4,256,768]{2,1,0:T(8,128)(2,1)} %get-tuple-element.36.refs_3_), calls=%async_computation.1 | async-start | bytes 3145728 | tf_op jit(solution)/shard_map/all_to_all | solution.py:486
  86.0 2.4 %shard_map.68.refs_0_ = bf16[8,256,512]{2,1,0:T(8,128)(2,1)} custom-call(bf16[4,256,512]{2,1,0:T(8,128)(2,1)} %copy-done, bf16[4,256,512]{2,1,0:T(8,128)(2,1)} %copy-done, bf16[4,256,512]{2,1,0:T(8,128)(2,1)} %copy-done, bf16[4,256,512]{2,1,0:T(8,128)(2,1)} %copy-done, bf16[256,512]{1,0:T(8,128)(2,1)} %collective-permute-done.2.refs_4_, ...), custom_call_target="tpu_custom_call" | custom-call | flops 1 | bytes 1 | tf_op jit(solution)/shard_map/pallas_call | solution.py:256
  88.5 7.4 %shard_map.69.refs_1_ = f32[18,512,256]{2,1,0:T(8,128)} custom-call(s32[18]{0:T(128)} %get-tuple-element.64.first, s32[18]{0:T(128)} %get-tuple-element.63.second, bf16[8,256,512]{2,1,0:T(8,128)(2,1)} %shard_map.68.refs_0_), custom_call_target="tpu_custom_call" | custom-call | flops 99999997952 | bytes 1 | tf_op jit(solution)/shard_map/pallas_call | solution.py:374
  95.9 1.7 collective-permute-done.6.refs_6_
  97.7 32.2 %collective-permute-start.1 = (bf16[256,768]{1,0:T(8,128)(2,1)}, bf16[256,768]{1,0:T(8,128)(2,1)}, u32[]{:S(2)}, u32[]{:S(2)}) collective-permute-start(bf16[256,768]{1,0:T(8,128)(2,1)} %get-tuple-element.39.refs_8_), channel_id=1, source_target_pairs={{0,8},{2,10},{4,12},{6,14},{8,0},{10,2},{12,4},{14,6},{1,9},{3,11}... | collective-permute-start | bytes 1179656 | tf_op jit(solution)/shard_map/ppermute | solution.py:31
  129.9 3.5 %collective-permute-start.10 = (bf16[256,768]{1,0:T(8,128)(2,1)}, bf16[256,768]{1,0:T(8,128)(2,1)}, u32[]{:S(2)}, u32[]{:S(2)}) collective-permute-start(bf16[256,768]{1,0:T(8,128)(2,1)} %get-tuple-element.52), channel_id=1, source_target_pairs={{0,14},{2,12},{4,10},{6,8},{8,6},{10,4},{12,2},{14,0},{1,15},{3,13... | collective-permute-start | bytes 1179656 | tf_op jit(solution)/shard_map/ppermute | solution.py:31
  133.3 1.3 collective-permute-start.7
  134.7 1.3 copy-done.4
  136.0 11.8 %shard_map.70.refs_8_.refs_1_ = f32[18,512,256]{2,1,0:T(8,128)} custom-call(s32[18]{0:T(128)} %get-tuple-element.64.first, s32[18]{0:T(128)} %get-tuple-element.63.second, bf16[8,256,512]{2,1,0:T(8,128)(2,1)} %copy-done.4, f32[18,512,256]{2,1,0:T(8,128)} %shard_map.69.refs_1_), custom_call_target="tpu_custom_call" | custom-call | flops 99999997952 | bytes 1 | tf_op jit(solution)/shard_map/pallas_call | solution.py:374
  147.8 3.9 %all-to-all-start = ((bf16[4,256,768]{2,1,0:T(8,128)(2,1)}), bf16[4,256,768]{2,1,0:T(8,128)(2,1)S(1)}, u32[]{:S(2)}, u32[]{:S(2)}) async-start(bf16[4,256,768]{2,1,0:T(8,128)(2,1)} %get-tuple-element.37), calls=%async_computation | async-start | bytes 3145728 | tf_op jit(solution)/shard_map/all_to_all | solution.py:486
  151.7 2.8 %shard_map.71.refs_0_ = bf16[8,256,768]{2,1,0:T(8,128)(2,1)} custom-call(bf16[4,256,768]{2,1,0:T(8,128)(2,1)} %all-to-all-done.1.refs_0_.refs_1_.refs_2_.refs_3_, bf16[4,256,768]{2,1,0:T(8,128)(2,1)} %all-to-all-done.1.refs_0_.refs_1_.refs_2_.refs_3_, bf16[4,256,768]{2,1,0:T(8,128)(2,1)} %all-to-all-done.1.refs_0_.refs_1_.refs_2_.refs_3_, ...), custom_call_target="tpu_custom_call" | custom-call | flops 1 | bytes 1 | tf_op jit(solution)/shard_map/pallas_call | solution.py:256
  154.6 11.7 %shard_map.72.refs_1_ = f32[18,512,256]{2,1,0:T(8,128)} custom-call(s32[18]{0:T(128)} %get-tuple-element.64.first, s32[18]{0:T(128)} %get-tuple-element.63.second, bf16[8,256,768]{2,1,0:T(8,128)(2,1)} %shard_map.71.refs_0_, f32[18,512,256]{2,1,0:T(8,128)} %shard_map.70.refs_8_.refs_1_), custom_call_target="tpu_custom_call" | custom-call | flops 99999997952 | bytes 1 | tf_op jit(solution)/shard_map/pallas_call | solution.py:374
  166.2 15.5 %all-to-all-done.refs_0_ = bf16[4,256,768]{2,1,0:T(8,128)(2,1)S(1)} async-done(((bf16[4,256,768]{2,1,0:T(8,128)(2,1)}), bf16[4,256,768]{2,1,0:T(8,128)(2,1)S(1)}, u32[]{:S(2)}, u32[]{:S(2)}) %all-to-all-start) | async-done | bytes 1572896 | tf_op jit(solution)/shard_map/all_to_all | solution.py:486
  181.8 11.7 %shard_map.73.refs_10_ = f32[18,512,256]{2,1,0:T(8,128)} custom-call(s32[18]{0:T(128)} %get-tuple-element.64.first, s32[18]{0:T(128)} %get-tuple-element.63.second, bf16[8,256,768]{2,1,0:T(8,128)(2,1)} %collective-permute-done.15.refs_0_, f32[18,512,256]{2,1,0:T(8,128)} %shard_map.72.refs_1_), custom_call_target="tpu_custom_call" | custom-call | flops 99999997952 | bytes 1 | tf_op jit(solution)/shard_map/pallas_call | solution.py:374
  193.6 7.7 %collective-permute-done.4.refs_2_ = bf16[256,768]{1,0:T(8,128)(2,1)} collective-permute-done((bf16[256,768]{1,0:T(8,128)(2,1)}, bf16[256,768]{1,0:T(8,128)(2,1)}, u32[]{:S(2)}, u32[]{:S(2)}) %collective-permute-start.4) | collective-permute-done | bytes 393248 | tf_op jit(solution)/shard_map/ppermute | solution.py:31
  202.3 0.9 collective-permute-done.16.refs_6_
  203.2 1.1 collective-permute-done.17.refs_7_
  205.1 12.6 %shard_map.74 = bf16[18,512,256]{2,1,0:T(8,128)(2,1)} custom-call(s32[18]{0:T(128)} %get-tuple-element.64.first, s32[18]{0:T(128)} %get-tuple-element.63.second, bf16[4,256,768]{2,1,0:T(8,128)(2,1)} %copy-done.1, bf16[256,768]{1,0:T(8,128)(2,1)} %collective-permute-done.1.refs_1_, bf16[256,768]{1,0:T(8,128)(2,1)} %collective-permute-done.4.refs_2_, ...), custom_call_target="tpu_custom_call" | custom-call | flops 99999997952 | bytes 1 | tf_op jit(solution)/shard_map/pallas_call | solution.py:374
  (46 shorter events, 3.5 us)
Async XLA Ops:
  8.9 41.4 %collective-permute-start.5 = (bf16[256,512]{1,0:T(8,128)(2,1)}, bf16[256,512]{1,0:T(8,128)(2,1)}, u32[]{:S(2)}, u32[]{:S(2)}) collective-permute-start(bf16[256,512]{1,0:T(8,128)(2,1)} %get-tuple-element.45), channel_id=1, source_target_pairs={{0,12},{2,14},{4,8},{6,10},{8,4},{10,6},{12,0},{14,2},{1,13},{3,15... | collective-permute-start | bytes 786440 | tf_op jit(solution)/shard_map/ppermute | solution.py:31
  14.0 36.3 %collective-permute-start.8 = (bf16[256,512]{1,0:T(8,128)(2,1)}, bf16[256,512]{1,0:T(8,128)(2,1)}, u32[]{:S(2)}, u32[]{:S(2)}) collective-permute-start(bf16[256,512]{1,0:T(8,128)(2,1)} %get-tuple-element.50), channel_id=1, source_target_pairs={{0,14},{2,12},{4,10},{6,8},{8,6},{10,4},{12,2},{14,0},{1,15},{3,13... | collective-permute-start | bytes 786440 | tf_op jit(solution)/shard_map/ppermute | solution.py:31
  15.2 40.4 %collective-permute-start.12 = (bf16[256,512]{1,0:T(8,128)(2,1)}, bf16[256,512]{1,0:T(8,128)(2,1)}, u32[]{:S(2)}, u32[]{:S(2)}) collective-permute-start(bf16[256,512]{1,0:T(8,128)(2,1)} %get-tuple-element.54), channel_id=1, source_target_pairs={{0,10},{2,8},{4,14},{6,12},{8,2},{10,0},{12,6},{14,4},{1,11},{3,9}... | collective-permute-start | bytes 786440 | tf_op jit(solution)/shard_map/ppermute | solution.py:31
  15.9 43.3 %collective-permute-start.2 = (bf16[256,512]{1,0:T(8,128)(2,1)}, bf16[256,512]{1,0:T(8,128)(2,1)}, u32[]{:S(2)}, u32[]{:S(2)}) collective-permute-start(bf16[256,512]{1,0:T(8,128)(2,1)} %get-tuple-element.34.refs_2_), channel_id=1, source_target_pairs={{0,8},{2,10},{4,12},{6,14},{8,0},{10,2},{12,4},{14,6},{1,9},{3,11}... | collective-permute-start | bytes 786440 | tf_op jit(solution)/shard_map/ppermute | solution.py:31
  17.9 49.0 %collective-permute-start = (bf16[2,256,3072]{2,1,0:T(8,128)(2,1)}, bf16[2,256,3072]{2,1,0:T(8,128)(2,1)}, u32[]{:S(2)}, u32[]{:S(2)}) collective-permute-start(bf16[2,256,3072]{2,1,0:T(8,128)(2,1)} %get-tuple-element.33), channel_id=1, source_target_pairs={{0,1},{2,3},{4,5},{6,7},{8,9},{10,11},{12,13},{14,15},{16,17},{18,... | collective-permute-start | bytes 9437192 | tf_op jit(solution)/shard_map/ppermute | solution.py:27
  31.4 18.1 %copy-start.8 = (s32[36]{0:T(128)S(1)}, s32[36]{0:T(128)}, u32[]{:S(2)}) copy-start(s32[36]{0:T(128)} %param.8) | copy-start | bytes 436
  31.4 18.1 %copy-start.2 = (s32[36]{0:T(128)S(1)}, s32[36]{0:T(128)}, u32[]{:S(2)}) copy-start(s32[36]{0:T(128)} %constant.74.clone) | copy-start | bytes 436
  31.4 18.1 %copy-start.3 = (s32[36]{0:T(128)S(1)}, s32[36]{0:T(128)}, u32[]{:S(2)}) copy-start(s32[36]{0:T(128)} %constant.73.clone) | copy-start | bytes 436
  45.8 35.7 %all-to-all-start.2 = ((bf16[4,256,512]{2,1,0:T(8,128)(2,1)}), bf16[4,256,512]{2,1,0:T(8,128)(2,1)S(1)}, u32[]{:S(2)}, u32[]{:S(2)}) async-start(bf16[4,256,512]{2,1,0:T(8,128)(2,1)} %get-tuple-element.56), calls=%async_computation.2 | async-start | bytes 2097152 | tf_op jit(solution)/shard_map/all_to_all | solution.py:486
  59.2 74.1 %collective-permute-start.3 = (bf16[256,768]{1,0:T(8,128)(2,1)}, bf16[256,768]{1,0:T(8,128)(2,1)}, u32[]{:S(2)}, u32[]{:S(2)}) collective-permute-start(bf16[256,768]{1,0:T(8,128)(2,1)} %get-tuple-element.41.refs_2_), channel_id=1, source_target_pairs={{0,8},{2,10},{4,12},{6,14},{8,0},{10,2},{12,4},{14,6},{1,9},{3,11}... | collective-permute-start | bytes 1179656 | tf_op jit(solution)/shard_map/ppermute | solution.py:31
  59.2 92.5 %collective-permute-start.13 = (bf16[256,768]{1,0:T(8,128)(2,1)}, bf16[256,768]{1,0:T(8,128)(2,1)}, u32[]{:S(2)}, u32[]{:S(2)}) collective-permute-start(bf16[256,768]{1,0:T(8,128)(2,1)} %get-tuple-element.55), channel_id=1, source_target_pairs={{0,10},{2,8},{4,14},{6,12},{8,2},{10,0},{12,6},{14,4},{1,11},{3,9}... | collective-permute-start | bytes 1179656 | tf_op jit(solution)/shard_map/ppermute | solution.py:31
  63.1 66.8 %collective-permute-start.9 = (bf16[256,768]{1,0:T(8,128)(2,1)}, bf16[256,768]{1,0:T(8,128)(2,1)}, u32[]{:S(2)}, u32[]{:S(2)}) collective-permute-start(bf16[256,768]{1,0:T(8,128)(2,1)} %get-tuple-element.51), channel_id=1, source_target_pairs={{0,14},{2,12},{4,10},{6,8},{8,6},{10,4},{12,2},{14,0},{1,15},{3,13... | collective-permute-start | bytes 1179656 | tf_op jit(solution)/shard_map/ppermute | solution.py:31
  65.5 32.2 %collective-permute-start.6 = (bf16[256,768]{1,0:T(8,128)(2,1)}, bf16[256,768]{1,0:T(8,128)(2,1)}, u32[]{:S(2)}, u32[]{:S(2)}) collective-permute-start(bf16[256,768]{1,0:T(8,128)(2,1)} %get-tuple-element.46), channel_id=1, source_target_pairs={{0,12},{2,14},{4,8},{6,10},{8,4},{10,6},{12,0},{14,2},{1,13},{3,15... | collective-permute-start | bytes 1179656 | tf_op jit(solution)/shard_map/ppermute | solution.py:31
  81.5 4.6 %copy-start = (bf16[4,256,512]{2,1,0:T(8,128)(2,1)}, bf16[4,256,512]{2,1,0:T(8,128)(2,1)S(1)}, u32[]{:S(2)}) copy-start(bf16[4,256,512]{2,1,0:T(8,128)(2,1)S(1)} %all-to-all-done.2.refs_0_.refs_1_.refs_2_.refs_3_) | copy-start | bytes 3145732
  81.5 66.3 %all-to-all-start.1 = ((bf16[4,256,768]{2,1,0:T(8,128)(2,1)}), bf16[4,256,768]{2,1,0:T(8,128)(2,1)}, u32[]{:S(2)}, u32[]{:S(2)}) async-start(bf16[4,256,768]{2,1,0:T(8,128)(2,1)} %get-tuple-element.36.refs_3_), calls=%async_computation.1 | async-start | bytes 3145728 | tf_op jit(solution)/shard_map/all_to_all | solution.py:486
  88.4 46.2 %collective-permute-start.14 = (bf16[8,256,512]{2,1,0:T(8,128)(2,1)}, bf16[8,256,512]{2,1,0:T(8,128)(2,1)S(1)}, u32[]{:S(2)}, u32[]{:S(2)}) collective-permute-start(bf16[8,256,512]{2,1,0:T(8,128)(2,1)} %shard_map.68.refs_0_), channel_id=1, source_target_pairs={{0,1},{1,0},{2,3},{3,2},{4,5},{5,4},{6,7},{7,6},{8,9},{9,8},{10,11... | collective-permute-start | bytes 6291464 | tf_op jit(solution)/shard_map/ppermute | solution.py:31
  97.7 103.6 %collective-permute-start.1 = (bf16[256,768]{1,0:T(8,128)(2,1)}, bf16[256,768]{1,0:T(8,128)(2,1)}, u32[]{:S(2)}, u32[]{:S(2)}) collective-permute-start(bf16[256,768]{1,0:T(8,128)(2,1)} %get-tuple-element.39.refs_8_), channel_id=1, source_target_pairs={{0,8},{2,10},{4,12},{6,14},{8,0},{10,2},{12,4},{14,6},{1,9},{3,11}... | collective-permute-start | bytes 1179656 | tf_op jit(solution)/shard_map/ppermute | solution.py:31
  129.9 63.7 %collective-permute-start.10 = (bf16[256,768]{1,0:T(8,128)(2,1)}, bf16[256,768]{1,0:T(8,128)(2,1)}, u32[]{:S(2)}, u32[]{:S(2)}) collective-permute-start(bf16[256,768]{1,0:T(8,128)(2,1)} %get-tuple-element.52), channel_id=1, source_target_pairs={{0,14},{2,12},{4,10},{6,8},{8,6},{10,4},{12,2},{14,0},{1,15},{3,13... | collective-permute-start | bytes 1179656 | tf_op jit(solution)/shard_map/ppermute | solution.py:31
  133.3 60.2 %collective-permute-start.7 = (bf16[256,768]{1,0:T(8,128)(2,1)}, bf16[256,768]{1,0:T(8,128)(2,1)}, u32[]{:S(2)}, u32[]{:S(2)}) collective-permute-start(bf16[256,768]{1,0:T(8,128)(2,1)} %get-tuple-element.47), channel_id=1, source_target_pairs={{0,12},{2,14},{4,8},{6,10},{8,4},{10,6},{12,0},{14,2},{1,13},{3,15... | collective-permute-start | bytes 1179656 | tf_op jit(solution)/shard_map/ppermute | solution.py:31
  134.7 1.3 copy-start.4
  134.7 66.6 %collective-permute-start.4 = (bf16[256,768]{1,0:T(8,128)(2,1)}, bf16[256,768]{1,0:T(8,128)(2,1)}, u32[]{:S(2)}, u32[]{:S(2)}) collective-permute-start(bf16[256,768]{1,0:T(8,128)(2,1)} %get-tuple-element.42), channel_id=1, source_target_pairs={{0,10},{2,8},{4,14},{6,12},{8,2},{10,0},{12,6},{14,4},{1,11},{3,9}... | collective-permute-start | bytes 1179656 | tf_op jit(solution)/shard_map/ppermute | solution.py:31
  147.8 34.0 %all-to-all-start = ((bf16[4,256,768]{2,1,0:T(8,128)(2,1)}), bf16[4,256,768]{2,1,0:T(8,128)(2,1)S(1)}, u32[]{:S(2)}, u32[]{:S(2)}) async-start(bf16[4,256,768]{2,1,0:T(8,128)(2,1)} %get-tuple-element.37), calls=%async_computation | async-start | bytes 3145728 | tf_op jit(solution)/shard_map/all_to_all | solution.py:486
  154.5 27.3 %collective-permute-start.15 = (bf16[8,256,768]{2,1,0:T(8,128)(2,1)}, bf16[8,256,768]{2,1,0:T(8,128)(2,1)}, u32[]{:S(2)}, u32[]{:S(2)}) collective-permute-start(bf16[8,256,768]{2,1,0:T(8,128)(2,1)} %shard_map.71.refs_0_), channel_id=1, source_target_pairs={{0,1},{1,0},{2,3},{3,2},{4,5},{5,4},{6,7},{7,6},{8,9},{9,8},{10,11... | collective-permute-start | bytes 9437192 | tf_op jit(solution)/shard_map/ppermute | solution.py:31
  181.8 11.7 %copy-start.1 = (bf16[4,256,768]{2,1,0:T(8,128)(2,1)}, bf16[4,256,768]{2,1,0:T(8,128)(2,1)S(1)}, u32[]{:S(2)}) copy-start(bf16[4,256,768]{2,1,0:T(8,128)(2,1)S(1)} %all-to-all-done.refs_0_) | copy-start | bytes 4718596
  181.8 20.5 %collective-permute-start.11 = (bf16[4,256,768]{2,1,0:T(8,128)(2,1)S(1)}, bf16[4,256,768]{2,1,0:T(8,128)(2,1)S(1)}, u32[]{:S(2)}, u32[]{:S(2)}) collective-permute-start(bf16[4,256,768]{2,1,0:T(8,128)(2,1)S(1)} %all-to-all-done.refs_0_), channel_id=1, source_target_pairs={{0,1},{1,0},{2,3},{3,2},{4,5},{5,4},{6,7},{7,6},{8,9},{9,8},{10,11... | collective-permute-start | bytes 4718600 | tf_op jit(solution)/shard_map/ppermute | solution.py:31
  201.3 1.9 collective-permute-start.16
  201.3 3.1 %collective-permute-start.17 = (bf16[256,768]{1,0:T(8,128)(2,1)}, bf16[256,768]{1,0:T(8,128)(2,1)S(1)}, u32[]{:S(2)}, u32[]{:S(2)}) collective-permute-start(bf16[256,768]{1,0:T(8,128)(2,1)} %collective-permute-done.4.refs_2_), channel_id=1, source_target_pairs={{0,1},{1,0},{2,3},{3,2},{4,5},{5,4},{6,7},{7,6},{8,9},{9,8},{10,11... | collective-permute-start | bytes 1179656 | tf_op jit(solution)/shard_map/ppermute | solution.py:31
  201.8 2.7 %collective-permute-start.18 = (bf16[256,768]{1,0:T(8,128)(2,1)}, bf16[256,768]{1,0:T(8,128)(2,1)}, u32[]{:S(2)}, u32[]{:S(2)}) collective-permute-start(bf16[256,768]{1,0:T(8,128)(2,1)} %collective-permute-done.7.refs_3_), channel_id=1, source_target_pairs={{0,1},{1,0},{2,3},{3,2},{4,5},{5,4},{6,7},{7,6},{8,9},{9,8},{10,11... | collective-permute-start | bytes 1179656 | tf_op jit(solution)/shard_map/ppermute | solution.py:31
  201.8 3.2 %collective-permute-start.19 = (bf16[256,768]{1,0:T(8,128)(2,1)}, bf16[256,768]{1,0:T(8,128)(2,1)}, u32[]{:S(2)}, u32[]{:S(2)}) collective-permute-start(bf16[256,768]{1,0:T(8,128)(2,1)} %collective-permute-done.10.refs_4_), channel_id=1, source_target_pairs={{0,1},{1,0},{2,3},{3,2},{4,5},{5,4},{6,7},{7,6},{8,9},{9,8},{10,11... | collective-permute-start | bytes 1179656 | tf_op jit(solution)/shard_map/ppermute | solution.py:31
  202.3 2.7 %copy-start.5 = (bf16[4,256,768]{2,1,0:T(8,128)(2,1)}, bf16[4,256,768]{2,1,0:T(8,128)(2,1)S(1)}, u32[]{:S(2)}) copy-start(bf16[4,256,768]{2,1,0:T(8,128)(2,1)S(1)} %collective-permute-done.11.refs_5_) | copy-start | bytes 4718596
  203.2 1.8 copy-start.6
  204.3 0.7 copy-start.7

commit v4 on v3

--- a/solution.py
+++ b/solution.py
@@ -16,9 +16,9 @@
 LANES = 128
 ROWS = 32
 SCALE = 2.0**-14
-VMEM_LIMIT = 60 * 1024 * 1024
-
-PLAN = (2, 3, 3)
+VMEM_LIMIT = 63 * 1024 * 1024
+
+PLAN = (1, 3, 4)
 
 
 def passed_along(block, axis, distance):
@@ -382,6 +382,40 @@
     )(first, second, *operands)
 
 
+def slots_kernel(groups, tile_order, gate, first, second):
+    me, core = lax.axis_index("chan"), lax.axis_index("pair")
+    slots, far = first.shape[0], groups // 2
+    starts = [a * groups - a * (a - 1) // 2 for a in range(groups)]
+    my_half = me >= far
+
+    def place(block):
+        return jnp.where((block >= far) == my_half, lax.rem(block, far), block ^ me)
+
+    def one(slot, carry):
+        tile = tile_order[core * slots + slot]
+        row, begin = jnp.int32(0), jnp.int32(0)
+        for a in range(1, groups):
+            row = row + jnp.where(tile >= starts[a], 1, 0)
+            begin = jnp.where(tile >= starts[a], starts[a], begin)
+        first[slot] = place(row)
+        second[slot] = place(tile - begin + row)
+        return carry
+
+    lax.fori_loop(0, slots, one, 0)
+
+
+def slot_places(tile_order, groups, slots, gate):
+    smem = pl.BlockSpec(memory_space=pltpu.SMEM)
+    places = jax.ShapeDtypeStruct((slots,), jnp.int32)
+    return pl.pallas_call(
+        functools.partial(slots_kernel, groups),
+        in_specs=[smem, pl.BlockSpec(memory_space=pl.ANY)],
+        out_specs=[smem, smem],
+        out_shape=[places, places],
+        cost_estimate=pl.CostEstimate(flops=COST, bytes_accessed=1, transcendentals=0),
+    )(tile_order, gate)
+
+
 def dft_table(length):
     index = jnp.arange(length, dtype=jnp.int32)
     phase = index[:, None] * index[None, :] % length
@@ -457,21 +491,10 @@
     fft_size = taps.shape[1]
     groups = lax.axis_size("chan")
     pair_size = lax.axis_size("pair")
-    me = lax.axis_index("chan").astype(jnp.int32)
     far = groups // 2
     table = jnp.asarray(grouped_table(fft_size, groups))
 
     slots = tile_order.shape[0] // pair_size
-    own_slots = lax.dynamic_slice(tile_order, (lax.axis_index("pair") * slots,), (slots,))
-    rows_np, cols_np = np.triu_indices(groups)
-    match = (own_slots[:, None] == jnp.arange(tile_order.shape[0], dtype=jnp.int32)[None, :]).astype(jnp.int32)
-
-    def place_of(blocks_np):
-        block = jnp.sum(match * jnp.asarray(blocks_np.astype(np.int32))[None, :], axis=1)
-        return jnp.where(block // far == me // far, block % far, block ^ me)
-
-    first, second = place_of(rows_np), place_of(cols_np)
-
     def after(value, *others):
         return lax.optimization_barrier((value, *others))[0]
 
@@ -494,31 +517,32 @@
     rim = passed_along(rim_here, "pair", 1)
     sends = ((SECOND,),) * far + ((),) * far
     made_b, _ = front(samples, rim, taps, table, made_a[0][0], start_b, SECOND, sends, False)
-    sends = ((),) * far + ((SECOND, FIRST),) * far
-    _, (near_b, near_a) = front(samples, rim, taps, table, made_b[0][0], start_b, SECOND + FIRST, sends, False)
     b = {}
     for mask, gate in zip(apart, [a[far], a[far + 1], a[far + 2], a[far + 3]]):
         b[mask] = to(mask, after(made_b[mask - far][0], gate))
+    sends = ((THIRD,),) * far + ((THIRD, SECOND, FIRST),) * far
+    made_c, (near_c, near_b, near_a) = front(samples, rim, taps, table, made_b[0][0], 0, end, sends, False)
     aa = among_near(near_a)
     bb = among_near(near_b)
-    sends = ((THIRD,),) * far + ((THIRD,),) * far
-    made_c, (near_c,) = front(samples, rim, taps, table, near_b, 0, THIRD, sends, False)
-    mine = gathered([[(aa, k, 0, FIRST)] for k in range(far)] + [[(a[mask], None, 0, FIRST)] for mask in apart], made_c[0][0])
+    first, second = slot_places(tile_order, groups, slots, made_c[0][0])
+    mine = gathered([[(aa, k, 0, FIRST)] for k in range(far)] + [[(a[mask], None, 0, FIRST)] for mask in apart], first)
     other = other_core(mine)
     sums = tiles(first, second, [mine], None, None)
+    half_sums = sums
     sums = tiles(first, second, [other], sums, None)
     c = {}
     for mask, gate in zip(apart, [rim, b[far], b[far + 2], b[far + 3]]):
-        c[mask] = to(mask, after(made_c[mask - far][0], gate))
+        c[mask] = to(mask, after(made_c[mask - far][0], gate, half_sums) if mask > far else after(made_c[mask - far][0], gate))
     cc = among_near(near_c)
     mine = gathered([[(bb, k, 0, SECOND)] for k in range(far)] + [[(b[mask], None, 0, SECOND)] for mask in apart], sums)
     other = other_core(mine)
     sums = tiles(first, second, [mine], sums, None)
     sums = tiles(first, second, [other], sums, None)
     last = [(cc, k) for k in range(far)] + [(c[mask], None) for mask in apart]
-    near_there = other_core(cc)
+    near_there = other_core(after(cc, sums))
     there = [(near_there, k) for k in range(far)] + [(other_core(after(c[mask], sums)), None) for mask in apart]
     factor = 1.0 / (end * pair_size * (fft_size // groups))
+    first, second = slot_places(tile_order, groups, slots, sums)
     sums = tiles(first, second, [last, there], sums, factor)
     return sums.reshape(1, slots, 2, BLOCK, BLOCK)
 

time: 219 us -> 218 us (level)
  the two profiles are of different devices: /device:TPU:0 before, /device:TPU:9 now
where the time goes in v4:
time: 218 us; the launch traced here: 217 us
  Pallas kernels  107 us (49%)
  waiting for transfers between devices  65.7 us (30%)
  starting transfers between devices  43.8 us (20%)
    pallas_call x5, Pallas kernels, tiles(): pl.pallas_call(functools.partial(tile_kernel, (tuple(layout), inputs, sum...  56.1 us
    ppermute x19, waiting for transfers between devices, swapped_with(): lax.ppermute(block, axis, [(i, i ^ mask) for i in range(lax.axis_size(axi...  53.3 us
    pallas_call x3, Pallas kernels, front(): pl.pallas_call(functools.partial(front_kernel, geometry), in_specs=in_spe...  42.6 us
    ppermute x19, starting transfers between devices, swapped_with(): lax.ppermute(block, axis, [(i, i ^ mask) for i in range(lax.axis_size(axi...  25.9 us
    all_to_all x3, starting transfers between devices, among_near(): lax.all_to_all(value, 'chan', 0, 0, axis_index_groups=halves, tiled=True)  16.6 us
    all_to_all x3, waiting for transfers between devices, among_near(): lax.all_to_all(value, 'chan', 0, 0, axis_index_groups=halves, tiled=True)  12.5 us
    pallas_call x2, Pallas kernels, gathered(): pl.pallas_call(functools.partial(gather_kernel, tuple(layout)), in_specs=...  4.9 us
  transfers between devices with their start and end apart: 23, of which 9 were waited for; matrix products, arithmetic and copies ran while one was open for 0% of the time, Pallas kernels for 39%

profile of v4, /device:TPU:9, one launch (start us, length us, event | category | flops | bytes accessed | tf_op | source)
XLA Modules:
  0.0 216.9 jit_solution(16159162198348508241)
XLA Ops:
  0.0 7.0 %shard_map.46 = (bf16[256,256]{1,0:T(8,128)(2,1)}, bf16[256,256]{1,0:T(8,128)(2,1)}, bf16[256,256]{1,0:T(8,128)(2,1)}, bf16[256,256]{1,0:T(8,128)(2,1)}, bf16[2,256,3072]{2,1,0:T(8,128)(2,1)}) custom-call(s32[2,256,8192]{2,1,0:T(8,128)} %samples.5, s32[4,1024]{1,0:T(4,128)} %refs_1_.3, bf16[8,1024,256]{2,1,0:T(8,128)(2,1)} %constant.2.clone.refs_1_.refs_2_), custom_call_target="tpu_custom_call" | custom-call | flops 99999997952 | bytes 1 | tf_op jit(solution)/shard_map/pallas_call | solution.py:208
  7.0 3.3 %collective-permute-start.3 = (bf16[256,256]{1,0:T(8,128)(2,1)}, bf16[256,256]{1,0:T(8,128)(2,1)S(1)}, u32[]{:S(2)}, u32[]{:S(2)}) collective-permute-start(bf16[256,256]{1,0:T(8,128)(2,1)} %get-tuple-element.47), channel_id=1, source_target_pairs={{0,10},{2,8},{4,14},{6,12},{8,2},{10,0},{12,6},{14,4},{1,11},{3,9}... | collective-permute-start | bytes 393224 | tf_op jit(solution)/shard_map/ppermute | solution.py:31
  10.4 1.4 collective-permute-start.7
  11.8 1.9 collective-permute-start.1
  15.0 10.6 %shard_map.47 = (bf16[256,768]{1,0:T(8,128)(2,1)}, bf16[256,768]{1,0:T(8,128)(2,1)}, bf16[256,768]{1,0:T(8,128)(2,1)}, bf16[256,768]{1,0:T(8,128)(2,1)}) custom-call(s32[2,256,8192]{2,1,0:T(8,128)} %samples.5, s32[4,1024]{1,0:T(4,128)} %refs_1_.3, bf16[8,1024,256]{2,1,0:T(8,128)(2,1)} %constant.2.clone.refs_1_.refs_2_, ...), custom_call_target="tpu_custom_call" | custom-call | flops 99999997952 | bytes 1 | tf_op jit(solution)/shard_map/pallas_call | solution.py:208
  25.6 2.2 %collective-permute-done.5.refs_6_ = bf16[256,256]{1,0:T(8,128)(2,1)S(1)} collective-permute-done((bf16[256,256]{1,0:T(8,128)(2,1)}, bf16[256,256]{1,0:T(8,128)(2,1)S(1)}, u32[]{:S(2)}, u32[]{:S(2)}) %collective-permute-start.5) | collective-permute-done | bytes 131104 | tf_op jit(solution)/shard_map/ppermute | solution.py:31
  27.8 2.8 %collective-permute-done.7.refs_7_ = bf16[256,256]{1,0:T(8,128)(2,1)S(1)} collective-permute-done((bf16[256,256]{1,0:T(8,128)(2,1)}, bf16[256,256]{1,0:T(8,128)(2,1)S(1)}, u32[]{:S(2)}, u32[]{:S(2)}) %collective-permute-start.7) | collective-permute-done | bytes 131104 | tf_op jit(solution)/shard_map/ppermute | solution.py:31
  30.6 2.8 %collective-permute-done.1.refs_4_ = bf16[256,256]{1,0:T(8,128)(2,1)S(1)} collective-permute-done((bf16[256,256]{1,0:T(8,128)(2,1)}, bf16[256,256]{1,0:T(8,128)(2,1)S(1)}, u32[]{:S(2)}, u32[]{:S(2)}) %collective-permute-start.1) | collective-permute-done | bytes 131104 | tf_op jit(solution)/shard_map/ppermute | solution.py:31
  33.4 3.0 %collective-permute-start.2 = (bf16[256,768]{1,0:T(8,128)(2,1)}, bf16[256,768]{1,0:T(8,128)(2,1)}, u32[]{:S(2)}, u32[]{:S(2)}) collective-permute-start(bf16[256,768]{1,0:T(8,128)(2,1)} %get-tuple-element.45.refs_3_), channel_id=1, source_target_pairs={{0,8},{2,10},{4,12},{6,14},{8,0},{10,2},{12,4},{14,6},{1,9},{3,11}... | collective-permute-start | bytes 1179656 | tf_op jit(solution)/shard_map/ppermute | solution.py:31
  37.8 2.8 %collective-permute-start.4 = (bf16[256,768]{1,0:T(8,128)(2,1)}, bf16[256,768]{1,0:T(8,128)(2,1)}, u32[]{:S(2)}, u32[]{:S(2)}) collective-permute-start(bf16[256,768]{1,0:T(8,128)(2,1)} %get-tuple-element.48), channel_id=1, source_target_pairs={{0,10},{2,8},{4,14},{6,12},{8,2},{10,0},{12,6},{14,4},{1,11},{3,9}... | collective-permute-start | bytes 1179656 | tf_op jit(solution)/shard_map/ppermute | solution.py:31
  40.6 25.0 %shard_map.48 = (bf16[256,1024]{1,0:T(8,128)(2,1)}, bf16[256,1024]{1,0:T(8,128)(2,1)}, bf16[256,1024]{1,0:T(8,128)(2,1)}, bf16[256,1024]{1,0:T(8,128)(2,1)}, bf1...) custom-call(s32[2,256,8192]{2,1,0:T(8,128)} %samples.5, ...), custom_call_target="tpu_custom_call" | custom-call | flops 99999997952 | bytes 1 | tf_op jit(solution)/shard_map/pallas_call | solution.py:208
  65.6 3.5 %all-to-all-start.1 = ((bf16[4,256,256]{2,1,0:T(8,128)(2,1)}), bf16[4,256,256]{2,1,0:T(8,128)(2,1)S(1)}, u32[]{:S(2)}, u32[]{:S(2)}) async-start(bf16[4,256,256]{2,1,0:T(8,128)(2,1)} %get-tuple-element.55), calls=%async_computation.1 | async-start | bytes 1048576 | tf_op jit(solution)/shard_map/all_to_all | solution.py:509
  69.1 1.7 shard_map.49
  70.8 10.3 %all-to-all-done.1.refs_0_.refs_1_.refs_2_.refs_3_ = bf16[4,256,256]{2,1,0:T(8,128)(2,1)S(1)} async-done(((bf16[4,256,256]{2,1,0:T(8,128)(2,1)}), bf16[4,256,256]{2,1,0:T(8,128)(2,1)S(1)}, u32[]{:S(2)}, u32[]{:S(2)}) %all-to-all-start.1) | async-done | bytes 524320 | tf_op jit(solution)/shard_map/all_to_all | solution.py:509
  81.1 6.4 %all-to-all-start = ((bf16[4,256,768]{2,1,0:T(8,128)(2,1)}), bf16[4,256,768]{2,1,0:T(8,128)(2,1)}, u32[]{:S(2)}, u32[]{:S(2)}) async-start(bf16[4,256,768]{2,1,0:T(8,128)(2,1)} %get-tuple-element.44), calls=%async_computation | async-start | bytes 3145728 | tf_op jit(solution)/shard_map/all_to_all | solution.py:509
  87.6 2.1 shard_map.50.refs_0_
  89.7 1.6 collective-permute-start.9
  91.3 6.2 %shard_map.51.refs_1_ = f32[18,512,256]{2,1,0:T(8,128)} custom-call(s32[18]{0:T(128)} %get-tuple-element.42.refs_8_.first, s32[18]{0:T(128)} %get-tuple-element.43.second, bf16[8,256,256]{2,1,0:T(8,128)(2,1)} %shard_map.50.refs_0_), custom_call_target="tpu_custom_call" | custom-call | flops 99999997952 | bytes 1 | tf_op jit(solution)/shard_map/pallas_call | solution.py:374
  98.3 2.6 %collective-permute-start.12 = (bf16[256,1024]{1,0:T(8,128)(2,1)}, bf16[256,1024]{1,0:T(8,128)(2,1)}, u32[]{:S(2)}, u32[]{:S(2)}) collective-permute-start(bf16[256,1024]{1,0:T(8,128)(2,1)} %get-tuple-element.61), channel_id=1, source_target_pairs={{0,10},{2,8},{4,14},{6,12},{8,2},{10,0},{12,6},{14,4},{1,11},{3,9}... | collective-permute-start | bytes 1572872 | tf_op jit(solution)/shard_map/ppermute | solution.py:31
  100.9 1.5 collective-permute-start.14
  102.3 11.2 %shard_map.52.refs_8_.refs_1_ = f32[18,512,256]{2,1,0:T(8,128)} custom-call(s32[18]{0:T(128)} %get-tuple-element.42.refs_8_.first, s32[18]{0:T(128)} %get-tuple-element.43.second, bf16[8,256,256]{2,1,0:T(8,128)(2,1)} %collective-permute-done.9.refs_0_, f32[18,512,256]{2,1,0:T(8,128)} %shard_map.51.refs_1_), custom_call_target="tpu_custom_call" | custom-call | flops 99999997952 | bytes 1 | tf_op jit(solution)/shard_map/pallas_call | solution.py:374
  113.5 2.2 all-to-all-done.refs_0_.refs_1_.refs_2_.refs_3_
  115.7 6.6 %all-to-all-start.2 = ((bf16[4,256,1024]{2,1,0:T(8,128)(2,1)}), bf16[4,256,1024]{2,1,0:T(8,128)(2,1)}, u32[]{:S(2)}, u32[]{:S(2)}) async-start(bf16[4,256,1024]{2,1,0:T(8,128)(2,1)} %get-tuple-element.58), calls=%async_computation.2 | async-start | bytes 4194304 | tf_op jit(solution)/shard_map/all_to_all | solution.py:509
  122.3 2.8 %shard_map.53.refs_0_ = bf16[8,256,768]{2,1,0:T(8,128)(2,1)} custom-call(bf16[4,256,768]{2,1,0:T(8,128)(2,1)} %all-to-all-done.refs_0_.refs_1_.refs_2_.refs_3_, bf16[4,256,768]{2,1,0:T(8,128)(2,1)} %all-to-all-done.refs_0_.refs_1_.refs_2_.refs_3_, bf16[4,256,768]{2,1,0:T(8,128)(2,1)} %all-to-all-done.refs_0_.refs_1_.refs_2_.refs_3_, ...), custom_call_target="tpu_custom_call" | custom-call | flops 1 | bytes 1 | tf_op jit(solution)/shard_map/pallas_call | solution.py:256
  125.1 2.5 %collective-permute-start.10 = (bf16[8,256,768]{2,1,0:T(8,128)(2,1)}, bf16[8,256,768]{2,1,0:T(8,128)(2,1)}, u32[]{:S(2)}, u32[]{:S(2)}) collective-permute-start(bf16[8,256,768]{2,1,0:T(8,128)(2,1)} %shard_map.53.refs_0_), channel_id=1, source_target_pairs={{0,1},{1,0},{2,3},{3,2},{4,5},{5,4},{6,7},{7,6},{8,9},{9,8},{10,11... | collective-permute-start | bytes 9437192 | tf_op jit(solution)/shard_map/ppermute | solution.py:31
  127.6 11.7 %shard_map.54.refs_1_ = f32[18,512,256]{2,1,0:T(8,128)} custom-call(s32[18]{0:T(128)} %get-tuple-element.42.refs_8_.first, s32[18]{0:T(128)} %get-tuple-element.43.second, bf16[8,256,768]{2,1,0:T(8,128)(2,1)} %shard_map.53.refs_0_, f32[18,512,256]{2,1,0:T(8,128)} %shard_map.52.refs_8_.refs_1_), custom_call_target="tpu_custom_call" | custom-call | flops 99999997952 | bytes 1 | tf_op jit(solution)/shard_map/pallas_call | solution.py:374
  139.3 11.7 %shard_map.55.gate.refs_10_ = f32[18,512,256]{2,1,0:T(8,128)} custom-call(s32[18]{0:T(128)} %get-tuple-element.42.refs_8_.first, s32[18]{0:T(128)} %get-tuple-element.43.second, bf16[8,256,768]{2,1,0:T(8,128)(2,1)} %collective-permute-done.10.refs_0_, f32[18,512,256]{2,1,0:T(8,128)} %shard_map.54.refs_1_), custom_call_target="tpu_custom_call" | custom-call | flops 99999997952 | bytes 1 | tf_op jit(solution)/shard_map/pallas_call | solution.py:374
  151.0 41.0 %collective-permute-done.14.refs_4_ = bf16[256,1024]{1,0:T(8,128)(2,1)} collective-permute-done((bf16[256,1024]{1,0:T(8,128)(2,1)}, bf16[256,1024]{1,0:T(8,128)(2,1)}, u32[]{:S(2)}, u32[]{:S(2)}) %collective-permute-start.14) | collective-permute-done | bytes 524320 | tf_op jit(solution)/shard_map/ppermute | solution.py:31
  192.1 2.2 %collective-permute-start.16 = (bf16[256,1024]{1,0:T(8,128)(2,1)}, bf16[256,1024]{1,0:T(8,128)(2,1)S(1)}, u32[]{:S(2)}, u32[]{:S(2)}) collective-permute-start(bf16[256,1024]{1,0:T(8,128)(2,1)} %collective-permute-done.11.refs_1_), channel_id=1, source_target_pairs={{0,1},{1,0},{2,3},{3,2},{4,5},{5,4},{6,7},{7,6},{8,9},{9,8},{10,11... | collective-permute-start | bytes 1572872 | tf_op jit(solution)/shard_map/ppermute | solution.py:31
  195.3 1.7 shard_map.56
  198.4 3.0 %collective-permute-done.15.refs_5_ = bf16[4,256,1024]{2,1,0:T(8,128)(2,1)} collective-permute-done((bf16[4,256,1024]{2,1,0:T(8,128)(2,1)}, bf16[4,256,1024]{2,1,0:T(8,128)(2,1)}, u32[]{:S(2)}, u32[]{:S(2)}) %collective-permute-start.15) | collective-permute-done | bytes 2097184 | tf_op jit(solution)/shard_map/ppermute | solution.py:31
  201.4 15.3 %shard_map.57 = bf16[18,512,256]{2,1,0:T(8,128)(2,1)} custom-call(s32[18]{0:T(128)} %get-tuple-element.56.first, s32[18]{0:T(128)} %get-tuple-element.57.second, bf16[4,256,1024]{2,1,0:T(8,128)(2,1)} %all-to-all-done.2.refs_0_, bf16[256,1024]{1,0:T(8,128)(2,1)} %collective-permute-done.11.refs_1_, bf16[256,1024]{1,0:T(8,128)(2,1)} %collective-permute-done.12.refs_2_, ...), custom_call_target="tpu_custom_call" | custom-call | flops 99999997952 | bytes 1 | tf_op jit(solution)/shard_map/pallas_call | solution.py:374
  (38 shorter events, 5.9 us)
Async XLA Ops:
  7.0 18.6 %collective-permute-start.3 = (bf16[256,256]{1,0:T(8,128)(2,1)}, bf16[256,256]{1,0:T(8,128)(2,1)S(1)}, u32[]{:S(2)}, u32[]{:S(2)}) collective-permute-start(bf16[256,256]{1,0:T(8,128)(2,1)} %get-tuple-element.47), channel_id=1, source_target_pairs={{0,10},{2,8},{4,14},{6,12},{8,2},{10,0},{12,6},{14,4},{1,11},{3,9}... | collective-permute-start | bytes 393224 | tf_op jit(solution)/shard_map/ppermute | solution.py:31
  10.3 17.5 %collective-permute-start.5 = (bf16[256,256]{1,0:T(8,128)(2,1)}, bf16[256,256]{1,0:T(8,128)(2,1)S(1)}, u32[]{:S(2)}, u32[]{:S(2)}) collective-permute-start(bf16[256,256]{1,0:T(8,128)(2,1)} %get-tuple-element.50), channel_id=1, source_target_pairs={{0,12},{2,14},{4,8},{6,10},{8,4},{10,6},{12,0},{14,2},{1,13},{3,15... | collective-permute-start | bytes 393224 | tf_op jit(solution)/shard_map/ppermute | solution.py:31
  10.4 20.3 %collective-permute-start.7 = (bf16[256,256]{1,0:T(8,128)(2,1)}, bf16[256,256]{1,0:T(8,128)(2,1)S(1)}, u32[]{:S(2)}, u32[]{:S(2)}) collective-permute-start(bf16[256,256]{1,0:T(8,128)(2,1)} %get-tuple-element.53), channel_id=1, source_target_pairs={{0,14},{2,12},{4,10},{6,8},{8,6},{10,4},{12,2},{14,0},{1,15},{3,13... | collective-permute-start | bytes 393224 | tf_op jit(solution)/shard_map/ppermute | solution.py:31
  11.8 21.7 %collective-permute-start.1 = (bf16[256,256]{1,0:T(8,128)(2,1)}, bf16[256,256]{1,0:T(8,128)(2,1)S(1)}, u32[]{:S(2)}, u32[]{:S(2)}) collective-permute-start(bf16[256,256]{1,0:T(8,128)(2,1)} %get-tuple-element.39.refs_2_), channel_id=1, source_target_pairs={{0,8},{2,10},{4,12},{6,14},{8,0},{10,2},{12,4},{14,6},{1,9},{3,11}... | collective-permute-start | bytes 393224 | tf_op jit(solution)/shard_map/ppermute | solution.py:31
  13.7 26.9 %collective-permute-start = (bf16[2,256,3072]{2,1,0:T(8,128)(2,1)}, bf16[2,256,3072]{2,1,0:T(8,128)(2,1)}, u32[]{:S(2)}, u32[]{:S(2)}) collective-permute-start(bf16[2,256,3072]{2,1,0:T(8,128)(2,1)} %get-tuple-element.38), channel_id=1, source_target_pairs={{0,1},{2,3},{4,5},{6,7},{8,9},{10,11},{12,13},{14,15},{16,17},{18,... | collective-permute-start | bytes 9437192 | tf_op jit(solution)/shard_map/ppermute | solution.py:27
  25.6 40.0 %copy-start.1 = (bf16[256,256]{1,0:T(8,128)(2,1)}, bf16[256,256]{1,0:T(8,128)(2,1)S(1)}, u32[]{:S(2)}) copy-start(bf16[256,256]{1,0:T(8,128)(2,1)S(1)} %collective-permute-done.3.refs_5_) | copy-start | bytes 393220
  27.8 37.8 %copy-start.2 = (bf16[256,256]{1,0:T(8,128)(2,1)}, bf16[256,256]{1,0:T(8,128)(2,1)S(1)}, u32[]{:S(2)}) copy-start(bf16[256,256]{1,0:T(8,128)(2,1)S(1)} %collective-permute-done.5.refs_6_) | copy-start | bytes 393220
  30.6 35.0 %copy-start.3 = (bf16[256,256]{1,0:T(8,128)(2,1)}, bf16[256,256]{1,0:T(8,128)(2,1)S(1)}, u32[]{:S(2)}) copy-start(bf16[256,256]{1,0:T(8,128)(2,1)S(1)} %collective-permute-done.7.refs_7_) | copy-start | bytes 393220
  33.4 32.2 %copy-start.4 = (bf16[256,256]{1,0:T(8,128)(2,1)}, bf16[256,256]{1,0:T(8,128)(2,1)S(1)}, u32[]{:S(2)}) copy-start(bf16[256,256]{1,0:T(8,128)(2,1)S(1)} %collective-permute-done.1.refs_4_) | copy-start | bytes 393220
  33.4 64.8 %collective-permute-start.2 = (bf16[256,768]{1,0:T(8,128)(2,1)}, bf16[256,768]{1,0:T(8,128)(2,1)}, u32[]{:S(2)}, u32[]{:S(2)}) collective-permute-start(bf16[256,768]{1,0:T(8,128)(2,1)} %get-tuple-element.45.refs_3_), channel_id=1, source_target_pairs={{0,8},{2,10},{4,12},{6,14},{8,0},{10,2},{12,4},{14,6},{1,9},{3,11}... | collective-permute-start | bytes 1179656 | tf_op jit(solution)/shard_map/ppermute | solution.py:31
  36.4 61.1 %collective-permute-start.8 = (bf16[256,768]{1,0:T(8,128)(2,1)}, bf16[256,768]{1,0:T(8,128)(2,1)}, u32[]{:S(2)}, u32[]{:S(2)}) collective-permute-start(bf16[256,768]{1,0:T(8,128)(2,1)} %get-tuple-element.54), channel_id=1, source_target_pairs={{0,14},{2,12},{4,10},{6,8},{8,6},{10,4},{12,2},{14,0},{1,15},{3,13... | collective-permute-start | bytes 1179656 | tf_op jit(solution)/shard_map/ppermute | solution.py:31
  36.4 61.8 %collective-permute-start.6 = (bf16[256,768]{1,0:T(8,128)(2,1)}, bf16[256,768]{1,0:T(8,128)(2,1)}, u32[]{:S(2)}, u32[]{:S(2)}) collective-permute-start(bf16[256,768]{1,0:T(8,128)(2,1)} %get-tuple-element.51), channel_id=1, source_target_pairs={{0,12},{2,14},{4,8},{6,10},{8,4},{10,6},{12,0},{14,2},{1,13},{3,15... | collective-permute-start | bytes 1179656 | tf_op jit(solution)/shard_map/ppermute | solution.py:31
  37.8 84.5 %collective-permute-start.4 = (bf16[256,768]{1,0:T(8,128)(2,1)}, bf16[256,768]{1,0:T(8,128)(2,1)}, u32[]{:S(2)}, u32[]{:S(2)}) collective-permute-start(bf16[256,768]{1,0:T(8,128)(2,1)} %get-tuple-element.48), channel_id=1, source_target_pairs={{0,10},{2,8},{4,14},{6,12},{8,2},{10,0},{12,6},{14,4},{1,11},{3,9}... | collective-permute-start | bytes 1179656 | tf_op jit(solution)/shard_map/ppermute | solution.py:31
  65.6 15.5 %all-to-all-start.1 = ((bf16[4,256,256]{2,1,0:T(8,128)(2,1)}), bf16[4,256,256]{2,1,0:T(8,128)(2,1)S(1)}, u32[]{:S(2)}, u32[]{:S(2)}) async-start(bf16[4,256,256]{2,1,0:T(8,128)(2,1)} %get-tuple-element.55), calls=%async_computation.1 | async-start | bytes 1048576 | tf_op jit(solution)/shard_map/all_to_all | solution.py:509
  81.1 6.4 %copy-start = (bf16[4,256,256]{2,1,0:T(8,128)(2,1)}, bf16[4,256,256]{2,1,0:T(8,128)(2,1)S(1)}, u32[]{:S(2)}) copy-start(bf16[4,256,256]{2,1,0:T(8,128)(2,1)S(1)} %all-to-all-done.1.refs_0_.refs_1_.refs_2_.refs_3_) | copy-start | bytes 1572868
  81.1 34.6 %all-to-all-start = ((bf16[4,256,768]{2,1,0:T(8,128)(2,1)}), bf16[4,256,768]{2,1,0:T(8,128)(2,1)}, u32[]{:S(2)}, u32[]{:S(2)}) async-start(bf16[4,256,768]{2,1,0:T(8,128)(2,1)} %get-tuple-element.44), calls=%async_computation | async-start | bytes 3145728 | tf_op jit(solution)/shard_map/all_to_all | solution.py:509
  89.7 11.2 %collective-permute-start.9 = (bf16[8,256,256]{2,1,0:T(8,128)(2,1)}, bf16[8,256,256]{2,1,0:T(8,128)(2,1)}, u32[]{:S(2)}, u32[]{:S(2)}) collective-permute-start(bf16[8,256,256]{2,1,0:T(8,128)(2,1)} %shard_map.50.refs_0_), channel_id=1, source_target_pairs={{0,1},{1,0},{2,3},{3,2},{4,5},{5,4},{6,7},{7,6},{8,9},{9,8},{10,11... | collective-permute-start | bytes 3145736 | tf_op jit(solution)/shard_map/ppermute | solution.py:31
  97.5 94.5 %collective-permute-start.11 = (bf16[256,1024]{1,0:T(8,128)(2,1)}, bf16[256,1024]{1,0:T(8,128)(2,1)}, u32[]{:S(2)}, u32[]{:S(2)}) collective-permute-start(bf16[256,1024]{1,0:T(8,128)(2,1)} %get-tuple-element.59.gate), channel_id=1, source_target_pairs={{0,8},{2,10},{4,12},{6,14},{8,0},{10,2},{12,4},{14,6},{1,9},{3,11}... | collective-permute-start | bytes 1572872 | tf_op jit(solution)/shard_map/ppermute | solution.py:31
  98.3 93.8 %collective-permute-start.12 = (bf16[256,1024]{1,0:T(8,128)(2,1)}, bf16[256,1024]{1,0:T(8,128)(2,1)}, u32[]{:S(2)}, u32[]{:S(2)}) collective-permute-start(bf16[256,1024]{1,0:T(8,128)(2,1)} %get-tuple-element.61), channel_id=1, source_target_pairs={{0,10},{2,8},{4,14},{6,12},{8,2},{10,0},{12,6},{14,4},{1,11},{3,9}... | collective-permute-start | bytes 1572872 | tf_op jit(solution)/shard_map/ppermute | solution.py:31
  100.9 91.2 %collective-permute-start.13 = (bf16[256,1024]{1,0:T(8,128)(2,1)}, bf16[256,1024]{1,0:T(8,128)(2,1)}, u32[]{:S(2)}, u32[]{:S(2)}) collective-permute-start(bf16[256,1024]{1,0:T(8,128)(2,1)} %get-tuple-element.63), channel_id=1, source_target_pairs={{0,12},{2,14},{4,8},{6,10},{8,4},{10,6},{12,0},{14,2},{1,13},{3,15... | collective-permute-start | bytes 1572872 | tf_op jit(solution)/shard_map/ppermute | solution.py:31
  100.9 91.2 %collective-permute-start.14 = (bf16[256,1024]{1,0:T(8,128)(2,1)}, bf16[256,1024]{1,0:T(8,128)(2,1)}, u32[]{:S(2)}, u32[]{:S(2)}) collective-permute-start(bf16[256,1024]{1,0:T(8,128)(2,1)} %get-tuple-element.65), channel_id=1, source_target_pairs={{0,14},{2,12},{4,10},{6,8},{8,6},{10,4},{12,2},{14,0},{1,15},{3,13... | collective-permute-start | bytes 1572872 | tf_op jit(solution)/shard_map/ppermute | solution.py:31
  115.7 76.4 %all-to-all-start.2 = ((bf16[4,256,1024]{2,1,0:T(8,128)(2,1)}), bf16[4,256,1024]{2,1,0:T(8,128)(2,1)}, u32[]{:S(2)}, u32[]{:S(2)}) async-start(bf16[4,256,1024]{2,1,0:T(8,128)(2,1)} %get-tuple-element.58), calls=%async_computation.2 | async-start | bytes 4194304 | tf_op jit(solution)/shard_map/all_to_all | solution.py:509
  125.1 14.2 %collective-permute-start.10 = (bf16[8,256,768]{2,1,0:T(8,128)(2,1)}, bf16[8,256,768]{2,1,0:T(8,128)(2,1)}, u32[]{:S(2)}, u32[]{:S(2)}) collective-permute-start(bf16[8,256,768]{2,1,0:T(8,128)(2,1)} %shard_map.53.refs_0_), channel_id=1, source_target_pairs={{0,1},{1,0},{2,3},{3,2},{4,5},{5,4},{6,7},{7,6},{8,9},{9,8},{10,11... | collective-permute-start | bytes 9437192 | tf_op jit(solution)/shard_map/ppermute | solution.py:31
  192.1 4.9 %collective-permute-start.16 = (bf16[256,1024]{1,0:T(8,128)(2,1)}, bf16[256,1024]{1,0:T(8,128)(2,1)S(1)}, u32[]{:S(2)}, u32[]{:S(2)}) collective-permute-start(bf16[256,1024]{1,0:T(8,128)(2,1)} %collective-permute-done.11.refs_1_), channel_id=1, source_target_pairs={{0,1},{1,0},{2,3},{3,2},{4,5},{5,4},{6,7},{7,6},{8,9},{9,8},{10,11... | collective-permute-start | bytes 1572872 | tf_op jit(solution)/shard_map/ppermute | solution.py:31
  194.3 2.7 %collective-permute-start.17 = (bf16[256,1024]{1,0:T(8,128)(2,1)}, bf16[256,1024]{1,0:T(8,128)(2,1)}, u32[]{:S(2)}, u32[]{:S(2)}) collective-permute-start(bf16[256,1024]{1,0:T(8,128)(2,1)} %collective-permute-done.12.refs_2_), channel_id=1, source_target_pairs={{0,1},{1,0},{2,3},{3,2},{4,5},{5,4},{6,7},{7,6},{8,9},{9,8},{10,11... | collective-permute-start | bytes 1572872 | tf_op jit(solution)/shard_map/ppermute | solution.py:31
  194.4 3.3 %collective-permute-start.18 = (bf16[256,1024]{1,0:T(8,128)(2,1)}, bf16[256,1024]{1,0:T(8,128)(2,1)}, u32[]{:S(2)}, u32[]{:S(2)}) collective-permute-start(bf16[256,1024]{1,0:T(8,128)(2,1)} %collective-permute-done.13.refs_3_), channel_id=1, source_target_pairs={{0,1},{1,0},{2,3},{3,2},{4,5},{5,4},{6,7},{7,6},{8,9},{9,8},{10,11... | collective-permute-start | bytes 1572872 | tf_op jit(solution)/shard_map/ppermute | solution.py:31
  194.8 3.6 %collective-permute-start.19 = (bf16[256,1024]{1,0:T(8,128)(2,1)}, bf16[256,1024]{1,0:T(8,128)(2,1)}, u32[]{:S(2)}, u32[]{:S(2)}) collective-permute-start(bf16[256,1024]{1,0:T(8,128)(2,1)} %collective-permute-done.14.refs_4_), channel_id=1, source_target_pairs={{0,1},{1,0},{2,3},{3,2},{4,5},{5,4},{6,7},{7,6},{8,9},{9,8},{10,11... | collective-permute-start | bytes 1572872 | tf_op jit(solution)/shard_map/ppermute | solution.py:31
  194.9 6.5 %collective-permute-start.15 = (bf16[4,256,1024]{2,1,0:T(8,128)(2,1)}, bf16[4,256,1024]{2,1,0:T(8,128)(2,1)}, u32[]{:S(2)}, u32[]{:S(2)}) collective-permute-start(bf16[4,256,1024]{2,1,0:T(8,128)(2,1)} %all-to-all-done.2.refs_0_), channel_id=1, source_target_pairs={{0,1},{1,0},{2,3},{3,2},{4,5},{5,4},{6,7},{7,6},{8,9},{9,8},{10,11... | collective-permute-start | bytes 6291464 | tf_op jit(solution)/shard_map/ppermute | solution.py:31
  197.0 4.4 %copy-start.5 = (bf16[256,1024]{1,0:T(8,128)(2,1)}, bf16[256,1024]{1,0:T(8,128)(2,1)S(1)}, u32[]{:S(2)}) copy-start(bf16[256,1024]{1,0:T(8,128)(2,1)S(1)} %collective-permute-done.16.refs_6_) | copy-start | bytes 1572868

commit v5 on v4

--- a/solution.py
+++ b/solution.py
@@ -294,7 +294,7 @@
     def copy_out(slot):
         return pltpu.make_async_copy(finished.at[slot], out.at[slot], out_sems.at[slot])
 
-    stage = -(-slots // 3)
+    stage = -(-slots // (2 if count == 2 else 3))
     stages = [range(start, min(start + stage, slots)) for start in range(0, slots, stage)]
     if has_sums and count == 1:
         for slot in stages[0]:
@@ -319,7 +319,7 @@
             copy.start()
         for slot in range(slots):
             copy_in(slot).start()
-        lax.fori_loop(0, slots, begin, 0, unroll=6)
+        lax.fori_loop(0, slots, begin, 0, unroll=9)
         for copy in copies[1]:
             copy.wait()
 
@@ -341,7 +341,7 @@
                 copy_in(slot).wait()
             for slot in stages[number + 1] if number + 1 < len(stages) and count == 1 else ():
                 copy_in(slot).start()
-        lax.fori_loop(several.start, several.stop, correlate, 0, unroll=UNROLL if factor is None else 6)
+        lax.fori_loop(several.start, several.stop, correlate, 0, unroll=UNROLL if factor is None else 9)
     for slot in range(slots):
         copy_out(slot).wait()
 

time: 218 us -> 218 us (level)
  no operation moved by 1% of the time
where the time goes in v5:
time: 218 us; the launch traced here: 217 us
  Pallas kernels  107 us (49%)
  waiting for transfers between devices  65.7 us (30%)
  starting transfers between devices  43.8 us (20%)
    pallas_call x5, Pallas kernels, tiles(): pl.pallas_call(functools.partial(tile_kernel, (tuple(layout), inputs, sum...  56 us
    ppermute x19, waiting for transfers between devices, swapped_with(): lax.ppermute(block, axis, [(i, i ^ mask) for i in range(lax.axis_size(axi...  53.3 us
    pallas_call x3, Pallas kernels, front(): pl.pallas_call(functools.partial(front_kernel, geometry), in_specs=in_spe...  42.6 us
    ppermute x19, starting transfers between devices, swapped_with(): lax.ppermute(block, axis, [(i, i ^ mask) for i in range(lax.axis_size(axi...  25.9 us
    all_to_all x3, starting transfers between devices, among_near(): lax.all_to_all(value, 'chan', 0, 0, axis_index_groups=halves, tiled=True)  16.6 us
    all_to_all x3, waiting for transfers between devices, among_near(): lax.all_to_all(value, 'chan', 0, 0, axis_index_groups=halves, tiled=True)  12.5 us
    pallas_call x2, Pallas kernels, gathered(): pl.pallas_call(functools.partial(gather_kernel, tuple(layout)), in_specs=...  4.9 us
  transfers between devices with their start and end apart: 23, of which 9 were waited for; matrix products, arithmetic and copies ran while one was open for 0% of the time, Pallas kernels for 39%

profile of v5, /device:TPU:9, one launch (start us, length us, event | category | flops | bytes accessed | tf_op | source)
XLA Modules:
  0.0 216.7 jit_solution(18146578750377356392)
XLA Ops:
  0.0 7.0 %shard_map.46 = (bf16[256,256]{1,0:T(8,128)(2,1)}, bf16[256,256]{1,0:T(8,128)(2,1)}, bf16[256,256]{1,0:T(8,128)(2,1)}, bf16[256,256]{1,0:T(8,128)(2,1)}, bf16[2,256,3072]{2,1,0:T(8,128)(2,1)}) custom-call(s32[2,256,8192]{2,1,0:T(8,128)} %samples.5, s32[4,1024]{1,0:T(4,128)} %refs_1_.3, bf16[8,1024,256]{2,1,0:T(8,128)(2,1)} %constant.2.clone.refs_1_.refs_2_), custom_call_target="tpu_custom_call" | custom-call | flops 99999997952 | bytes 1 | tf_op jit(solution)/shard_map/pallas_call | solution.py:208
  7.0 3.3 %collective-permute-start.3 = (bf16[256,256]{1,0:T(8,128)(2,1)}, bf16[256,256]{1,0:T(8,128)(2,1)S(1)}, u32[]{:S(2)}, u32[]{:S(2)}) collective-permute-start(bf16[256,256]{1,0:T(8,128)(2,1)} %get-tuple-element.47), channel_id=1, source_target_pairs={{0,10},{2,8},{4,14},{6,12},{8,2},{10,0},{12,6},{14,4},{1,11},{3,9}... | collective-permute-start | bytes 393224 | tf_op jit(solution)/shard_map/ppermute | solution.py:31
  10.4 1.4 collective-permute-start.7
  11.8 1.9 collective-permute-start.1
  15.0 10.6 %shard_map.47 = (bf16[256,768]{1,0:T(8,128)(2,1)}, bf16[256,768]{1,0:T(8,128)(2,1)}, bf16[256,768]{1,0:T(8,128)(2,1)}, bf16[256,768]{1,0:T(8,128)(2,1)}) custom-call(s32[2,256,8192]{2,1,0:T(8,128)} %samples.5, s32[4,1024]{1,0:T(4,128)} %refs_1_.3, bf16[8,1024,256]{2,1,0:T(8,128)(2,1)} %constant.2.clone.refs_1_.refs_2_, ...), custom_call_target="tpu_custom_call" | custom-call | flops 99999997952 | bytes 1 | tf_op jit(solution)/shard_map/pallas_call | solution.py:208
  25.6 2.2 %collective-permute-done.5.refs_6_ = bf16[256,256]{1,0:T(8,128)(2,1)S(1)} collective-permute-done((bf16[256,256]{1,0:T(8,128)(2,1)}, bf16[256,256]{1,0:T(8,128)(2,1)S(1)}, u32[]{:S(2)}, u32[]{:S(2)}) %collective-permute-start.5) | collective-permute-done | bytes 131104 | tf_op jit(solution)/shard_map/ppermute | solution.py:31
  27.8 2.8 %collective-permute-done.7.refs_7_ = bf16[256,256]{1,0:T(8,128)(2,1)S(1)} collective-permute-done((bf16[256,256]{1,0:T(8,128)(2,1)}, bf16[256,256]{1,0:T(8,128)(2,1)S(1)}, u32[]{:S(2)}, u32[]{:S(2)}) %collective-permute-start.7) | collective-permute-done | bytes 131104 | tf_op jit(solution)/shard_map/ppermute | solution.py:31
  30.6 2.8 %collective-permute-done.1.refs_4_ = bf16[256,256]{1,0:T(8,128)(2,1)S(1)} collective-permute-done((bf16[256,256]{1,0:T(8,128)(2,1)}, bf16[256,256]{1,0:T(8,128)(2,1)S(1)}, u32[]{:S(2)}, u32[]{:S(2)}) %collective-permute-start.1) | collective-permute-done | bytes 131104 | tf_op jit(solution)/shard_map/ppermute | solution.py:31
  33.4 3.0 %collective-permute-start.2 = (bf16[256,768]{1,0:T(8,128)(2,1)}, bf16[256,768]{1,0:T(8,128)(2,1)}, u32[]{:S(2)}, u32[]{:S(2)}) collective-permute-start(bf16[256,768]{1,0:T(8,128)(2,1)} %get-tuple-element.45.refs_3_), channel_id=1, source_target_pairs={{0,8},{2,10},{4,12},{6,14},{8,0},{10,2},{12,4},{14,6},{1,9},{3,11}... | collective-permute-start | bytes 1179656 | tf_op jit(solution)/shard_map/ppermute | solution.py:31
  37.8 2.8 %collective-permute-start.4 = (bf16[256,768]{1,0:T(8,128)(2,1)}, bf16[256,768]{1,0:T(8,128)(2,1)}, u32[]{:S(2)}, u32[]{:S(2)}) collective-permute-start(bf16[256,768]{1,0:T(8,128)(2,1)} %get-tuple-element.48), channel_id=1, source_target_pairs={{0,10},{2,8},{4,14},{6,12},{8,2},{10,0},{12,6},{14,4},{1,11},{3,9}... | collective-permute-start | bytes 1179656 | tf_op jit(solution)/shard_map/ppermute | solution.py:31
  40.6 25.0 %shard_map.48 = (bf16[256,1024]{1,0:T(8,128)(2,1)}, bf16[256,1024]{1,0:T(8,128)(2,1)}, bf16[256,1024]{1,0:T(8,128)(2,1)}, bf16[256,1024]{1,0:T(8,128)(2,1)}, bf1...) custom-call(s32[2,256,8192]{2,1,0:T(8,128)} %samples.5, ...), custom_call_target="tpu_custom_call" | custom-call | flops 99999997952 | bytes 1 | tf_op jit(solution)/shard_map/pallas_call | solution.py:208
  65.6 3.5 %all-to-all-start.1 = ((bf16[4,256,256]{2,1,0:T(8,128)(2,1)}), bf16[4,256,256]{2,1,0:T(8,128)(2,1)S(1)}, u32[]{:S(2)}, u32[]{:S(2)}) async-start(bf16[4,256,256]{2,1,0:T(8,128)(2,1)} %get-tuple-element.55), calls=%async_computation.1 | async-start | bytes 1048576 | tf_op jit(solution)/shard_map/all_to_all | solution.py:509
  69.1 1.7 shard_map.49
  70.8 10.3 %all-to-all-done.1.refs_0_.refs_1_.refs_2_.refs_3_ = bf16[4,256,256]{2,1,0:T(8,128)(2,1)S(1)} async-done(((bf16[4,256,256]{2,1,0:T(8,128)(2,1)}), bf16[4,256,256]{2,1,0:T(8,128)(2,1)S(1)}, u32[]{:S(2)}, u32[]{:S(2)}) %all-to-all-start.1) | async-done | bytes 524320 | tf_op jit(solution)/shard_map/all_to_all | solution.py:509
  81.1 6.4 %all-to-all-start = ((bf16[4,256,768]{2,1,0:T(8,128)(2,1)}), bf16[4,256,768]{2,1,0:T(8,128)(2,1)}, u32[]{:S(2)}, u32[]{:S(2)}) async-start(bf16[4,256,768]{2,1,0:T(8,128)(2,1)} %get-tuple-element.44), calls=%async_computation | async-start | bytes 3145728 | tf_op jit(solution)/shard_map/all_to_all | solution.py:509
  87.6 2.1 shard_map.50.refs_0_
  89.7 1.6 collective-permute-start.9
  91.3 6.2 %shard_map.51.refs_1_ = f32[18,512,256]{2,1,0:T(8,128)} custom-call(s32[18]{0:T(128)} %get-tuple-element.42.refs_8_.first, s32[18]{0:T(128)} %get-tuple-element.43.second, bf16[8,256,256]{2,1,0:T(8,128)(2,1)} %shard_map.50.refs_0_), custom_call_target="tpu_custom_call" | custom-call | flops 99999997952 | bytes 1 | tf_op jit(solution)/shard_map/pallas_call | solution.py:374
  98.3 2.6 %collective-permute-start.12 = (bf16[256,1024]{1,0:T(8,128)(2,1)}, bf16[256,1024]{1,0:T(8,128)(2,1)}, u32[]{:S(2)}, u32[]{:S(2)}) collective-permute-start(bf16[256,1024]{1,0:T(8,128)(2,1)} %get-tuple-element.61), channel_id=1, source_target_pairs={{0,10},{2,8},{4,14},{6,12},{8,2},{10,0},{12,6},{14,4},{1,11},{3,9}... | collective-permute-start | bytes 1572872 | tf_op jit(solution)/shard_map/ppermute | solution.py:31
  100.9 1.5 collective-permute-start.14
  102.3 11.2 %shard_map.52.refs_8_.refs_1_ = f32[18,512,256]{2,1,0:T(8,128)} custom-call(s32[18]{0:T(128)} %get-tuple-element.42.refs_8_.first, s32[18]{0:T(128)} %get-tuple-element.43.second, bf16[8,256,256]{2,1,0:T(8,128)(2,1)} %collective-permute-done.9.refs_0_, f32[18,512,256]{2,1,0:T(8,128)} %shard_map.51.refs_1_), custom_call_target="tpu_custom_call" | custom-call | flops 99999997952 | bytes 1 | tf_op jit(solution)/shard_map/pallas_call | solution.py:374
  113.5 2.2 all-to-all-done.refs_0_.refs_1_.refs_2_.refs_3_
  115.7 6.6 %all-to-all-start.2 = ((bf16[4,256,1024]{2,1,0:T(8,128)(2,1)}), bf16[4,256,1024]{2,1,0:T(8,128)(2,1)}, u32[]{:S(2)}, u32[]{:S(2)}) async-start(bf16[4,256,1024]{2,1,0:T(8,128)(2,1)} %get-tuple-element.58), calls=%async_computation.2 | async-start | bytes 4194304 | tf_op jit(solution)/shard_map/all_to_all | solution.py:509
  122.3 2.8 %shard_map.53.refs_0_ = bf16[8,256,768]{2,1,0:T(8,128)(2,1)} custom-call(bf16[4,256,768]{2,1,0:T(8,128)(2,1)} %all-to-all-done.refs_0_.refs_1_.refs_2_.refs_3_, bf16[4,256,768]{2,1,0:T(8,128)(2,1)} %all-to-all-done.refs_0_.refs_1_.refs_2_.refs_3_, bf16[4,256,768]{2,1,0:T(8,128)(2,1)} %all-to-all-done.refs_0_.refs_1_.refs_2_.refs_3_, ...), custom_call_target="tpu_custom_call" | custom-call | flops 1 | bytes 1 | tf_op jit(solution)/shard_map/pallas_call | solution.py:256
  125.1 2.5 %collective-permute-start.10 = (bf16[8,256,768]{2,1,0:T(8,128)(2,1)}, bf16[8,256,768]{2,1,0:T(8,128)(2,1)}, u32[]{:S(2)}, u32[]{:S(2)}) collective-permute-start(bf16[8,256,768]{2,1,0:T(8,128)(2,1)} %shard_map.53.refs_0_), channel_id=1, source_target_pairs={{0,1},{1,0},{2,3},{3,2},{4,5},{5,4},{6,7},{7,6},{8,9},{9,8},{10,11... | collective-permute-start | bytes 9437192 | tf_op jit(solution)/shard_map/ppermute | solution.py:31
  127.6 11.7 %shard_map.54.refs_1_ = f32[18,512,256]{2,1,0:T(8,128)} custom-call(s32[18]{0:T(128)} %get-tuple-element.42.refs_8_.first, s32[18]{0:T(128)} %get-tuple-element.43.second, bf16[8,256,768]{2,1,0:T(8,128)(2,1)} %shard_map.53.refs_0_, f32[18,512,256]{2,1,0:T(8,128)} %shard_map.52.refs_8_.refs_1_), custom_call_target="tpu_custom_call" | custom-call | flops 99999997952 | bytes 1 | tf_op jit(solution)/shard_map/pallas_call | solution.py:374
  139.3 11.7 %shard_map.55.gate.refs_10_ = f32[18,512,256]{2,1,0:T(8,128)} custom-call(s32[18]{0:T(128)} %get-tuple-element.42.refs_8_.first, s32[18]{0:T(128)} %get-tuple-element.43.second, bf16[8,256,768]{2,1,0:T(8,128)(2,1)} %collective-permute-done.10.refs_0_, f32[18,512,256]{2,1,0:T(8,128)} %shard_map.54.refs_1_), custom_call_target="tpu_custom_call" | custom-call | flops 99999997952 | bytes 1 | tf_op jit(solution)/shard_map/pallas_call | solution.py:374
  151.0 41.0 %collective-permute-done.14.refs_4_ = bf16[256,1024]{1,0:T(8,128)(2,1)} collective-permute-done((bf16[256,1024]{1,0:T(8,128)(2,1)}, bf16[256,1024]{1,0:T(8,128)(2,1)}, u32[]{:S(2)}, u32[]{:S(2)}) %collective-permute-start.14) | collective-permute-done | bytes 524320 | tf_op jit(solution)/shard_map/ppermute | solution.py:31
  192.1 2.2 %collective-permute-start.16 = (bf16[256,1024]{1,0:T(8,128)(2,1)}, bf16[256,1024]{1,0:T(8,128)(2,1)S(1)}, u32[]{:S(2)}, u32[]{:S(2)}) collective-permute-start(bf16[256,1024]{1,0:T(8,128)(2,1)} %collective-permute-done.11.refs_1_), channel_id=1, source_target_pairs={{0,1},{1,0},{2,3},{3,2},{4,5},{5,4},{6,7},{7,6},{8,9},{9,8},{10,11... | collective-permute-start | bytes 1572872 | tf_op jit(solution)/shard_map/ppermute | solution.py:31
  195.3 1.7 shard_map.56
  198.4 3.0 %collective-permute-done.15.refs_5_ = bf16[4,256,1024]{2,1,0:T(8,128)(2,1)} collective-permute-done((bf16[4,256,1024]{2,1,0:T(8,128)(2,1)}, bf16[4,256,1024]{2,1,0:T(8,128)(2,1)}, u32[]{:S(2)}, u32[]{:S(2)}) %collective-permute-start.15) | collective-permute-done | bytes 2097184 | tf_op jit(solution)/shard_map/ppermute | solution.py:31
  201.4 15.2 %shard_map.57 = bf16[18,512,256]{2,1,0:T(8,128)(2,1)} custom-call(s32[18]{0:T(128)} %get-tuple-element.56.first, s32[18]{0:T(128)} %get-tuple-element.57.second, bf16[4,256,1024]{2,1,0:T(8,128)(2,1)} %all-to-all-done.2.refs_0_, bf16[256,1024]{1,0:T(8,128)(2,1)} %collective-permute-done.11.refs_1_, bf16[256,1024]{1,0:T(8,128)(2,1)} %collective-permute-done.12.refs_2_, ...), custom_call_target="tpu_custom_call" | custom-call | flops 99999997952 | bytes 1 | tf_op jit(solution)/shard_map/pallas_call | solution.py:374
  (38 shorter events, 5.9 us)
Async XLA Ops:
  7.0 18.6 %collective-permute-start.3 = (bf16[256,256]{1,0:T(8,128)(2,1)}, bf16[256,256]{1,0:T(8,128)(2,1)S(1)}, u32[]{:S(2)}, u32[]{:S(2)}) collective-permute-start(bf16[256,256]{1,0:T(8,128)(2,1)} %get-tuple-element.47), channel_id=1, source_target_pairs={{0,10},{2,8},{4,14},{6,12},{8,2},{10,0},{12,6},{14,4},{1,11},{3,9}... | collective-permute-start | bytes 393224 | tf_op jit(solution)/shard_map/ppermute | solution.py:31
  10.3 17.5 %collective-permute-start.5 = (bf16[256,256]{1,0:T(8,128)(2,1)}, bf16[256,256]{1,0:T(8,128)(2,1)S(1)}, u32[]{:S(2)}, u32[]{:S(2)}) collective-permute-start(bf16[256,256]{1,0:T(8,128)(2,1)} %get-tuple-element.50), channel_id=1, source_target_pairs={{0,12},{2,14},{4,8},{6,10},{8,4},{10,6},{12,0},{14,2},{1,13},{3,15... | collective-permute-start | bytes 393224 | tf_op jit(solution)/shard_map/ppermute | solution.py:31
  10.4 20.3 %collective-permute-start.7 = (bf16[256,256]{1,0:T(8,128)(2,1)}, bf16[256,256]{1,0:T(8,128)(2,1)S(1)}, u32[]{:S(2)}, u32[]{:S(2)}) collective-permute-start(bf16[256,256]{1,0:T(8,128)(2,1)} %get-tuple-element.53), channel_id=1, source_target_pairs={{0,14},{2,12},{4,10},{6,8},{8,6},{10,4},{12,2},{14,0},{1,15},{3,13... | collective-permute-start | bytes 393224 | tf_op jit(solution)/shard_map/ppermute | solution.py:31
  11.8 21.7 %collective-permute-start.1 = (bf16[256,256]{1,0:T(8,128)(2,1)}, bf16[256,256]{1,0:T(8,128)(2,1)S(1)}, u32[]{:S(2)}, u32[]{:S(2)}) collective-permute-start(bf16[256,256]{1,0:T(8,128)(2,1)} %get-tuple-element.39.refs_2_), channel_id=1, source_target_pairs={{0,8},{2,10},{4,12},{6,14},{8,0},{10,2},{12,4},{14,6},{1,9},{3,11}... | collective-permute-start | bytes 393224 | tf_op jit(solution)/shard_map/ppermute | solution.py:31
  13.7 26.9 %collective-permute-start = (bf16[2,256,3072]{2,1,0:T(8,128)(2,1)}, bf16[2,256,3072]{2,1,0:T(8,128)(2,1)}, u32[]{:S(2)}, u32[]{:S(2)}) collective-permute-start(bf16[2,256,3072]{2,1,0:T(8,128)(2,1)} %get-tuple-element.38), channel_id=1, source_target_pairs={{0,1},{2,3},{4,5},{6,7},{8,9},{10,11},{12,13},{14,15},{16,17},{18,... | collective-permute-start | bytes 9437192 | tf_op jit(solution)/shard_map/ppermute | solution.py:27
  25.6 40.0 %copy-start.1 = (bf16[256,256]{1,0:T(8,128)(2,1)}, bf16[256,256]{1,0:T(8,128)(2,1)S(1)}, u32[]{:S(2)}) copy-start(bf16[256,256]{1,0:T(8,128)(2,1)S(1)} %collective-permute-done.3.refs_5_) | copy-start | bytes 393220
  27.8 37.8 %copy-start.2 = (bf16[256,256]{1,0:T(8,128)(2,1)}, bf16[256,256]{1,0:T(8,128)(2,1)S(1)}, u32[]{:S(2)}) copy-start(bf16[256,256]{1,0:T(8,128)(2,1)S(1)} %collective-permute-done.5.refs_6_) | copy-start | bytes 393220
  30.6 35.0 %copy-start.3 = (bf16[256,256]{1,0:T(8,128)(2,1)}, bf16[256,256]{1,0:T(8,128)(2,1)S(1)}, u32[]{:S(2)}) copy-start(bf16[256,256]{1,0:T(8,128)(2,1)S(1)} %collective-permute-done.7.refs_7_) | copy-start | bytes 393220
  33.4 32.2 %copy-start.4 = (bf16[256,256]{1,0:T(8,128)(2,1)}, bf16[256,256]{1,0:T(8,128)(2,1)S(1)}, u32[]{:S(2)}) copy-start(bf16[256,256]{1,0:T(8,128)(2,1)S(1)} %collective-permute-done.1.refs_4_) | copy-start | bytes 393220
  33.4 64.8 %collective-permute-start.2 = (bf16[256,768]{1,0:T(8,128)(2,1)}, bf16[256,768]{1,0:T(8,128)(2,1)}, u32[]{:S(2)}, u32[]{:S(2)}) collective-permute-start(bf16[256,768]{1,0:T(8,128)(2,1)} %get-tuple-element.45.refs_3_), channel_id=1, source_target_pairs={{0,8},{2,10},{4,12},{6,14},{8,0},{10,2},{12,4},{14,6},{1,9},{3,11}... | collective-permute-start | bytes 1179656 | tf_op jit(solution)/shard_map/ppermute | solution.py:31
  36.4 61.1 %collective-permute-start.8 = (bf16[256,768]{1,0:T(8,128)(2,1)}, bf16[256,768]{1,0:T(8,128)(2,1)}, u32[]{:S(2)}, u32[]{:S(2)}) collective-permute-start(bf16[256,768]{1,0:T(8,128)(2,1)} %get-tuple-element.54), channel_id=1, source_target_pairs={{0,14},{2,12},{4,10},{6,8},{8,6},{10,4},{12,2},{14,0},{1,15},{3,13... | collective-permute-start | bytes 1179656 | tf_op jit(solution)/shard_map/ppermute | solution.py:31
  36.4 61.8 %collective-permute-start.6 = (bf16[256,768]{1,0:T(8,128)(2,1)}, bf16[256,768]{1,0:T(8,128)(2,1)}, u32[]{:S(2)}, u32[]{:S(2)}) collective-permute-start(bf16[256,768]{1,0:T(8,128)(2,1)} %get-tuple-element.51), channel_id=1, source_target_pairs={{0,12},{2,14},{4,8},{6,10},{8,4},{10,6},{12,0},{14,2},{1,13},{3,15... | collective-permute-start | bytes 1179656 | tf_op jit(solution)/shard_map/ppermute | solution.py:31
  37.8 84.5 %collective-permute-start.4 = (bf16[256,768]{1,0:T(8,128)(2,1)}, bf16[256,768]{1,0:T(8,128)(2,1)}, u32[]{:S(2)}, u32[]{:S(2)}) collective-permute-start(bf16[256,768]{1,0:T(8,128)(2,1)} %get-tuple-element.48), channel_id=1, source_target_pairs={{0,10},{2,8},{4,14},{6,12},{8,2},{10,0},{12,6},{14,4},{1,11},{3,9}... | collective-permute-start | bytes 1179656 | tf_op jit(solution)/shard_map/ppermute | solution.py:31
  65.6 15.5 %all-to-all-start.1 = ((bf16[4,256,256]{2,1,0:T(8,128)(2,1)}), bf16[4,256,256]{2,1,0:T(8,128)(2,1)S(1)}, u32[]{:S(2)}, u32[]{:S(2)}) async-start(bf16[4,256,256]{2,1,0:T(8,128)(2,1)} %get-tuple-element.55), calls=%async_computation.1 | async-start | bytes 1048576 | tf_op jit(solution)/shard_map/all_to_all | solution.py:509
  81.1 6.4 %copy-start = (bf16[4,256,256]{2,1,0:T(8,128)(2,1)}, bf16[4,256,256]{2,1,0:T(8,128)(2,1)S(1)}, u32[]{:S(2)}) copy-start(bf16[4,256,256]{2,1,0:T(8,128)(2,1)S(1)} %all-to-all-done.1.refs_0_.refs_1_.refs_2_.refs_3_) | copy-start | bytes 1572868
  81.1 34.6 %all-to-all-start = ((bf16[4,256,768]{2,1,0:T(8,128)(2,1)}), bf16[4,256,768]{2,1,0:T(8,128)(2,1)}, u32[]{:S(2)}, u32[]{:S(2)}) async-start(bf16[4,256,768]{2,1,0:T(8,128)(2,1)} %get-tuple-element.44), calls=%async_computation | async-start | bytes 3145728 | tf_op jit(solution)/shard_map/all_to_all | solution.py:509
  89.7 11.2 %collective-permute-start.9 = (bf16[8,256,256]{2,1,0:T(8,128)(2,1)}, bf16[8,256,256]{2,1,0:T(8,128)(2,1)}, u32[]{:S(2)}, u32[]{:S(2)}) collective-permute-start(bf16[8,256,256]{2,1,0:T(8,128)(2,1)} %shard_map.50.refs_0_), channel_id=1, source_target_pairs={{0,1},{1,0},{2,3},{3,2},{4,5},{5,4},{6,7},{7,6},{8,9},{9,8},{10,11... | collective-permute-start | bytes 3145736 | tf_op jit(solution)/shard_map/ppermute | solution.py:31
  97.5 94.5 %collective-permute-start.11 = (bf16[256,1024]{1,0:T(8,128)(2,1)}, bf16[256,1024]{1,0:T(8,128)(2,1)}, u32[]{:S(2)}, u32[]{:S(2)}) collective-permute-start(bf16[256,1024]{1,0:T(8,128)(2,1)} %get-tuple-element.59.gate), channel_id=1, source_target_pairs={{0,8},{2,10},{4,12},{6,14},{8,0},{10,2},{12,4},{14,6},{1,9},{3,11}... | collective-permute-start | bytes 1572872 | tf_op jit(solution)/shard_map/ppermute | solution.py:31
  98.3 93.8 %collective-permute-start.12 = (bf16[256,1024]{1,0:T(8,128)(2,1)}, bf16[256,1024]{1,0:T(8,128)(2,1)}, u32[]{:S(2)}, u32[]{:S(2)}) collective-permute-start(bf16[256,1024]{1,0:T(8,128)(2,1)} %get-tuple-element.61), channel_id=1, source_target_pairs={{0,10},{2,8},{4,14},{6,12},{8,2},{10,0},{12,6},{14,4},{1,11},{3,9}... | collective-permute-start | bytes 1572872 | tf_op jit(solution)/shard_map/ppermute | solution.py:31
  100.9 91.2 %collective-permute-start.13 = (bf16[256,1024]{1,0:T(8,128)(2,1)}, bf16[256,1024]{1,0:T(8,128)(2,1)}, u32[]{:S(2)}, u32[]{:S(2)}) collective-permute-start(bf16[256,1024]{1,0:T(8,128)(2,1)} %get-tuple-element.63), channel_id=1, source_target_pairs={{0,12},{2,14},{4,8},{6,10},{8,4},{10,6},{12,0},{14,2},{1,13},{3,15... | collective-permute-start | bytes 1572872 | tf_op jit(solution)/shard_map/ppermute | solution.py:31
  100.9 91.2 %collective-permute-start.14 = (bf16[256,1024]{1,0:T(8,128)(2,1)}, bf16[256,1024]{1,0:T(8,128)(2,1)}, u32[]{:S(2)}, u32[]{:S(2)}) collective-permute-start(bf16[256,1024]{1,0:T(8,128)(2,1)} %get-tuple-element.65), channel_id=1, source_target_pairs={{0,14},{2,12},{4,10},{6,8},{8,6},{10,4},{12,2},{14,0},{1,15},{3,13... | collective-permute-start | bytes 1572872 | tf_op jit(solution)/shard_map/ppermute | solution.py:31
  115.7 76.4 %all-to-all-start.2 = ((bf16[4,256,1024]{2,1,0:T(8,128)(2,1)}), bf16[4,256,1024]{2,1,0:T(8,128)(2,1)}, u32[]{:S(2)}, u32[]{:S(2)}) async-start(bf16[4,256,1024]{2,1,0:T(8,128)(2,1)} %get-tuple-element.58), calls=%async_computation.2 | async-start | bytes 4194304 | tf_op jit(solution)/shard_map/all_to_all | solution.py:509
  125.1 14.2 %collective-permute-start.10 = (bf16[8,256,768]{2,1,0:T(8,128)(2,1)}, bf16[8,256,768]{2,1,0:T(8,128)(2,1)}, u32[]{:S(2)}, u32[]{:S(2)}) collective-permute-start(bf16[8,256,768]{2,1,0:T(8,128)(2,1)} %shard_map.53.refs_0_), channel_id=1, source_target_pairs={{0,1},{1,0},{2,3},{3,2},{4,5},{5,4},{6,7},{7,6},{8,9},{9,8},{10,11... | collective-permute-start | bytes 9437192 | tf_op jit(solution)/shard_map/ppermute | solution.py:31
  192.1 4.9 %collective-permute-start.16 = (bf16[256,1024]{1,0:T(8,128)(2,1)}, bf16[256,1024]{1,0:T(8,128)(2,1)S(1)}, u32[]{:S(2)}, u32[]{:S(2)}) collective-permute-start(bf16[256,1024]{1,0:T(8,128)(2,1)} %collective-permute-done.11.refs_1_), channel_id=1, source_target_pairs={{0,1},{1,0},{2,3},{3,2},{4,5},{5,4},{6,7},{7,6},{8,9},{9,8},{10,11... | collective-permute-start | bytes 1572872 | tf_op jit(solution)/shard_map/ppermute | solution.py:31
  194.3 2.7 %collective-permute-start.17 = (bf16[256,1024]{1,0:T(8,128)(2,1)}, bf16[256,1024]{1,0:T(8,128)(2,1)}, u32[]{:S(2)}, u32[]{:S(2)}) collective-permute-start(bf16[256,1024]{1,0:T(8,128)(2,1)} %collective-permute-done.12.refs_2_), channel_id=1, source_target_pairs={{0,1},{1,0},{2,3},{3,2},{4,5},{5,4},{6,7},{7,6},{8,9},{9,8},{10,11... | collective-permute-start | bytes 1572872 | tf_op jit(solution)/shard_map/ppermute | solution.py:31
  194.4 3.3 %collective-permute-start.18 = (bf16[256,1024]{1,0:T(8,128)(2,1)}, bf16[256,1024]{1,0:T(8,128)(2,1)}, u32[]{:S(2)}, u32[]{:S(2)}) collective-permute-start(bf16[256,1024]{1,0:T(8,128)(2,1)} %collective-permute-done.13.refs_3_), channel_id=1, source_target_pairs={{0,1},{1,0},{2,3},{3,2},{4,5},{5,4},{6,7},{7,6},{8,9},{9,8},{10,11... | collective-permute-start | bytes 1572872 | tf_op jit(solution)/shard_map/ppermute | solution.py:31
  194.8 3.6 %collective-permute-start.19 = (bf16[256,1024]{1,0:T(8,128)(2,1)}, bf16[256,1024]{1,0:T(8,128)(2,1)}, u32[]{:S(2)}, u32[]{:S(2)}) collective-permute-start(bf16[256,1024]{1,0:T(8,128)(2,1)} %collective-permute-done.14.refs_4_), channel_id=1, source_target_pairs={{0,1},{1,0},{2,3},{3,2},{4,5},{5,4},{6,7},{7,6},{8,9},{9,8},{10,11... | collective-permute-start | bytes 1572872 | tf_op jit(solution)/shard_map/ppermute | solution.py:31
  194.9 6.5 %collective-permute-start.15 = (bf16[4,256,1024]{2,1,0:T(8,128)(2,1)}, bf16[4,256,1024]{2,1,0:T(8,128)(2,1)}, u32[]{:S(2)}, u32[]{:S(2)}) collective-permute-start(bf16[4,256,1024]{2,1,0:T(8,128)(2,1)} %all-to-all-done.2.refs_0_), channel_id=1, source_target_pairs={{0,1},{1,0},{2,3},{3,2},{4,5},{5,4},{6,7},{7,6},{8,9},{9,8},{10,11... | collective-permute-start | bytes 6291464 | tf_op jit(solution)/shard_map/ppermute | solution.py:31
  197.0 4.4 %copy-start.5 = (bf16[256,1024]{1,0:T(8,128)(2,1)}, bf16[256,1024]{1,0:T(8,128)(2,1)S(1)}, u32[]{:S(2)}) copy-start(bf16[256,1024]{1,0:T(8,128)(2,1)S(1)} %collective-permute-done.16.refs_6_) | copy-start | bytes 1572868
